TPU v7x, 32 devices: a whole 2x2x4 slice. The times are simulated.
32 devices in a mesh: ctx: 8 (over z, y), fsdp: 4 (over x, core).
Axes of the slice: x: 2, y: 2, z: 4, core: 2. Of those that a mesh axis runs over, the one named last changes fastest.
Arguments:
- inputs: bfloat16 [2048, 7168], P('ctx'), may hold values from -12 to 12
- w_qkv: bfloat16 [7168, 3, 1024], P('ctx', None, 'fsdp'), may hold values from -1 to 1, as said below
- selected: int32 [4, 4], replicated, may hold values from -1 to 3, as said below
- d_attn: bfloat16 [2048, 1024], P('ctx', 'fsdp'), may hold values from -6 to 6
Outputs:
- d_input: bfloat16 [2048, 7168], P('ctx', 'fsdp')
Inputs may be any that keep to these rules, and one draw needn't show every extreme that they name: `selected`: row b lists min(b + 1, 4) different blocks of 0 to b, b among them, in the first slots; the other slots hold -1. `w_qkv`: projection weights scaled by the fan-in.
All inputs are finite; a program needn't handle non-finite values.
Results may differ from a plain program's by a relative error of at most 0.023.
Values may be sent and summed in bfloat16 or wider, within the bound.
No kernel may reach another device: no remote copies, remote signals or barrier semaphores. Data moves between devices by JAX's collectives and lax.ppermute only.
A program may use at most 128 MiB of HBM per device.

v0:
```python
import jax
import jax.numpy as jnp
from jax import lax
from jax.sharding import PartitionSpec as P

HD = 128
BLOCK = 512


def stat_rows(stat, row_count, heads):
    return stat[..., 0].transpose(0, 2, 1).reshape(row_count, heads)


def attend_chosen(query, keys_all, values_all, grad_out, selected, first_row):
    row_count, col_count = query.shape
    seq_len = keys_all.shape[0]
    nblocks = seq_len // BLOCK
    heads = col_count // HD
    top_count = selected.shape[1]
    group = min(BLOCK, row_count)
    groups = row_count // group
    scaling = HD ** (-0.5)
    block_ids = jnp.arange(nblocks, dtype=jnp.int32)
    q_block = (first_row + jnp.arange(groups, dtype=jnp.int32) * group) // BLOCK
    picked = q_block[:, None] == block_ids[None, :]
    chosen_ids = jnp.sum(jnp.where(picked[:, :, None], selected[None], 0), axis=1)
    index = jnp.maximum(chosen_ids, 0)
    key_pos = index[:, :, None] * BLOCK + jnp.arange(BLOCK, dtype=jnp.int32)[None, None, :]
    key_pos = key_pos.reshape(groups, top_count * BLOCK)
    slot_valid = jnp.repeat(chosen_ids >= 0, BLOCK, axis=1)
    position_q = (first_row + jnp.arange(row_count, dtype=jnp.int32)).reshape(groups, group)
    allowed = slot_valid[:, None, :] & (position_q[:, :, None] >= key_pos[:, None, :])
    key_heads = keys_all.reshape(nblocks, BLOCK, col_count)[index].reshape(
        groups, top_count * BLOCK, heads, HD
    )
    value_heads = values_all.reshape(nblocks, BLOCK, col_count)[index].reshape(
        groups, top_count * BLOCK, heads, HD
    )
    query_heads = query.reshape(groups, group, heads, HD)
    grad_heads = grad_out.reshape(groups, group, heads, HD)
    scores = (
        jnp.einsum("bqhd,bkhd->bhqk", query_heads, key_heads, preferred_element_type=jnp.float32)
        * scaling
    )
    masked = jnp.where(allowed[:, None], scores, -jnp.inf)
    highest = jnp.max(masked, axis=-1, keepdims=True)
    expo = jnp.exp(masked - highest)
    totals = jnp.sum(expo, axis=-1, keepdims=True)
    probs = expo / totals
    probs_low = probs.astype(jnp.bfloat16)
    attended = jnp.einsum(
        "bhqk,bkhd->bqhd", probs_low, value_heads, preferred_element_type=jnp.float32
    ).astype(jnp.bfloat16)
    delta_rows = jnp.sum(grad_heads.astype(jnp.float32) * attended.astype(jnp.float32), axis=3)
    delta = delta_rows.transpose(0, 2, 1)[..., None]
    dprobs = jnp.einsum(
        "bqhd,bkhd->bhqk", grad_heads, value_heads, preferred_element_type=jnp.float32
    )
    dscores = (probs * (dprobs - delta)).astype(jnp.bfloat16)
    dquery = (
        jnp.einsum("bhqk,bkhd->bqhd", dscores, key_heads, preferred_element_type=jnp.float32)
        * scaling
    )
    dquery = dquery.astype(jnp.bfloat16).reshape(row_count, col_count)
    highest_rows = stat_rows(highest, row_count, heads)
    total_rows = stat_rows(totals, row_count, heads)
    delta_flat = delta_rows.reshape(row_count, heads)
    key_slots = (
        jnp.einsum("bhqk,bqhd->bkhd", dscores, query_heads, preferred_element_type=jnp.float32)
        * scaling
    )
    value_slots = jnp.einsum(
        "bhqk,bqhd->bkhd", probs_low, grad_heads, preferred_element_type=jnp.float32
    )
    onehot = (chosen_ids[:, :, None] == block_ids[None, None, :]).astype(jnp.float32)
    key_term = jnp.einsum(
        "gtn,gtkc->nkc",
        onehot,
        key_slots.reshape(groups, top_count, BLOCK, col_count),
        precision=lax.Precision.HIGHEST,
    ).reshape(seq_len, col_count)
    value_term = jnp.einsum(
        "gtn,gtkc->nkc",
        onehot,
        value_slots.reshape(groups, top_count, BLOCK, col_count),
        precision=lax.Precision.HIGHEST,
    ).reshape(seq_len, col_count)
    return (dquery, key_term, value_term, highest_rows, total_rows, delta_flat)


def shards(inputs, w_qkv, selected, d_attn):
    row_count, width = inputs.shape
    col_count = w_qkv.shape[2]
    first_row = lax.axis_index("ctx") * row_count
    whole_w = lax.all_gather(w_qkv, "ctx", axis=0, tiled=True).reshape(width, 3 * col_count)
    projected = jnp.dot(inputs, whole_w, preferred_element_type=jnp.float32)
    projected = projected.astype(jnp.bfloat16).reshape(row_count, 3, col_count)
    query = projected[:, 0]
    keys_local = projected[:, 1]
    values_local = projected[:, 2]
    keys_all, values_all = (
        lax.all_gather(keys_local, "ctx", axis=0, tiled=True),
        lax.all_gather(values_local, "ctx", axis=0, tiled=True),
    )
    dquery, key_term, value_term, _, _, _ = attend_chosen(
        query, keys_all, values_all, d_attn, selected, first_row
    )
    key_total, value_total = (
        lax.psum_scatter(
            key_term.astype(jnp.bfloat16), "ctx", scatter_dimension=0, tiled=True
        ).astype(jnp.float32),
        lax.psum_scatter(
            value_term.astype(jnp.bfloat16), "ctx", scatter_dimension=0, tiled=True
        ).astype(jnp.float32),
    )
    key_sum = key_total.astype(jnp.bfloat16)
    value_sum = value_total.astype(jnp.bfloat16)
    flat_grads = jnp.stack([dquery, key_sum, value_sum], axis=1).reshape(row_count, 3 * col_count)
    contract = (((1,), (1,)), ((), ()))
    partial_grad = lax.dot_general(
        flat_grads, whole_w, contract, preferred_element_type=jnp.float32
    )
    total = lax.psum_scatter(
        partial_grad.astype(jnp.bfloat16), "fsdp", scatter_dimension=1, tiled=True
    )
    return total


def solution(mesh):
    placed = (P("ctx", None), P("ctx", None, "fsdp"), P(), P("ctx", "fsdp"))
    return jax.shard_map(
        shards, mesh=mesh, in_specs=placed, out_specs=P("ctx", "fsdp"), check_vma=False
    )
```

profile of v0, /device:TPU:0, one launch (start us, length us, event | category | flops | bytes accessed | tf_op | source)
XLA Modules:
  0.0 485.8 jit_solution(17881157930767470618)
XLA Ops:
  6.5 0.7 all-gather.6.cloned.1.call-update
  7.3 162.2 %all-gather.6.cloned.1.call-done = bf16[7168,3,256]{2,0,1:T(8,128)(2,1)} async-done(((bf16[896,3,256]{2,0,1:T(8,128)(2,1)}), bf16[7168,3,256]{2,0,1:T(8,128)(2,1)}) %all-gather.6.cloned.1.call-update) | async-done | bytes 11010064 | tf_op jit(solution)/shard_map/all_gather | solution.py:95
  169.5 14.8 %copy.17 = bf16[7168,3,256]{0,2,1:T(8,128)(2,1)} copy(bf16[7168,3,256]{2,0,1:T(8,128)(2,1)} %all-gather.6.cloned.1.call-done) | data formatting | bytes 22020096 | tf_op jit(solution)/shard_map/all_gather | solution.py:95
  184.3 8.3 %convolution_convert_fusion.1 = bf16[256,768]{1,0:T(8,128)(2,1)S(1)} fusion(bf16[256,7168]{1,0:T(8,128)(2,1)} %param.4, bf16[7168,768]{0,1:T(8,128)(2,1)} %bitcast.101), kind=kOutput, calls=%fused_computation.23 | convolution fusion | flops 2818768896 | bytes 15073280 | tf_op jit(solution)/shard_map/dot_general | solution.py:96
  192.6 0.2 copy.18
  192.8 0.8 fusion.39
  193.6 0.0 all-gather.10.cloned.1.call-start
  193.7 0.7 all-gather.10.cloned.1.call-update
  194.4 0.2 reduce-scatter.4.cloned.1.call-start
  194.7 0.1 select_reduce_fusion
  194.8 0.1 broadcast_bitcast_fusion
  194.8 0.1 copy.25
  195.0 0.1 add.48
  195.1 1.2 compare_and_fusion
  196.3 35.2 %all-gather.8.cloned.1.call-done = bf16[2048,1,256]{0,2,1:T(8,128)(2,1)} async-done(((bf16[256,1,256]{0,2,1:T(8,128)(2,1)}), bf16[2048,1,256]{0,2,1:T(8,128)(2,1)}) %all-gather.8.cloned.1.call-update) | async-done | bytes 1048592 | tf_op jit(solution)/shard_map/all_gather | solution.py:102
  231.5 1.5 copy.19
  233.0 0.6 gather_fusion
  233.6 0.3 reshape.318
  233.9 0.8 copy.28
  234.7 37.3 %all-gather.10.cloned.1.call-done = bf16[2048,1,256]{0,2,1:T(8,128)(2,1)} async-done(((bf16[256,1,256]{0,2,1:T(8,128)(2,1)}), bf16[2048,1,256]{0,2,1:T(8,128)(2,1)}) %all-gather.10.cloned.1.call-update) | async-done | bytes 1048592 | tf_op jit(solution)/shard_map/all_gather | solution.py:103
  272.0 1.5 copy.22
  273.5 0.6 gather_fusion.1
  274.1 0.3 reshape.321
  274.4 2.1 copy.26
  276.5 3.7 fusion.40
  280.2 2.9 fusion.10
  283.1 0.9 fusion.19
  284.0 0.7 fusion.2
  284.7 1.4 copy-done
  286.1 1.8 fusion.4
  287.9 3.6 reshape.323
  291.5 4.1 copy.30
  295.7 4.1 convolution_convert_fusion
  299.7 1.1 copy.31
  300.9 0.3 reduce-scatter.6.cloned.1.call-start
  301.2 0.9 convolution_bitcast_fusion.1
  302.1 8.6 %copy.34 = f32[1,2048,2,128]{3,2,1,0:T(2,128)} copy(f32[1,2048,2,128]{3,1,2,0:T(8,128)S(1)} %convolution_bitcast_fusion.1) | data formatting | bytes 4194304 | tf_op jit(solution)/shard_map/bhqk,bqhd->bkhd/transpose | solution.py:72
  310.7 2.9 reshape.324
  313.6 3.4 fusion.11
  317.0 1.1 copy.37
  318.1 0.0 reduce-scatter.8.cloned.1.call-start
  318.2 0.8 copy-done.1
  319.0 0.8 fusion.14
  319.8 0.1 copy.38
  319.9 43.4 %reduce-scatter.4.cloned.1.call-done = bf16[256,256]{1,0:T(8,128)(2,1)} async-done(((bf16[2048,256]{1,0:T(8,128)(2,1)}), bf16[256,256]{1,0:T(8,128)(2,1)}) %reduce-scatter.4.cloned.1.call-update) | async-done | bytes 131088 | tf_op jit(solution)/shard_map/reduce_scatter | solution.py:109
  363.3 66.1 %reduce-scatter.6.cloned.1.call-done = bf16[256,256]{1,0:T(8,128)(2,1)} async-done(((bf16[2048,256]{1,0:T(8,128)(2,1)}), bf16[256,256]{1,0:T(8,128)(2,1)}) %reduce-scatter.6.cloned.1.call-update) | async-done | bytes 131088 | tf_op jit(solution)/shard_map/reduce_scatter | solution.py:112
  429.4 9.2 %fusion.1 = bf16[256,7168]{1,0:T(8,128)(2,1)} fusion(bf16[7168,3,256]{2,0,1:T(8,128)(2,1)} %all-gather.6.cloned.1.call-done, bf16[256,1,256]{2,0,1:T(8,128)(2,1)} %bitcast.116, bf16[256,1,256]{2,0,1:T(8,128)(2,1)} %bitcast.115, bf16[256,1,256]{2,0,1:T(8,128)(2,1)S(1)} %copy.38), kind=kOutput, calls=%fused_computation.4 | convolution fusion | flops 2820800512 | bytes 15073280 | tf_op jit(solution)/shard_map/dot_general | solution.py:120
  438.6 40.4 %reduce-scatter.8.cloned.1.call-done = bf16[256,1792]{1,0:T(8,128)(2,1)} async-done(((bf16[256,7168]{1,0:T(8,128)(2,1)}), bf16[256,1792]{1,0:T(8,128)(2,1)}) %reduce-scatter.8.cloned.1.call-update) | async-done | bytes 917520 | tf_op jit(solution)/shard_map/reduce_scatter | solution.py:123
  (31 shorter events, 0.2 us)
Async XLA Ops:
  6.5 163.0 %all-gather.6.cloned.1.call-start = ((), (), s32[]{:S(2)}) async-start(), calls=%async_computation.3 | async-start | bytes 12386304 | tf_op jit(solution)/shard_map/all_gather | solution.py:95
  7.3 224.2 %all-gather.8.cloned.1.call-start = ((), (), s32[]{:S(2)}) async-start(), calls=%async_computation.7 | async-start | bytes 1179648 | tf_op jit(solution)/shard_map/all_gather | solution.py:102
  184.3 10.3 %copy-start.8 = (s32[4,4]{1,0:T(4,128)S(1)}, s32[4,4]{1,0:T(4,128)}, u32[]{:S(2)}) copy-start(s32[4,4]{1,0:T(4,128)} %param.6) | copy-start | bytes 196
  184.3 10.5 %copy-start.4 = (bf16[256,256]{1,0:T(8,128)(2,1)S(1)}, bf16[256,256]{1,0:T(8,128)(2,1)}, u32[]{:S(2)}) copy-start(bf16[256,256]{1,0:T(8,128)(2,1)} %param.7) | copy-start | bytes 393220
  193.6 78.4 %all-gather.10.cloned.1.call-start = ((), (), s32[]{:S(2)}) async-start(), calls=%async_computation.8 | async-start | bytes 1179648 | tf_op jit(solution)/shard_map/all_gather | solution.py:103
  194.4 168.9 %reduce-scatter.4.cloned.1.call-start = ((), (), s32[]{:S(2)}) async-start(), calls=%async_computation.4 | async-start | bytes 1179648 | tf_op jit(solution)/shard_map/reduce_scatter | solution.py:109
  274.4 2.1 copy-start.5
  274.4 2.1 copy-start.6
  280.2 3.0 copy-start.2
  280.2 3.8 copy-start.3
  284.0 2.1 copy-start.7
  284.7 1.4 copy-start
  300.9 128.5 %reduce-scatter.6.cloned.1.call-start = ((), (), s32[]{:S(2)}) async-start(), calls=%async_computation.5 | async-start | bytes 1179648 | tf_op jit(solution)/shard_map/reduce_scatter | solution.py:112
  317.0 2.0 copy-start.1
  318.1 160.9 %reduce-scatter.8.cloned.1.call-start = ((), (), s32[]{:S(2)}) async-start(), calls=%async_computation.6 | async-start | bytes 4587520 | tf_op jit(solution)/shard_map/reduce_scatter | solution.py:123
Sparse Core Ops, SparseCore 0:
  9.5 159.9 all-gather.5
  193.7 37.7 all-gather.7
  233.5 38.4 all-gather.9
  301.0 62.2 reduce-scatter.3
  366.9 62.3 reduce-scatter.5
  438.7 40.2 reduce-scatter.7
where the time goes:
time: 487 us; the launch traced here: 486 us
  waiting for transfers between devices  386 us (79%)
  local copies, waits for them, and re-layouts  47.4 us (10%)
  matrix products  33.8 us (7%)
  between operations  13.8 us (3%)
    all_gather x1, waiting for transfers between devices, shards(): lax.all_gather(w_qkv, 'ctx', axis=0, tiled=True)  162 us
    reduce_scatter x1, waiting for transfers between devices, shards(): lax.psum_scatter(value_term.astype(jnp.bfloat16), 'ctx', scatter_dimensio...  66.1 us
    reduce_scatter x1, waiting for transfers between devices, shards(): lax.psum_scatter(key_term.astype(jnp.bfloat16), 'ctx', scatter_dimension=...  43.4 us
    reduce_scatter x1, waiting for transfers between devices, shards(): lax.psum_scatter(partial_grad.astype(jnp.bfloat16), 'fsdp', scatter_dimen...  40.4 us
    all_gather x1, waiting for transfers between devices, shards(): lax.all_gather(values_local, 'ctx', axis=0, tiled=True)  37.3 us
    all_gather x1, waiting for transfers between devices, shards(): lax.all_gather(keys_local, 'ctx', axis=0, tiled=True)  35.2 us
    all_gather x1, local copies, waits for them, and re-layouts, shards(): lax.all_gather(w_qkv, 'ctx', axis=0, tiled=True)  14.8 us
    another operation x7, local copies, waits for them, and re-layouts  14.2 us
  transfers between devices with their start and end apart: 6, of which 6 were waited for; matrix products, arithmetic and copies ran while one was open for 5% of the time, Pallas kernels for 0%

commit v1 on v0

v1 whole, which is shorter than its diff:
```python
import functools

import jax
import jax.numpy as jnp
from jax import lax
from jax.experimental import pallas as pl
from jax.experimental.pallas import tpu as pltpu
from jax.sharding import PartitionSpec as P

HD = 128
BLOCK = 512
FAR = 1 << 20
PAIR = 2
F32 = jnp.float32
BF16 = jnp.bfloat16
VMEM_LIMIT = 48 * 1024 * 1024


def swap(array, axis, size, distance):
    return lax.ppermute(array, axis, [(i, i ^ distance) for i in range(size)])


def dot_nt(a, b):
    return lax.dot_general(a, b, (((1,), (1,)), ((), ())), preferred_element_type=F32)


def dot_nn(a, b):
    return lax.dot_general(a, b, (((1,), (0,)), ((), ())), preferred_element_type=F32)


def masked_scores(products, gap, limits, run):
    scaled = products * (HD ** -0.5)
    parts = [
        jnp.where(gap <= limit, scaled[:, i * run : (i + 1) * run], -jnp.inf)
        for i, limit in enumerate(limits)
    ]
    return jnp.concatenate(parts, axis=1)


def query_kernel(sets, run, limit_ref, q_ref, grad_ref, *refs):
    kv_refs, (dq_ref, stat_ref) = refs[:sets], refs[sets:]
    gap = lax.broadcasted_iota(jnp.int32, (run, run), 1) - lax.broadcasted_iota(
        jnp.int32, (run, run), 0
    )
    lane = lax.broadcasted_iota(jnp.int32, (run, HD), 1)
    for half in range(2):
        rows = pl.ds(half * run, run)
        q, grad = q_ref[rows, :], grad_ref[rows, :]
        scores = [
            masked_scores(
                dot_nt(q, kv_refs[j][:, :HD]),
                gap,
                [limit_ref[half, 2 * j], limit_ref[half, 2 * j + 1]],
                run,
            )
            for j in range(sets)
        ]
        highest = functools.reduce(
            jnp.maximum, [jnp.max(s, axis=1, keepdims=True) for s in scores]
        )
        expo = [jnp.exp(s - highest) for s in scores]
        total = sum(jnp.sum(e, axis=1, keepdims=True) for e in expo)
        inverse = 1.0 / total
        probs = [e * inverse for e in expo]
        attended = sum(
            dot_nn(p.astype(BF16), kv_refs[j][:, HD:]) for j, p in enumerate(probs)
        ).astype(BF16)
        delta = jnp.sum(
            grad.astype(F32) * attended.astype(F32), axis=1, keepdims=True
        )
        dq = jnp.zeros((run, HD), F32)
        for j, p in enumerate(probs):
            dprobs = dot_nt(grad, kv_refs[j][:, HD:])
            dscores = (p * (dprobs - delta)).astype(BF16)
            dq += dot_nn(dscores, kv_refs[j][:, :HD])
        dq_ref[rows, :] = (dq * (HD ** -0.5)).astype(BF16)
        stats = jnp.where(
            lane == 0, highest, jnp.where(lane == 1, inverse, delta)
        )
        stat_ref[:, rows] = jnp.transpose(stats)[:8]


def key_kernel(sets, run, limit_ref, kv_ref, *refs):
    q_refs, grad_refs, stat_refs = refs[:sets], refs[sets : 2 * sets], refs[2 * sets : 3 * sets]
    out_ref = refs[3 * sets]
    gap = lax.broadcasted_iota(jnp.int32, (run, run), 0) - lax.broadcasted_iota(
        jnp.int32, (run, run), 1
    )
    for half in range(2):
        rows = pl.ds(half * run, run)
        keys, values = kv_ref[rows, :HD], kv_ref[rows, HD:]
        dk = jnp.zeros((run, HD), F32)
        dv = jnp.zeros((run, HD), F32)
        for j in range(sets):
            q, grad, stat = q_refs[j][...], grad_refs[j][...], stat_refs[j]
            scores = masked_scores(
                dot_nt(keys, q),
                gap,
                [limit_ref[half, 2 * j], limit_ref[half, 2 * j + 1]],
                run,
            )
            probs = jnp.exp(scores - stat[0:1, :]) * stat[1:2, :]
            dprobs = dot_nt(values, grad)
            dscores = (probs * (dprobs - stat[2:3, :])).astype(BF16)
            dk += dot_nn(dscores, q)
            dv += dot_nn(probs.astype(BF16), grad)
        out_ref[rows, :HD] = (dk * (HD ** -0.5)).astype(BF16)
        out_ref[rows, HD:] = dv.astype(BF16)


def local_call(kernel, out_shape, n_vmem, flops):
    return pl.pallas_call(
        kernel,
        out_shape=out_shape,
        in_specs=[pl.BlockSpec(memory_space=pltpu.SMEM)]
        + [pl.BlockSpec(memory_space=pltpu.VMEM)] * n_vmem,
        out_specs=jax.tree.map(lambda _: pl.BlockSpec(memory_space=pltpu.VMEM), out_shape),
        compiler_params=pltpu.CompilerParams(vmem_limit_bytes=VMEM_LIMIT),
        cost_estimate=pl.CostEstimate(flops=flops, bytes_accessed=4 << 20, transcendentals=1 << 20),
    )


def shards(n_ctx, n_f, inputs, w_qkv, selected, d_attn):
    run, width = inputs.shape
    depth = w_qkv.shape[0]
    per_f = width // n_f
    c = lax.axis_index("ctx")
    f = lax.axis_index("fsdp")
    mine = (c // PAIR) % 2
    over_ctx = functools.partial(swap, axis="ctx", size=n_ctx)
    over_f = functools.partial(swap, axis="fsdp", size=n_f)
    even = [d for d in range(n_ctx) if d % 2 == 0]
    group = [d for d in range(n_ctx) if not d & PAIR]
    sets = len(group)

    def head_of(array, which):
        return lax.dynamic_slice_in_dim(array, which * HD, HD, axis=array.ndim - 1)

    own_w = head_of(w_qkv, mine)
    other_w = head_of(w_qkv, 1 - mine)
    kv_of = lambda w: jnp.concatenate([w[:, 1], w[:, 2]], axis=1)
    q_of = lambda w: w[:, 0]

    def gather_pieces(own, other):
        pieces = {0: own}
        for d in even[1:]:
            pieces[d] = over_ctx(other if d & PAIR else own, distance=d)
        for d in even:
            pieces[d ^ 1] = over_ctx(pieces[d], distance=1)
        return pieces

    part = lax.dynamic_slice_in_dim(inputs, f * per_f, per_f, axis=1)
    parts = {0: over_ctx(part, distance=PAIR)}
    bit = n_f // 2
    while bit:
        for e in list(parts):
            parts[e ^ bit] = over_f(parts[e], distance=bit)
        bit //= 2
    both = jnp.concatenate([inputs, jnp.zeros_like(inputs)], axis=0)
    for e, value in parts.items():
        both = lax.dynamic_update_slice(both, value, (run, (f ^ e) * per_f))

    kv_pieces = gather_pieces(kv_of(own_w), kv_of(other_w))
    q_pieces = gather_pieces(q_of(own_w), q_of(other_w))

    def project(pieces):
        total = None
        for d, w in pieces.items():
            rows = lax.dynamic_slice_in_dim(both, (c ^ d) * depth, depth, axis=1)
            term = dot_nn(rows, w)
            total = term if total is None else total + term
        return total.astype(BF16)

    own_grad = head_of(d_attn, mine)
    grad = jnp.concatenate(
        [own_grad, over_ctx(head_of(d_attn, 1 - mine), distance=PAIR)], axis=0
    )
    grads = [grad] + [over_ctx(grad, distance=d) for d in group[1:]]

    kv = project(kv_pieces)
    kvs = [kv] + [over_ctx(kv, distance=d) for d in group[1:]]
    q = project(q_pieces)
    qs = [q] + [over_ctx(q, distance=d) for d in group[1:]]

    order = jnp.stack([c ^ d ^ p for d in group for p in (0, PAIR)])
    blocks = order * run // BLOCK
    here = order[:2]

    def limits(query_runs, key_runs, query_blocks, key_blocks):
        chosen = jnp.any(
            selected[query_blocks][:, :, None] == key_blocks[None, None, :], axis=1
        )
        ahead = query_runs[:, None] - key_runs[None, :]
        bound = jnp.where(ahead > 0, FAR, jnp.where(ahead == 0, 0, -FAR))
        return jnp.where(chosen, bound, -FAR).astype(jnp.int32)

    query_limits = limits(here, order, blocks[:2], blocks)
    key_limits = limits(order, here, blocks, blocks[:2]).T

    dq, stat = local_call(
        functools.partial(query_kernel, sets, run),
        (
            jax.ShapeDtypeStruct((2 * run, HD), BF16),
            jax.ShapeDtypeStruct((8, 2 * run), F32),
        ),
        2 + sets,
        2 * 2 * run * sets * 2 * run * HD * 5,
    )(query_limits, q, grad, *kvs)
    stats = [stat] + [over_ctx(stat, distance=d) for d in group[1:]]
    dkv = local_call(
        functools.partial(key_kernel, sets, run),
        jax.ShapeDtypeStruct((2 * run, 2 * HD), BF16),
        1 + 3 * sets,
        2 * 2 * run * sets * 2 * run * HD * 5,
    )(key_limits, kv, *qs, *grads, *stats)

    all_grads = jnp.concatenate([dkv, dq], axis=1)
    whole_w = jnp.zeros((width, 3 * HD), BF16)
    for d in kv_pieces:
        whole_w = lax.dynamic_update_slice(whole_w, kv_pieces[d], ((c ^ d) * depth, 0))
        whole_w = lax.dynamic_update_slice(
            whole_w, q_pieces[d], ((c ^ d) * depth, 2 * HD)
        )

    if n_f != 4:
        partial_out = dot_nt(all_grads, whole_w).astype(BF16)
        total = partial_out[:run].astype(F32) + over_ctx(partial_out[run:], distance=PAIR).astype(F32)
        return lax.psum_scatter(total.astype(BF16), "fsdp", scatter_dimension=1, tiled=True)

    def term(e):
        rows = lax.dynamic_slice_in_dim(whole_w, (f ^ e) * per_f, per_f, axis=0)
        return dot_nt(all_grads, rows)

    half = per_f // 2
    far = term(2) + over_f(term(3).astype(BF16), distance=1).astype(F32)
    near = term(0) + over_f(term(1).astype(BF16), distance=1).astype(F32)
    by_x = functools.partial(over_f, distance=2)
    by_z = functools.partial(over_ctx, distance=PAIR)
    corner_x = by_x(far[run:, :half].astype(BF16))
    corner_z = by_z(far[run:, half:].astype(BF16))
    from_x_a = by_x(far[:run, :half].astype(BF16))
    from_z_b = by_z(near[run:, half:].astype(BF16))
    from_z_a = by_z((near[run:, :half] + corner_x.astype(F32)).astype(BF16))
    from_x_b = by_x((far[:run, half:] + corner_z.astype(F32)).astype(BF16))
    left = near[:run, :half] + from_x_a.astype(F32) + from_z_a.astype(F32)
    right = near[:run, half:] + from_x_b.astype(F32) + from_z_b.astype(F32)
    return jnp.concatenate([left, right], axis=1).astype(BF16)


def solution(mesh):
    placed = (P("ctx", None), P("ctx", None, "fsdp"), P(), P("ctx", "fsdp"))
    body = functools.partial(shards, mesh.shape["ctx"], mesh.shape["fsdp"])
    return jax.shard_map(
        body, mesh=mesh, in_specs=placed, out_specs=P("ctx", "fsdp"), check_vma=False
    )
```

time: 487 us -> 236 us (0.48)
  waiting for transfers between devices: 386 us -> 128 us
  starting transfers between devices: 0.61 us -> 49.7 us
  local copies, waits for them, and re-layouts: 47.4 us -> 28.5 us
  matrix products: 33.8 us -> 16.9 us
  between operations: 13.8 us -> 0.39 us
  Pallas kernels: 0 us -> 8.35 us
    all_gather x3 -> x0, waiting for transfers between devices: 235 us -> none  [the longest x1 162 us: shards(): lax.all_gather(w_qkv, 'ctx', axis=0, tiled=True)]
    reduce_scatter x3 -> x0, waiting for transfers between devices: 150 us -> none  [the longest x1 66.1 us: shards(): lax.psum_scatter(value_term.astype(jnp.bfloat16), 'ctx', scatter_dimensio...]
    ppermute x0 -> x39, waiting for transfers between devices: none -> 128 us  [swap(): return lax.ppermute(array, axis, [(i, i ^ distance) for i in range(size)])]
    ppermute x0 -> x39, starting transfers between devices: none -> 49.7 us  [swap(): return lax.ppermute(array, axis, [(i, i ^ distance) for i in range(size)])]
    all_gather x3 -> x0, local copies, waits for them, and re-layouts: 17.7 us -> none  [the longest x1 14.8 us: shards(): lax.all_gather(w_qkv, 'ctx', axis=0, tiled=True)]
    another operation x8 -> x2, local copies, waits for them, and re-layouts: 14.3 us -> 0.19 us  [shards(): order = jnp.stack([c ^ d ^ p for d in group for p in (0, PAIR)])]
    dot_general x9 -> x20, matrix products: 30.1 us -> 16.9 us  [the longest x4 9.99 us: dot_nt(): lax.dot_general(a, b, (((1,), (1,)), ((), ())), preferred_element_type=F32)]
    dynamic_update_slice x0 -> x19, local copies, waits for them, and re-layouts: none -> 13.1 us  [the longest x8 6.97 us: shards(): lax.dynamic_update_slice(whole_w, q_pieces[d], ((c ^ d) * depth, 2 * HD))]
  transfers between devices with their start and end apart: 6 -> 39, of which waited for: 6 -> 15; matrix products, arithmetic and copies ran while one was open for 5% -> 17% of each run, Pallas kernels for 0% -> 2%
where the time goes in v1:
time: 236 us
  waiting for transfers between devices  128 us (54%)
  starting transfers between devices  49.7 us (21%)
  local copies, waits for them, and re-layouts  28.5 us (12%)
  matrix products  16.9 us (7%)
  Pallas kernels  8.35 us (4%)
  other arithmetic  3.81 us (2%)
    ppermute x39, waiting for transfers between devices, swap(): return lax.ppermute(array, axis, [(i, i ^ distance) for i in range(size)])  128 us
    ppermute x39, starting transfers between devices, swap(): return lax.ppermute(array, axis, [(i, i ^ distance) for i in range(size)])  49.7 us
    dot_general x4, matrix products, dot_nt(): lax.dot_general(a, b, (((1,), (1,)), ((), ())), preferred_element_type=F32)  9.99 us
    dynamic_update_slice x8, local copies, waits for them, and re-layouts, shards(): lax.dynamic_update_slice(whole_w, q_pieces[d], ((c ^ d) * depth, 2 * HD))  6.97 us
    dot_general x16, matrix products, dot_nn(): lax.dot_general(a, b, (((1,), (0,)), ((), ())), preferred_element_type=F32)  6.9 us
    concatenate x1, local copies, waits for them, and re-layouts, shards(): both = jnp.concatenate([inputs, jnp.zeros_like(inputs)], axis=0)  5.76 us
    dynamic_update_slice x7, local copies, waits for them, and re-layouts, shards(): lax.dynamic_update_slice(whole_w, kv_pieces[d], ((c ^ d) * depth, 0))  5.75 us
  transfers between devices with their start and end apart: 39, of which 15 were waited for; matrix products, arithmetic and copies ran while one was open for 17% of the time, Pallas kernels for 2%

profile of v1, /device:TPU:0, one launch (start us, length us, event | category | flops | bytes accessed | tf_op | source)
XLA Modules:
  0.0 236.0 jit_solution(15930750023142136043)
XLA Ops:
  0.0 1.4 dynamic-slice_bitcast_fusion
  1.4 2.9 %broadcast_in_dim.26 = bf16[7168,384]{1,0:T(8,128)(2,1)} broadcast(bf16[]{:T(256)} %constant.75.clone.1), dimensions={} | broadcast | bytes 5505026 | tf_op jit(solution)/shard_map/broadcast_in_dim | solution.py:218
  4.4 1.1 pad_maximum_fusion.1
  5.4 2.9 %collective-permute-start.7 = (bf16[896,256]{1,0:T(8,128)(2,1)}, bf16[896,256]{1,0:T(8,128)(2,1)S(1)}, u32[]{:S(2)}, u32[]{:S(2)}) collective-permute-start(bf16[896,256]{1,0:T(8,128)(2,1)} %get-tuple-element.21), channel_id=1, source_target_pairs={{0,4},{4,0},{8,12},{12,8},{16,20},{20,16},{24,28},{28,24},{1,5},{5... | collective-permute-start | bytes 1376264 | tf_op jit(solution)/shard_map/ppermute | solution.py:20
  8.4 2.5 %collective-permute-start.5 = (bf16[896,256]{1,0:T(8,128)(2,1)}, bf16[896,256]{1,0:T(8,128)(2,1)S(1)}, u32[]{:S(2)}, u32[]{:S(2)}) collective-permute-start(bf16[896,256]{1,0:T(8,128)(2,1)} %get-tuple-element.21), channel_id=1, source_target_pairs={{0,16},{4,20},{8,24},{12,28},{16,0},{20,4},{24,8},{28,12},{1,17},{... | collective-permute-start | bytes 1376264 | tf_op jit(solution)/shard_map/ppermute | solution.py:20
  10.9 2.2 constant_dynamic-slice_fusion.2
  13.1 1.6 collective-permute-start
  15.2 1.5 constant_dynamic-slice_fusion.1
  16.7 1.6 collective-permute-start.21
  18.3 5.8 %concatenate.31 = bf16[512,7168]{1,0:T(8,128)(2,1)} pad(bf16[256,7168]{1,0:T(8,128)(2,1)} %param.4, bf16[]{:T(256)} %constant.75.clone.1), padding=0_256x0_0 | pad | bytes 11010050 | tf_op jit(solution)/shard_map/concatenate | solution.py:159
  25.9 1.9 constant_dynamic-update-slice_fusion.15
  27.7 27.2 %collective-permute-done.21 = bf16[256,128]{1,0:T(8,128)(2,1)} collective-permute-done((bf16[256,128]{1,0:T(8,128)(2,1)}, bf16[256,128]{1,0:T(8,128)(2,1)}, u32[]{:S(2)}, u32[]{:S(2)}) %collective-permute-start.21) | collective-permute-done | bytes 65568 | tf_op jit(solution)/shard_map/ppermute | solution.py:20
  55.8 2.4 %collective-permute-start.6 = (bf16[896,256]{1,0:T(8,128)(2,1)S(1)}, bf16[896,256]{1,0:T(8,128)(2,1)S(1)}, u32[]{:S(2)}, u32[]{:S(2)}) collective-permute-start(bf16[896,256]{1,0:T(8,128)(2,1)S(1)} %pad_maximum_fusion.2), channel_id=1, source_target_pairs={{0,24},{4,28},{8,16},{12,20},{16,8},{20,12},{24,0},{28,4},{1,25},{... | collective-permute-start | bytes 1376264 | tf_op jit(solution)/shard_map/ppermute | solution.py:20
  59.0 4.1 %collective-permute-done.11 = bf16[896,128]{1,0:T(8,128)(2,1)S(1)} collective-permute-done((bf16[896,128]{1,0:T(8,128)(2,1)S(1)}, bf16[896,128]{1,0:T(8,128)(2,1)S(1)}, u32[]{:S(2)}, u32[]{:S(2)}) %collective-permute-start.11) | collective-permute-done | bytes 229408 | tf_op jit(solution)/shard_map/ppermute | solution.py:20
  63.1 6.5 %collective-permute-start.12 = (bf16[896,128]{1,0:T(8,128)(2,1)S(1)}, bf16[896,128]{1,0:T(8,128)(2,1)S(1)}, u32[]{:S(2)}, u32[]{:S(2)}) collective-permute-start(bf16[896,128]{1,0:T(8,128)(2,1)S(1)} %get-tuple-element.10), channel_id=1, source_target_pairs={{0,16},{4,20},{8,24},{12,28},{16,0},{20,4},{24,8},{28,12},{1,17},{... | collective-permute-start | bytes 688136 | tf_op jit(solution)/shard_map/ppermute | solution.py:20
  71.0 1.3 collective-permute-start.1
  73.1 14.3 %collective-permute-done.12 = bf16[896,128]{1,0:T(8,128)(2,1)S(1)} collective-permute-done((bf16[896,128]{1,0:T(8,128)(2,1)S(1)}, bf16[896,128]{1,0:T(8,128)(2,1)S(1)}, u32[]{:S(2)}, u32[]{:S(2)}) %collective-permute-start.12) | collective-permute-done | bytes 229408 | tf_op jit(solution)/shard_map/ppermute | solution.py:20
  87.4 3.5 %collective-permute-start.13 = (bf16[896,128]{1,0:T(8,128)(2,1)S(1)}, bf16[896,128]{1,0:T(8,128)(2,1)S(1)}, u32[]{:S(2)}, u32[]{:S(2)}) collective-permute-start(bf16[896,128]{1,0:T(8,128)(2,1)S(1)} %get-tuple-element.16), channel_id=1, source_target_pairs={{0,24},{4,28},{8,16},{12,20},{16,8},{20,12},{24,0},{28,4},{1,25},{... | collective-permute-start | bytes 688136 | tf_op jit(solution)/shard_map/ppermute | solution.py:20
  93.0 2.3 collective-permute-done.13
  96.4 1.7 collective-permute-start.9
  98.1 0.9 constant_dynamic-update-slice_fusion.3
  100.0 5.0 %collective-permute-done.8 = bf16[896,256]{1,0:T(8,128)(2,1)S(1)} collective-permute-done((bf16[896,256]{1,0:T(8,128)(2,1)S(1)}, bf16[896,256]{1,0:T(8,128)(2,1)S(1)}, u32[]{:S(2)}, u32[]{:S(2)}) %collective-permute-start.8) | collective-permute-done | bytes 458784 | tf_op jit(solution)/shard_map/ppermute | solution.py:20
  105.9 14.0 %collective-permute-done.15 = bf16[896,128]{1,0:T(8,128)(2,1)S(1)} collective-permute-done((bf16[896,128]{1,0:T(8,128)(2,1)S(1)}, bf16[896,128]{1,0:T(8,128)(2,1)S(1)}, u32[]{:S(2)}, u32[]{:S(2)}) %collective-permute-start.15) | collective-permute-done | bytes 229408 | tf_op jit(solution)/shard_map/ppermute | solution.py:20
  122.1 4.3 %collective-permute-done.16 = bf16[896,128]{1,0:T(8,128)(2,1)S(1)} collective-permute-done((bf16[896,128]{1,0:T(8,128)(2,1)S(1)}, bf16[896,128]{1,0:T(8,128)(2,1)S(1)}, u32[]{:S(2)}, u32[]{:S(2)}) %collective-permute-start.16) | collective-permute-done | bytes 229408 | tf_op jit(solution)/shard_map/ppermute | solution.py:20
  127.5 2.1 collective-permute-start.10
  132.5 8.6 %collective-permute-done.10 = bf16[896,256]{1,0:T(8,128)(2,1)S(1)} collective-permute-done((bf16[896,256]{1,0:T(8,128)(2,1)S(1)}, bf16[896,256]{1,0:T(8,128)(2,1)S(1)}, u32[]{:S(2)}, u32[]{:S(2)}) %collective-permute-start.10) | collective-permute-done | bytes 458784 | tf_op jit(solution)/shard_map/ppermute | solution.py:20
  142.4 2.9 %collective-permute-start.26 = (bf16[512,256]{1,0:T(8,128)(2,1)S(1)}, bf16[512,256]{1,0:T(8,128)(2,1)S(1)}, u32[]{:S(2)}, u32[]{:S(2)}) collective-permute-start(bf16[512,256]{1,0:T(8,128)(2,1)S(1)} %fusion.9.refs_0_.kv_ref), channel_id=1, source_target_pairs={{0,16},{4,20},{8,24},{12,28},{16,0},{20,4},{24,8},{28,12},{1,17},{... | collective-permute-start | bytes 786440 | tf_op jit(solution)/shard_map/ppermute | solution.py:20
  147.8 1.2 collective-permute-start.27
  149.9 2.7 %collective-permute-start.24 = (bf16[512,128]{1,0:T(8,128)(2,1)S(1)}, bf16[512,128]{1,0:T(8,128)(2,1)S(1)}, u32[]{:S(2)}, u32[]{:S(2)}) collective-permute-start(bf16[512,128]{1,0:T(8,128)(2,1)S(1)} %pad_maximum_fusion.4.grad_ref.refs_4_), channel_id=1, source_target_pairs={{0,20},{4,16},{8,28},{12,24},{16,4},{20,0},{24,12},{28,8},{1,21},{... | collective-permute-start | bytes 393224 | tf_op jit(solution)/shard_map/ppermute | solution.py:20
  154.1 12.7 %collective-permute-done.26.refs_2_ = bf16[512,256]{1,0:T(8,128)(2,1)S(1)} collective-permute-done((bf16[512,256]{1,0:T(8,128)(2,1)S(1)}, bf16[512,256]{1,0:T(8,128)(2,1)S(1)}, u32[]{:S(2)}, u32[]{:S(2)}) %collective-permute-start.26) | collective-permute-done | bytes 262176 | tf_op jit(solution)/shard_map/ppermute | solution.py:20
  166.7 8.2 %collective-permute-done.27.refs_3_ = bf16[512,256]{1,0:T(8,128)(2,1)S(1)} collective-permute-done((bf16[512,256]{1,0:T(8,128)(2,1)S(1)}, bf16[512,256]{1,0:T(8,128)(2,1)S(1)}, u32[]{:S(2)}, u32[]{:S(2)}) %collective-permute-start.27) | collective-permute-done | bytes 262176 | tf_op jit(solution)/shard_map/ppermute | solution.py:20
  175.0 4.6 %shard_map.46 = (bf16[512,128]{1,0:T(8,128)(2,1)S(1)}, f32[8,512]{1,0:T(8,128)S(1)}) custom-call(s32[2,8]{1,0:T(2,128)S(1)} %get-tuple-element.26.limit_ref, bf16[512,128]{1,0:T(8,128)(2,1)S(1)} %fusion.15.q_ref.refs_0_, bf16[512,128]{1,0:T(8,128)(2,1)S(1)} %pad_maximum_fusion.4.grad_ref.refs_4_, bf16[512,256]{1,0:T(8,128)(2,1)S(1)} %fusion.9.refs_0_.kv_ref, ...), custom_call_target="tpu_custom_call" | custom-call | flops 1342177280 | bytes 4194304 | tf_op jit(solution)/shard_map/pallas_call | solution.py:200
  179.6 1.8 collective-permute-start.28
  181.3 2.7 %collective-permute-start.29 = (f32[8,512]{1,0:T(8,128)S(1)}, f32[8,512]{1,0:T(8,128)S(1)}, u32[]{:S(2)}, u32[]{:S(2)}) collective-permute-start(f32[8,512]{1,0:T(8,128)S(1)} %get-tuple-element.7.refs_8_), channel_id=1, source_target_pairs={{0,16},{4,20},{8,24},{12,28},{16,0},{20,4},{24,8},{28,12},{1,17},{... | collective-permute-start | bytes 49160 | tf_op jit(solution)/shard_map/ppermute | solution.py:20
  184.1 1.2 collective-permute-start.30
  186.0 3.6 %collective-permute-done.30.refs_11_ = f32[8,512]{1,0:T(8,128)S(1)} collective-permute-done((f32[8,512]{1,0:T(8,128)S(1)}, f32[8,512]{1,0:T(8,128)S(1)}, u32[]{:S(2)}, u32[]{:S(2)}) %collective-permute-start.30) | collective-permute-done | bytes 16416 | tf_op jit(solution)/shard_map/ppermute | solution.py:20
  189.6 3.8 %shard_map.47 = bf16[512,256]{1,0:T(8,128)(2,1)S(1)} custom-call(s32[2,8]{1,0:T(2,128)S(1)} %get-tuple-element.25.limit_ref, bf16[512,256]{1,0:T(8,128)(2,1)S(1)} %fusion.9.refs_0_.kv_ref, bf16[512,128]{1,0:T(8,128)(2,1)S(1)} %fusion.15.q_ref.refs_0_, bf16[512,128]{1,0:T(8,128)(2,1)S(1)} %collective-permute-done.18.refs_1_, ...), custom_call_target="tpu_custom_call" | custom-call | flops 1342177280 | bytes 4194304 | tf_op jit(solution)/shard_map/pallas_call | solution.py:210
  193.4 2.5 %convolution_convert_fusion = bf16[512,1792]{1,0:T(8,128)(2,1)S(1)} fusion(bf16[7168,384]{1,0:T(8,128)(2,1)} %constant_dynamic-update-slice_fusion.8, s32[]{:T(128)S(6)} %select_n.151, bf16[512,128]{1,0:T(8,128)(2,1)S(1)} %get-tuple-element.8, bf16[512,256]{1,0:T(8,128)(2,1)S(1)} %shard_map.47), kind=kOutput, calls=%fused_computation.4 | convolution fusion | flops 706347008 | bytes 3604484 | tf_op jit(solution)/shard_map/dot_general | solution.py:24
  196.0 2.5 %convolution_convert_fusion.1 = bf16[512,1792]{1,0:T(8,128)(2,1)S(1)} fusion(bf16[7168,384]{1,0:T(8,128)(2,1)} %constant_dynamic-update-slice_fusion.8, s32[]{:T(128)S(6)} %select_n.150, bf16[512,128]{1,0:T(8,128)(2,1)S(1)} %get-tuple-element.8, bf16[512,256]{1,0:T(8,128)(2,1)S(1)} %shard_map.47), kind=kOutput, calls=%fused_computation.5 | convolution fusion | flops 706347008 | bytes 3604484 | tf_op jit(solution)/shard_map/dot_general | solution.py:24
  199.7 2.5 %fusion.74 = (bf16[512,1792]{1,0:T(8,128)(2,1)S(1)}, f32[512,1792]{1,0:T(8,128)S(1)}) fusion(bf16[512,1792]{1,0:T(8,128)(2,1)S(1)} %collective-permute-done.32, bf16[7168,384]{1,0:T(8,128)(2,1)} %constant_dynamic-update-slice_fusion.8, s32[]{:T(128)S(6)} %select_n.149, bf16[512,128]{1,0:T(8,128)(2,1)S(1)} %get-tuple-element.8, ...), kind=kOutput, calls=%fused_computation.143 | convolution fusion | flops 708182016 | bytes 9109508 | tf_op jit(solution)/shard_map/dot_general | solution.py:24
  202.4 1.6 collective-permute-start.34
  204.5 2.5 %convert_add_fusion.1 = f32[512,1792]{1,0:T(8,128)S(1)} fusion(bf16[512,1792]{1,0:T(8,128)(2,1)S(1)} %collective-permute-done.31, bf16[7168,384]{1,0:T(8,128)(2,1)} %constant_dynamic-update-slice_fusion.8, s32[]{:T(128)S(6)} %select_n.148, bf16[512,128]{1,0:T(8,128)(2,1)S(1)} %get-tuple-element.8, bf16[512,256]{1,0:T(8,128)(2,1)S(1)} %shard_map.47), kind=kOutput, calls=%fused_computation.3 | convolution fusion | flops 707264512 | bytes 7274500 | tf_op jit(solution)/shard_map/dot_general | solution.py:24
  207.1 2.0 collective-permute-start.38
  209.1 6.7 %collective-permute-done.36 = bf16[256,896]{1,0:T(8,128)(2,1)S(1)} collective-permute-done((bf16[256,896]{1,0:T(8,128)(2,1)S(1)}, bf16[256,896]{1,0:T(8,128)(2,1)S(1)}, u32[]{:S(2)}, u32[]{:S(2)}) %collective-permute-start.36) | collective-permute-done | bytes 458784 | tf_op jit(solution)/shard_map/ppermute | solution.py:20
  215.9 1.6 collective-permute-start.37
  218.0 7.7 %collective-permute-done.33 = bf16[256,896]{1,0:T(8,128)(2,1)S(1)} collective-permute-done((bf16[256,896]{1,0:T(8,128)(2,1)S(1)}, bf16[256,896]{1,0:T(8,128)(2,1)S(1)}, u32[]{:S(2)}, u32[]{:S(2)}) %collective-permute-start.33) | collective-permute-done | bytes 458784 | tf_op jit(solution)/shard_map/ppermute | solution.py:20
  225.7 9.0 %collective-permute-done.37 = bf16[256,896]{1,0:T(8,128)(2,1)S(1)} collective-permute-done((bf16[256,896]{1,0:T(8,128)(2,1)S(1)}, bf16[256,896]{1,0:T(8,128)(2,1)S(1)}, u32[]{:S(2)}, u32[]{:S(2)}) %collective-permute-start.37) | collective-permute-done | bytes 458784 | tf_op jit(solution)/shard_map/ppermute | solution.py:20
  235.0 1.0 pad_maximum_fusion
  (103 shorter events, 27.2 us)
Async XLA Ops:
  0.0 24.3 %copy-start = (s32[4,4]{1,0:T(4,128)S(1)}, s32[4,4]{1,0:T(4,128)}, u32[]{:S(2)}) copy-start(s32[4,4]{1,0:T(4,128)} %param.6) | copy-start | bytes 196
  5.4 90.9 %collective-permute-start.7 = (bf16[896,256]{1,0:T(8,128)(2,1)}, bf16[896,256]{1,0:T(8,128)(2,1)S(1)}, u32[]{:S(2)}, u32[]{:S(2)}) collective-permute-start(bf16[896,256]{1,0:T(8,128)(2,1)} %get-tuple-element.21), channel_id=1, source_target_pairs={{0,4},{4,0},{8,12},{12,8},{16,20},{20,16},{24,28},{28,24},{1,5},{5... | collective-permute-start | bytes 1376264 | tf_op jit(solution)/shard_map/ppermute | solution.py:20
  8.4 62.0 %collective-permute-start.5 = (bf16[896,256]{1,0:T(8,128)(2,1)}, bf16[896,256]{1,0:T(8,128)(2,1)S(1)}, u32[]{:S(2)}, u32[]{:S(2)}) collective-permute-start(bf16[896,256]{1,0:T(8,128)(2,1)} %get-tuple-element.21), channel_id=1, source_target_pairs={{0,16},{4,20},{8,24},{12,28},{16,0},{20,4},{24,8},{28,12},{1,17},{... | collective-permute-start | bytes 1376264 | tf_op jit(solution)/shard_map/ppermute | solution.py:20
  13.1 58.0 %collective-permute-start = (bf16[256,1792]{1,0:T(8,128)(2,1)}, bf16[256,1792]{1,0:T(8,128)(2,1)S(1)}, u32[]{:S(2)}, u32[]{:S(2)}) collective-permute-start(bf16[256,1792]{1,0:T(8,128)(2,1)} %constant_dynamic-slice_fusion.2), channel_id=1, source_target_pairs={{0,8},{4,12},{8,0},{12,4},{16,24},{20,28},{24,16},{28,20},{1,9},{5... | collective-permute-start | bytes 2752520 | tf_op jit(solution)/shard_map/ppermute | solution.py:20
  14.7 41.0 %collective-permute-start.4 = (bf16[896,256]{1,0:T(8,128)(2,1)S(1)}, bf16[896,256]{1,0:T(8,128)(2,1)S(1)}, u32[]{:S(2)}, u32[]{:S(2)}) collective-permute-start(bf16[896,256]{1,0:T(8,128)(2,1)S(1)} %pad_maximum_fusion.2), channel_id=1, source_target_pairs={{0,8},{4,12},{8,0},{12,4},{16,24},{20,28},{24,16},{28,20},{1,9},{5... | collective-permute-start | bytes 1376264 | tf_op jit(solution)/shard_map/ppermute | solution.py:20
  16.7 38.2 %collective-permute-start.21 = (bf16[256,128]{1,0:T(8,128)(2,1)}, bf16[256,128]{1,0:T(8,128)(2,1)}, u32[]{:S(2)}, u32[]{:S(2)}) collective-permute-start(bf16[256,128]{1,0:T(8,128)(2,1)} %get-tuple-element.24), channel_id=1, source_target_pairs={{0,8},{4,12},{8,0},{12,4},{16,24},{20,28},{24,16},{28,20},{1,9},{5... | collective-permute-start | bytes 196616 | tf_op jit(solution)/shard_map/ppermute | solution.py:20
  25.6 101.7 %copy-start.1 = (bf16[512,7168]{1,0:T(8,128)(2,1)S(1)}, bf16[512,7168]{1,0:T(8,128)(2,1)}, u32[]{:S(2)}) copy-start(bf16[512,7168]{1,0:T(8,128)(2,1)} %concatenate.31) | copy-start | bytes 22020100
  54.9 8.2 %collective-permute-start.11 = (bf16[896,128]{1,0:T(8,128)(2,1)S(1)}, bf16[896,128]{1,0:T(8,128)(2,1)S(1)}, u32[]{:S(2)}, u32[]{:S(2)}) collective-permute-start(bf16[896,128]{1,0:T(8,128)(2,1)S(1)} %get-tuple-element.16), channel_id=1, source_target_pairs={{0,8},{4,12},{8,0},{12,4},{16,24},{20,28},{24,16},{28,20},{1,9},{5... | collective-permute-start | bytes 688136 | tf_op jit(solution)/shard_map/ppermute | solution.py:20
  55.8 35.9 %collective-permute-start.6 = (bf16[896,256]{1,0:T(8,128)(2,1)S(1)}, bf16[896,256]{1,0:T(8,128)(2,1)S(1)}, u32[]{:S(2)}, u32[]{:S(2)}) collective-permute-start(bf16[896,256]{1,0:T(8,128)(2,1)S(1)} %pad_maximum_fusion.2), channel_id=1, source_target_pairs={{0,24},{4,28},{8,16},{12,20},{16,8},{20,12},{24,0},{28,4},{1,25},{... | collective-permute-start | bytes 1376264 | tf_op jit(solution)/shard_map/ppermute | solution.py:20
  63.1 24.4 %collective-permute-start.12 = (bf16[896,128]{1,0:T(8,128)(2,1)S(1)}, bf16[896,128]{1,0:T(8,128)(2,1)S(1)}, u32[]{:S(2)}, u32[]{:S(2)}) collective-permute-start(bf16[896,128]{1,0:T(8,128)(2,1)S(1)} %get-tuple-element.10), channel_id=1, source_target_pairs={{0,16},{4,20},{8,24},{12,28},{16,0},{20,4},{24,8},{28,12},{1,17},{... | collective-permute-start | bytes 688136 | tf_op jit(solution)/shard_map/ppermute | solution.py:20
  70.4 28.6 %collective-permute-start.14 = (bf16[896,128]{1,0:T(8,128)(2,1)S(1)}, bf16[896,128]{1,0:T(8,128)(2,1)S(1)}, u32[]{:S(2)}, u32[]{:S(2)}) collective-permute-start(bf16[896,128]{1,0:T(8,128)(2,1)S(1)} %get-tuple-element.10), channel_id=1, source_target_pairs={{0,4},{4,0},{8,12},{12,8},{16,20},{20,16},{24,28},{28,24},{1,5},{5... | collective-permute-start | bytes 688136 | tf_op jit(solution)/shard_map/ppermute | solution.py:20
  71.0 50.2 %collective-permute-start.1 = (bf16[256,1792]{1,0:T(8,128)(2,1)S(1)}, bf16[256,1792]{1,0:T(8,128)(2,1)S(1)}, u32[]{:S(2)}, u32[]{:S(2)}) collective-permute-start(bf16[256,1792]{1,0:T(8,128)(2,1)S(1)} %collective-permute-done), channel_id=1, source_target_pairs={{0,2},{1,3},{2,0},{3,1},{4,6},{5,7},{6,4},{7,5},{8,10},{9,11},{10,... | collective-permute-start | bytes 2752520 | tf_op jit(solution)/shard_map/ppermute | solution.py:20
  87.4 7.9 %collective-permute-start.13 = (bf16[896,128]{1,0:T(8,128)(2,1)S(1)}, bf16[896,128]{1,0:T(8,128)(2,1)S(1)}, u32[]{:S(2)}, u32[]{:S(2)}) collective-permute-start(bf16[896,128]{1,0:T(8,128)(2,1)S(1)} %get-tuple-element.16), channel_id=1, source_target_pairs={{0,24},{4,28},{8,16},{12,20},{16,8},{20,12},{24,0},{28,4},{1,25},{... | collective-permute-start | bytes 688136 | tf_op jit(solution)/shard_map/ppermute | solution.py:20
  91.6 13.5 %collective-permute-start.8 = (bf16[896,256]{1,0:T(8,128)(2,1)S(1)}, bf16[896,256]{1,0:T(8,128)(2,1)S(1)}, u32[]{:S(2)}, u32[]{:S(2)}) collective-permute-start(bf16[896,256]{1,0:T(8,128)(2,1)S(1)} %collective-permute-done.4), channel_id=1, source_target_pairs={{0,4},{4,0},{8,12},{12,8},{16,20},{20,16},{24,28},{28,24},{1,5},{5... | collective-permute-start | bytes 1376264 | tf_op jit(solution)/shard_map/ppermute | solution.py:20
  95.3 54.6 %collective-permute-start.22 = (bf16[512,128]{1,0:T(8,128)(2,1)S(1)}, bf16[512,128]{1,0:T(8,128)(2,1)S(1)}, u32[]{:S(2)}, u32[]{:S(2)}) collective-permute-start(bf16[512,128]{1,0:T(8,128)(2,1)S(1)} %pad_maximum_fusion.4.grad_ref.refs_4_), channel_id=1, source_target_pairs={{0,4},{4,0},{8,12},{12,8},{16,20},{20,16},{24,28},{28,24},{1,5},{5... | collective-permute-start | bytes 393224 | tf_op jit(solution)/shard_map/ppermute | solution.py:20
  96.4 24.8 %collective-permute-start.9 = (bf16[896,256]{1,0:T(8,128)(2,1)S(1)}, bf16[896,256]{1,0:T(8,128)(2,1)S(1)}, u32[]{:S(2)}, u32[]{:S(2)}) collective-permute-start(bf16[896,256]{1,0:T(8,128)(2,1)S(1)} %collective-permute-done.5), channel_id=1, source_target_pairs={{0,4},{4,0},{8,12},{12,8},{16,20},{20,16},{24,28},{28,24},{1,5},{5... | collective-permute-start | bytes 1376264 | tf_op jit(solution)/shard_map/ppermute | solution.py:20
  98.9 20.9 %collective-permute-start.15 = (bf16[896,128]{1,0:T(8,128)(2,1)S(1)}, bf16[896,128]{1,0:T(8,128)(2,1)S(1)}, u32[]{:S(2)}, u32[]{:S(2)}) collective-permute-start(bf16[896,128]{1,0:T(8,128)(2,1)S(1)} %collective-permute-done.11), channel_id=1, source_target_pairs={{0,4},{4,0},{8,12},{12,8},{16,20},{20,16},{24,28},{28,24},{1,5},{5... | collective-permute-start | bytes 688136 | tf_op jit(solution)/shard_map/ppermute | solution.py:20
  105.1 22.4 %collective-permute-start.2 = (bf16[256,1792]{1,0:T(8,128)(2,1)S(1)}, bf16[256,1792]{1,0:T(8,128)(2,1)S(1)}, u32[]{:S(2)}, u32[]{:S(2)}) collective-permute-start(bf16[256,1792]{1,0:T(8,128)(2,1)S(1)} %collective-permute-done), channel_id=1, source_target_pairs={{0,1},{1,0},{2,3},{3,2},{4,5},{5,4},{6,7},{7,6},{8,9},{9,8},{10,11... | collective-permute-start | bytes 2752520 | tf_op jit(solution)/shard_map/ppermute | solution.py:20
  119.9 6.6 %collective-permute-start.16 = (bf16[896,128]{1,0:T(8,128)(2,1)S(1)}, bf16[896,128]{1,0:T(8,128)(2,1)S(1)}, u32[]{:S(2)}, u32[]{:S(2)}) collective-permute-start(bf16[896,128]{1,0:T(8,128)(2,1)S(1)} %collective-permute-done.12), channel_id=1, source_target_pairs={{0,4},{4,0},{8,12},{12,8},{16,20},{20,16},{24,28},{28,24},{1,5},{5... | collective-permute-start | bytes 688136 | tf_op jit(solution)/shard_map/ppermute | solution.py:20
  121.2 58.3 %collective-permute-start.23 = (bf16[512,128]{1,0:T(8,128)(2,1)S(1)}, bf16[512,128]{1,0:T(8,128)(2,1)S(1)}, u32[]{:S(2)}, u32[]{:S(2)}) collective-permute-start(bf16[512,128]{1,0:T(8,128)(2,1)S(1)} %pad_maximum_fusion.4.grad_ref.refs_4_), channel_id=1, source_target_pairs={{0,16},{4,20},{8,24},{12,28},{16,0},{20,4},{24,8},{28,12},{1,17},{... | collective-permute-start | bytes 393224 | tf_op jit(solution)/shard_map/ppermute | solution.py:20
  121.2 8.4 %collective-permute-start.3 = (bf16[256,1792]{1,0:T(8,128)(2,1)S(1)}, bf16[256,1792]{1,0:T(8,128)(2,1)S(1)}, u32[]{:S(2)}, u32[]{:S(2)}) collective-permute-start(bf16[256,1792]{1,0:T(8,128)(2,1)S(1)} %collective-permute-done.1), channel_id=1, source_target_pairs={{0,1},{1,0},{2,3},{3,2},{4,5},{5,4},{6,7},{7,6},{8,9},{9,8},{10,11... | collective-permute-start | bytes 2752520 | tf_op jit(solution)/shard_map/ppermute | solution.py:20
  126.5 21.3 %collective-permute-start.17 = (bf16[896,128]{1,0:T(8,128)(2,1)S(1)}, bf16[896,128]{1,0:T(8,128)(2,1)S(1)}, u32[]{:S(2)}, u32[]{:S(2)}) collective-permute-start(bf16[896,128]{1,0:T(8,128)(2,1)S(1)} %collective-permute-done.13), channel_id=1, source_target_pairs={{0,4},{4,0},{8,12},{12,8},{16,20},{20,16},{24,28},{28,24},{1,5},{5... | collective-permute-start | bytes 688136 | tf_op jit(solution)/shard_map/ppermute | solution.py:20
  127.5 13.6 %collective-permute-start.10 = (bf16[896,256]{1,0:T(8,128)(2,1)S(1)}, bf16[896,256]{1,0:T(8,128)(2,1)S(1)}, u32[]{:S(2)}, u32[]{:S(2)}) collective-permute-start(bf16[896,256]{1,0:T(8,128)(2,1)S(1)} %collective-permute-done.6), channel_id=1, source_target_pairs={{0,4},{4,0},{8,12},{12,8},{16,20},{20,16},{24,28},{28,24},{1,5},{5... | collective-permute-start | bytes 1376264 | tf_op jit(solution)/shard_map/ppermute | solution.py:20
  142.0 10.6 %collective-permute-start.25 = (bf16[512,256]{1,0:T(8,128)(2,1)S(1)}, bf16[512,256]{1,0:T(8,128)(2,1)S(1)}, u32[]{:S(2)}, u32[]{:S(2)}) collective-permute-start(bf16[512,256]{1,0:T(8,128)(2,1)S(1)} %fusion.9.refs_0_.kv_ref), channel_id=1, source_target_pairs={{0,4},{4,0},{8,12},{12,8},{16,20},{20,16},{24,28},{28,24},{1,5},{5... | collective-permute-start | bytes 786440 | tf_op jit(solution)/shard_map/ppermute | solution.py:20
  142.4 24.4 %collective-permute-start.26 = (bf16[512,256]{1,0:T(8,128)(2,1)S(1)}, bf16[512,256]{1,0:T(8,128)(2,1)S(1)}, u32[]{:S(2)}, u32[]{:S(2)}) collective-permute-start(bf16[512,256]{1,0:T(8,128)(2,1)S(1)} %fusion.9.refs_0_.kv_ref), channel_id=1, source_target_pairs={{0,16},{4,20},{8,24},{12,28},{16,0},{20,4},{24,8},{28,12},{1,17},{... | collective-permute-start | bytes 786440 | tf_op jit(solution)/shard_map/ppermute | solution.py:20
  147.8 27.2 %collective-permute-start.27 = (bf16[512,256]{1,0:T(8,128)(2,1)S(1)}, bf16[512,256]{1,0:T(8,128)(2,1)S(1)}, u32[]{:S(2)}, u32[]{:S(2)}) collective-permute-start(bf16[512,256]{1,0:T(8,128)(2,1)S(1)} %fusion.9.refs_0_.kv_ref), channel_id=1, source_target_pairs={{0,20},{4,16},{8,28},{12,24},{16,4},{20,0},{24,12},{28,8},{1,21},{... | collective-permute-start | bytes 786440 | tf_op jit(solution)/shard_map/ppermute | solution.py:20
  149.9 31.4 %collective-permute-start.24 = (bf16[512,128]{1,0:T(8,128)(2,1)S(1)}, bf16[512,128]{1,0:T(8,128)(2,1)S(1)}, u32[]{:S(2)}, u32[]{:S(2)}) collective-permute-start(bf16[512,128]{1,0:T(8,128)(2,1)S(1)} %pad_maximum_fusion.4.grad_ref.refs_4_), channel_id=1, source_target_pairs={{0,20},{4,16},{8,28},{12,24},{16,4},{20,0},{24,12},{28,8},{1,21},{... | collective-permute-start | bytes 393224 | tf_op jit(solution)/shard_map/ppermute | solution.py:20
  152.6 31.4 %collective-permute-start.18 = (bf16[512,128]{1,0:T(8,128)(2,1)S(1)}, bf16[512,128]{1,0:T(8,128)(2,1)S(1)}, u32[]{:S(2)}, u32[]{:S(2)}) collective-permute-start(bf16[512,128]{1,0:T(8,128)(2,1)S(1)} %fusion.15.q_ref.refs_0_), channel_id=1, source_target_pairs={{0,4},{4,0},{8,12},{12,8},{16,20},{20,16},{24,28},{28,24},{1,5},{5... | collective-permute-start | bytes 393224 | tf_op jit(solution)/shard_map/ppermute | solution.py:20
  166.7 19.2 %collective-permute-start.19 = (bf16[512,128]{1,0:T(8,128)(2,1)S(1)}, bf16[512,128]{1,0:T(8,128)(2,1)S(1)}, u32[]{:S(2)}, u32[]{:S(2)}) collective-permute-start(bf16[512,128]{1,0:T(8,128)(2,1)S(1)} %fusion.15.q_ref.refs_0_), channel_id=1, source_target_pairs={{0,16},{4,20},{8,24},{12,28},{16,0},{20,4},{24,8},{28,12},{1,17},{... | collective-permute-start | bytes 393224 | tf_op jit(solution)/shard_map/ppermute | solution.py:20
  175.0 11.0 %collective-permute-start.20 = (bf16[512,128]{1,0:T(8,128)(2,1)S(1)}, bf16[512,128]{1,0:T(8,128)(2,1)S(1)}, u32[]{:S(2)}, u32[]{:S(2)}) collective-permute-start(bf16[512,128]{1,0:T(8,128)(2,1)S(1)} %fusion.15.q_ref.refs_0_), channel_id=1, source_target_pairs={{0,20},{4,16},{8,28},{12,24},{16,4},{20,0},{24,12},{28,8},{1,21},{... | collective-permute-start | bytes 393224 | tf_op jit(solution)/shard_map/ppermute | solution.py:20
  179.6 6.4 %collective-permute-start.28 = (f32[8,512]{1,0:T(8,128)S(1)}, f32[8,512]{1,0:T(8,128)S(1)}, u32[]{:S(2)}, u32[]{:S(2)}) collective-permute-start(f32[8,512]{1,0:T(8,128)S(1)} %get-tuple-element.7.refs_8_), channel_id=1, source_target_pairs={{0,4},{4,0},{8,12},{12,8},{16,20},{20,16},{24,28},{28,24},{1,5},{5... | collective-permute-start | bytes 49160 | tf_op jit(solution)/shard_map/ppermute | solution.py:20
  181.3 4.6 %collective-permute-start.29 = (f32[8,512]{1,0:T(8,128)S(1)}, f32[8,512]{1,0:T(8,128)S(1)}, u32[]{:S(2)}, u32[]{:S(2)}) collective-permute-start(f32[8,512]{1,0:T(8,128)S(1)} %get-tuple-element.7.refs_8_), channel_id=1, source_target_pairs={{0,16},{4,20},{8,24},{12,28},{16,0},{20,4},{24,8},{28,12},{1,17},{... | collective-permute-start | bytes 49160 | tf_op jit(solution)/shard_map/ppermute | solution.py:20
  184.1 5.5 %collective-permute-start.30 = (f32[8,512]{1,0:T(8,128)S(1)}, f32[8,512]{1,0:T(8,128)S(1)}, u32[]{:S(2)}, u32[]{:S(2)}) collective-permute-start(f32[8,512]{1,0:T(8,128)S(1)} %get-tuple-element.7.refs_8_), channel_id=1, source_target_pairs={{0,20},{4,16},{8,28},{12,24},{16,4},{20,0},{24,12},{28,8},{1,21},{... | collective-permute-start | bytes 49160 | tf_op jit(solution)/shard_map/ppermute | solution.py:20
  195.9 3.9 %collective-permute-start.32 = (bf16[512,1792]{1,0:T(8,128)(2,1)S(1)}, bf16[512,1792]{1,0:T(8,128)(2,1)S(1)}, u32[]{:S(2)}, u32[]{:S(2)}) collective-permute-start(bf16[512,1792]{1,0:T(8,128)(2,1)S(1)} %convolution_convert_fusion), channel_id=1, source_target_pairs={{0,1},{1,0},{2,3},{3,2},{4,5},{5,4},{6,7},{7,6},{8,9},{9,8},{10,11... | collective-permute-start | bytes 5505032 | tf_op jit(solution)/shard_map/ppermute | solution.py:20
  198.5 6.1 %collective-permute-start.31 = (bf16[512,1792]{1,0:T(8,128)(2,1)S(1)}, bf16[512,1792]{1,0:T(8,128)(2,1)S(1)}, u32[]{:S(2)}, u32[]{:S(2)}) collective-permute-start(bf16[512,1792]{1,0:T(8,128)(2,1)S(1)} %convolution_convert_fusion.1), channel_id=1, source_target_pairs={{0,1},{1,0},{2,3},{3,2},{4,5},{5,4},{6,7},{7,6},{8,9},{9,8},{10,11... | collective-permute-start | bytes 5505032 | tf_op jit(solution)/shard_map/ppermute | solution.py:20
  202.4 13.4 %collective-permute-start.36 = (bf16[256,896]{1,0:T(8,128)(2,1)S(1)}, bf16[256,896]{1,0:T(8,128)(2,1)S(1)}, u32[]{:S(2)}, u32[]{:S(2)}) collective-permute-start(bf16[256,896]{1,0:T(8,128)(2,1)S(1)} %get-tuple-element.14), channel_id=1, source_target_pairs={{0,8},{4,12},{8,0},{12,4},{16,24},{20,28},{24,16},{28,20},{1,9},{5... | collective-permute-start | bytes 1376264 | tf_op jit(solution)/shard_map/ppermute | solution.py:20
  202.4 15.1 %collective-permute-start.34 = (bf16[256,896]{1,0:T(8,128)(2,1)S(1)}, bf16[256,896]{1,0:T(8,128)(2,1)S(1)}, u32[]{:S(2)}, u32[]{:S(2)}) collective-permute-start(bf16[256,896]{1,0:T(8,128)(2,1)S(1)} %get-tuple-element.15), channel_id=1, source_target_pairs={{0,2},{1,3},{2,0},{3,1},{4,6},{5,7},{6,4},{7,5},{8,10},{9,11},{10,... | collective-permute-start | bytes 1376264 | tf_op jit(solution)/shard_map/ppermute | solution.py:20
  204.0 21.7 %collective-permute-start.33 = (bf16[256,896]{1,0:T(8,128)(2,1)S(1)}, bf16[256,896]{1,0:T(8,128)(2,1)S(1)}, u32[]{:S(2)}, u32[]{:S(2)}) collective-permute-start(bf16[256,896]{1,0:T(8,128)(2,1)S(1)} %get-tuple-element.13), channel_id=1, source_target_pairs={{0,2},{1,3},{2,0},{3,1},{4,6},{5,7},{6,4},{7,5},{8,10},{9,11},{10,... | collective-permute-start | bytes 1376264 | tf_op jit(solution)/shard_map/ppermute | solution.py:20
  207.1 18.6 %collective-permute-start.38 = (bf16[256,896]{1,0:T(8,128)(2,1)S(1)}, bf16[256,896]{1,0:T(8,128)(2,1)S(1)}, u32[]{:S(2)}, u32[]{:S(2)}) collective-permute-start(bf16[256,896]{1,0:T(8,128)(2,1)S(1)} %slice.97), channel_id=1, source_target_pairs={{0,8},{4,12},{8,0},{12,4},{16,24},{20,28},{24,16},{28,20},{1,9},{5... | collective-permute-start | bytes 1376264 | tf_op jit(solution)/shard_map/ppermute | solution.py:20
  215.9 18.8 %collective-permute-start.37 = (bf16[256,896]{1,0:T(8,128)(2,1)S(1)}, bf16[256,896]{1,0:T(8,128)(2,1)S(1)}, u32[]{:S(2)}, u32[]{:S(2)}) collective-permute-start(bf16[256,896]{1,0:T(8,128)(2,1)S(1)} %fusion.16), channel_id=1, source_target_pairs={{0,2},{1,3},{2,0},{3,1},{4,6},{5,7},{6,4},{7,5},{8,10},{9,11},{10,... | collective-permute-start | bytes 1376264 | tf_op jit(solution)/shard_map/ppermute | solution.py:20
  217.6 17.1 %collective-permute-start.35 = (bf16[256,896]{1,0:T(8,128)(2,1)S(1)}, bf16[256,896]{1,0:T(8,128)(2,1)S(1)}, u32[]{:S(2)}, u32[]{:S(2)}) collective-permute-start(bf16[256,896]{1,0:T(8,128)(2,1)S(1)} %fusion.19), channel_id=1, source_target_pairs={{0,8},{4,12},{8,0},{12,4},{16,24},{20,28},{24,16},{28,20},{1,9},{5... | collective-permute-start | bytes 1376264 | tf_op jit(solution)/shard_map/ppermute | solution.py:20

commit v2 on v1

--- a/solution.py
+++ b/solution.py
@@ -13,11 +13,39 @@
 PAIR = 2
 F32 = jnp.float32
 BF16 = jnp.bfloat16
+HOLD_FLOPS = 20_000_000_000
 VMEM_LIMIT = 48 * 1024 * 1024
 
 
-def swap(array, axis, size, distance):
-    return lax.ppermute(array, axis, [(i, i ^ distance) for i in range(size)])
+def swap(array, axis, size, distance, sender=lambda i: True):
+    pairs = [(i, i ^ distance) for i in range(size) if sender(i)]
+    return lax.ppermute(array, axis, pairs)
+
+
+def hold_kernel(in_ref, out_ref):
+    out_ref[...] = in_ref[...]
+
+
+def hold(token):
+    return pl.pallas_call(
+        hold_kernel,
+        out_shape=jax.ShapeDtypeStruct(token.shape, token.dtype),
+        cost_estimate=pl.CostEstimate(flops=HOLD_FLOPS, bytes_accessed=1024, transcendentals=0),
+    )(token)
+
+
+class Order:
+    def __init__(self, token):
+        self.token = token
+
+    def wait(self, value):
+        value, token = lax.optimization_barrier((value, self.token))
+        self.token = hold(token)
+        return value
+
+    def after(self, *values):
+        tied = lax.optimization_barrier((*values, self.token))[: len(values)]
+        return tied if len(values) > 1 else tied[0]
 
 
 def dot_nt(a, b):
@@ -141,50 +169,109 @@
     kv_of = lambda w: jnp.concatenate([w[:, 1], w[:, 2]], axis=1)
     q_of = lambda w: w[:, 0]
 
-    def gather_pieces(own, other):
-        pieces = {0: own}
-        for d in even[1:]:
-            pieces[d] = over_ctx(other if d & PAIR else own, distance=d)
-        for d in even:
-            pieces[d ^ 1] = over_ctx(pieces[d], distance=1)
-        return pieces
-
-    part = lax.dynamic_slice_in_dim(inputs, f * per_f, per_f, axis=1)
-    parts = {0: over_ctx(part, distance=PAIR)}
-    bit = n_f // 2
-    while bit:
-        for e in list(parts):
-            parts[e ^ bit] = over_f(parts[e], distance=bit)
-        bit //= 2
-    both = jnp.concatenate([inputs, jnp.zeros_like(inputs)], axis=0)
-    for e, value in parts.items():
-        both = lax.dynamic_update_slice(both, value, (run, (f ^ e) * per_f))
-
-    kv_pieces = gather_pieces(kv_of(own_w), kv_of(other_w))
-    q_pieces = gather_pieces(q_of(own_w), q_of(other_w))
+    kv_own, kv_other, q_own, q_other = kv_of(own_w), kv_of(other_w), q_of(own_w), q_of(other_w)
+    order = Order(jnp.zeros((8, HD), F32))
+    near, *mids = even[1:]
+    parity = c % 2
+    kv_pieces, q_pieces = {0: kv_own}, {0: q_own}
+
+    def part(which):
+        return lax.dynamic_slice_in_dim(inputs, f * per_f + which * step, step, axis=1)
+
+    step = per_f // 2 if per_f > depth else per_f
+    part_a, part_b = part(parity if per_f > depth else 0), part(1 - parity)
+
+    def send(pieces, d, own, other):
+        pieces[d] = over_ctx(other if d & PAIR else own, distance=d)
+
+    def relay(pieces, d):
+        pieces[d ^ 1] = over_ctx(pieces[d], distance=1)
+
+    def arrive(pieces, *ds):
+        for d in ds:
+            pieces[d] = order.wait(pieces[d])
+
+    def spread(held, bit):
+        for e in list(held):
+            held[e ^ bit] = over_f(held[e], distance=bit)
+
+    relay(kv_pieces, 0)
+    send(kv_pieces, mids[0], kv_own, kv_other)
+    send(kv_pieces, near, kv_own, kv_other)
+    arrive(kv_pieces, near, mids[0])
+    relay(kv_pieces, mids[0])
+    relay(kv_pieces, near)
+    part_a, kv_other, kv_own, q_pieces[0], other_grad = order.after(
+        part_a, kv_other, kv_own, q_own, head_of(d_attn, 1 - mine)
+    )
+    held_a = {0: over_ctx(part_a, distance=PAIR)}
+    for d in mids[1:]:
+        send(kv_pieces, d, kv_own, kv_other)
+    relay(q_pieces, 0)
+    arrive(held_a, 0)
+    bits = [1 << i for i in reversed(range(n_f.bit_length() - 1))]
+    spread(held_a, bits[0])
+    part_b, other_grad = order.after(part_b, other_grad)
+    held_b = {0: over_ctx(part_b, distance=PAIR)}
+    other_grad = over_ctx(other_grad, distance=PAIR)
+    for d in mids[1:]:
+        arrive(kv_pieces, d)
+        relay(kv_pieces, d)
+    q_own, q_other = order.after(q_own, q_other)
+    for d in mids + [near]:
+        send(q_pieces, d, q_own, q_other)
+    arrive(held_a, bits[0])
+    for bit in bits[1:]:
+        spread(held_a, bit)
+    arrive(held_b, 0)
+    spread(held_b, bits[0])
+    arrive(kv_pieces, 1, near ^ 1, mids[0] ^ 1)
+    for d in mids + [near]:
+        arrive(q_pieces, d)
+        relay(q_pieces, d)
+    arrive(held_b, bits[0])
+    for bit in bits[1:]:
+        spread(held_b, bit)
+    arrive(kv_pieces, *[d ^ 1 for d in mids[1:]])
+
+    if per_f > depth:
+        partner = [jnp.concatenate([held[e] for e in range(n_f)], axis=1) for held in (held_a, held_b)]
+    else:
+        partner = [jnp.concatenate([held_a[e] for e in range(n_f)], axis=1)] * 2
 
     def project(pieces):
-        total = None
-        for d, w in pieces.items():
-            rows = lax.dynamic_slice_in_dim(both, (c ^ d) * depth, depth, axis=1)
-            term = dot_nn(rows, w)
-            total = term if total is None else total + term
-        return total.astype(BF16)
-
-    own_grad = head_of(d_attn, mine)
-    grad = jnp.concatenate(
-        [own_grad, over_ctx(head_of(d_attn, 1 - mine), distance=PAIR)], axis=0
-    )
-    grads = [grad] + [over_ctx(grad, distance=d) for d in group[1:]]
+        totals = [None, None]
+        for d in sorted(pieces, key=lambda d: (d & 1, d)):
+            start = (c ^ d) * depth
+            other_start = ((start // per_f) ^ f) * step
+            for i, (rows, at) in enumerate(((inputs, start), (partner[d & 1], other_start))):
+                term = dot_nn(lax.dynamic_slice_in_dim(rows, at, depth, axis=1), pieces[d])
+                totals[i] = term if totals[i] is None else totals[i] + term
+        return jnp.concatenate(totals, axis=0).astype(BF16)
+
+    def top(d):
+        return 1 << (d.bit_length() - 1)
+
+    def to_later(array, d):
+        ordered = top(d) > PAIR
+        return over_ctx(array, distance=d, sender=lambda i: not (ordered and i & top(d)))
+
+    def to_earlier(array, d):
+        ordered = top(d) > PAIR
+        return over_ctx(array, distance=d, sender=lambda i: not ordered or i & top(d))
 
     kv = project(kv_pieces)
-    kvs = [kv] + [over_ctx(kv, distance=d) for d in group[1:]]
+    kvs = [kv] + [to_later(kv, d) for d in group[1:]]
+    grad = jnp.concatenate([head_of(d_attn, mine), order.wait(other_grad)], axis=0)
+    grad = lax.optimization_barrier((grad, kv))[0]
+    grads = [grad] + [to_earlier(grad, d) for d in group[1:]]
+    arrive(q_pieces, 1, *[d ^ 1 for d in mids + [near]])
     q = project(q_pieces)
-    qs = [q] + [over_ctx(q, distance=d) for d in group[1:]]
-
-    order = jnp.stack([c ^ d ^ p for d in group for p in (0, PAIR)])
-    blocks = order * run // BLOCK
-    here = order[:2]
+    qs = [q] + [to_earlier(q, d) for d in group[1:]]
+
+    runs = jnp.stack([c ^ d ^ p for d in group for p in (0, PAIR)])
+    blocks = runs * run // BLOCK
+    here = runs[:2]
 
     def limits(query_runs, key_runs, query_blocks, key_blocks):
         chosen = jnp.any(
@@ -194,8 +281,8 @@
         bound = jnp.where(ahead > 0, FAR, jnp.where(ahead == 0, 0, -FAR))
         return jnp.where(chosen, bound, -FAR).astype(jnp.int32)
 
-    query_limits = limits(here, order, blocks[:2], blocks)
-    key_limits = limits(order, here, blocks, blocks[:2]).T
+    query_limits = limits(here, runs, blocks[:2], blocks)
+    key_limits = limits(runs, here, blocks, blocks[:2]).T
 
     dq, stat = local_call(
         functools.partial(query_kernel, sets, run),
@@ -206,7 +293,7 @@
         2 + sets,
         2 * 2 * run * sets * 2 * run * HD * 5,
     )(query_limits, q, grad, *kvs)
-    stats = [stat] + [over_ctx(stat, distance=d) for d in group[1:]]
+    stats = [stat] + [to_earlier(stat, d) for d in group[1:]]
     dkv = local_call(
         functools.partial(key_kernel, sets, run),
         jax.ShapeDtypeStruct((2 * run, 2 * HD), BF16),
@@ -215,36 +302,44 @@
     )(key_limits, kv, *qs, *grads, *stats)
 
     all_grads = jnp.concatenate([dkv, dq], axis=1)
-    whole_w = jnp.zeros((width, 3 * HD), BF16)
-    for d in kv_pieces:
-        whole_w = lax.dynamic_update_slice(whole_w, kv_pieces[d], ((c ^ d) * depth, 0))
-        whole_w = lax.dynamic_update_slice(
-            whole_w, q_pieces[d], ((c ^ d) * depth, 2 * HD)
-        )
-
-    if n_f != 4:
+    if n_f != 4 or n_ctx != 2 * n_f:
+        whole_w = jnp.zeros((width, 3 * HD), BF16)
+        for d in kv_pieces:
+            piece = jnp.concatenate([kv_pieces[d], q_pieces[d]], axis=1)
+            whole_w = lax.dynamic_update_slice(whole_w, piece, ((c ^ d) * depth, 0))
         partial_out = dot_nt(all_grads, whole_w).astype(BF16)
         total = partial_out[:run].astype(F32) + over_ctx(partial_out[run:], distance=PAIR).astype(F32)
         return lax.psum_scatter(total.astype(BF16), "fsdp", scatter_dimension=1, tiled=True)
 
+    stacked = jnp.concatenate(
+        [
+            jnp.concatenate([kv_pieces[d] for d in range(n_ctx)], axis=0),
+            jnp.concatenate([q_pieces[d] for d in range(n_ctx)], axis=0),
+        ],
+        axis=1,
+    )
+
     def term(e):
-        rows = lax.dynamic_slice_in_dim(whole_w, (f ^ e) * per_f, per_f, axis=0)
-        return dot_nt(all_grads, rows)
+        at = ((f ^ e) ^ (c // 2)) * per_f
+        return dot_nt(all_grads, lax.dynamic_slice_in_dim(stacked, at, per_f, axis=0))
 
     half = per_f // 2
-    far = term(2) + over_f(term(3).astype(BF16), distance=1).astype(F32)
-    near = term(0) + over_f(term(1).astype(BF16), distance=1).astype(F32)
+    outer = term(2) + over_f(term(3).astype(BF16), distance=1).astype(F32)
+    inner = term(0) + over_f(term(1).astype(BF16), distance=1).astype(F32)
     by_x = functools.partial(over_f, distance=2)
     by_z = functools.partial(over_ctx, distance=PAIR)
-    corner_x = by_x(far[run:, :half].astype(BF16))
-    corner_z = by_z(far[run:, half:].astype(BF16))
-    from_x_a = by_x(far[:run, :half].astype(BF16))
-    from_z_b = by_z(near[run:, half:].astype(BF16))
-    from_z_a = by_z((near[run:, :half] + corner_x.astype(F32)).astype(BF16))
-    from_x_b = by_x((far[:run, half:] + corner_z.astype(F32)).astype(BF16))
-    left = near[:run, :half] + from_x_a.astype(F32) + from_z_a.astype(F32)
-    right = near[:run, half:] + from_x_b.astype(F32) + from_z_b.astype(F32)
-    return jnp.concatenate([left, right], axis=1).astype(BF16)
+    corner_x = by_x(outer[run:, :half].astype(BF16))
+    corner_z = by_z(outer[run:, half:].astype(BF16))
+    from_x_a = by_x(outer[:run, :half].astype(BF16))
+    from_z_b = by_z(inner[run:, half:].astype(BF16))
+    from_z_a = by_z((inner[run:, :half] + corner_x.astype(F32)).astype(BF16))
+    from_x_b = by_x((outer[:run, half:] + corner_z.astype(F32)).astype(BF16))
+    left = inner[:run, :half] + from_x_a.astype(F32) + from_z_a.astype(F32)
+    right = inner[:run, half:] + from_x_b.astype(F32) + from_z_b.astype(F32)
+    swapped = c % 2 == 1
+    return jnp.concatenate(
+        [jnp.where(swapped, right, left), jnp.where(swapped, left, right)], axis=1
+    ).astype(BF16)
 
 
 def solution(mesh):

time: 236 us -> 193 us (0.82)
  waiting for transfers between devices: 128 us -> 82.4 us
  local copies, waits for them, and re-layouts: 28.5 us -> 8.66 us
  matrix products: 16.9 us -> 27.2 us
  starting transfers between devices: 49.7 us -> 59 us
  other arithmetic: 3.81 us -> 6.42 us
    ppermute x39 -> x43, waiting for transfers between devices: 128 us -> 82.4 us  [swap(): return lax.ppermute(array, axis, pairs)]
    dynamic_update_slice x19 -> x0, local copies, waits for them, and re-layouts: 13.1 us -> none  [the longest x8 6.97 us: shards(): lax.dynamic_update_slice(whole_w, q_pieces[d], ((c ^ d) * depth, 2 * HD))]
    ppermute x39 -> x43, starting transfers between devices: 49.7 us -> 59 us  [swap(): return lax.ppermute(array, axis, pairs)]
    dot_general x16 -> x32, matrix products: 6.9 us -> 13.6 us  [dot_nn(): lax.dot_general(a, b, (((1,), (0,)), ((), ())), preferred_element_type=F32)]
    concatenate x1 -> x3, local copies, waits for them, and re-layouts: 5.76 us -> 0.11 us  [the longest x1 0.05 us: shards(): jnp.concatenate([held[e] for e in range(n_f)], axis=1)]
    dot_general x4, matrix products: 9.99 us -> 13.6 us  [dot_nt(): lax.dot_general(a, b, (((1,), (1,)), ((), ())), preferred_element_type=F32)]
    broadcast_in_dim x1 -> x0, local copies, waits for them, and re-layouts: 2.93 us -> none  [shards(): whole_w = jnp.zeros((width, 3 * HD), BF16)]
  transfers between devices with their start and end apart: 39 -> 43, of which waited for: 15 -> 20; matrix products, arithmetic and copies ran while one was open for 17% -> 17% of each run, Pallas kernels for 2% -> 2%
where the time goes in v2:
time: 193 us
  waiting for transfers between devices  82.4 us (43%)
  starting transfers between devices  59 us (31%)
  matrix products  27.2 us (14%)
  local copies, waits for them, and re-layouts  8.66 us (4%)
  Pallas kernels  8.17 us (4%)
  other arithmetic  6.42 us (3%)
    ppermute x43, waiting for transfers between devices, swap(): return lax.ppermute(array, axis, pairs)  82.4 us
    ppermute x43, starting transfers between devices, swap(): return lax.ppermute(array, axis, pairs)  59 us
    dot_general x4, matrix products, dot_nt(): lax.dot_general(a, b, (((1,), (1,)), ((), ())), preferred_element_type=F32)  13.6 us
    dot_general x32, matrix products, dot_nn(): lax.dot_general(a, b, (((1,), (0,)), ((), ())), preferred_element_type=F32)  13.6 us
    pallas_call x1, Pallas kernels, shards(): local_call(functools.partial(query_kernel, sets, run), (jax.ShapeDtypeStr...  4.42 us
  transfers between devices with their start and end apart: 43, of which 20 were waited for; matrix products, arithmetic and copies ran while one was open for 17% of the time, Pallas kernels for 2%

profile of v2, /device:TPU:0, one launch (start us, length us, event | category | flops | bytes accessed | tf_op | source)
XLA Modules:
  0.0 192.7 jit_solution(18047246804833606021)
XLA Ops:
  0.0 2.2 %dynamic-slice_bitcast_fusion = (bf16[896,128]{1,0:T(8,128)(2,1)}, bf16[896,128]{1,0:T(8,128)(2,1)S(1)}, bf16[896,128]{1,0:T(8,128)(2,1)S(1)}, bf16[896,128]{1,0...) fusion(bf16[896,3,256]{2,0,1:T(8,128)(2,1)} %param.5, s32[]{:T(128)S(6)} %select_n.226, ...), kind=kLoop, calls=%fused_computation.125 | loop fusion | bytes 2752528 | tf_op jit(solution)/shard_map/squeeze | solution.py:170
  3.1 4.0 %collective-permute-start.1 = (bf16[896,256]{1,0:T(8,128)(2,1)S(1)}, bf16[896,256]{1,0:T(8,128)(2,1)S(1)}, u32[]{:S(2)}, u32[]{:S(2)}) collective-permute-start(bf16[896,256]{1,0:T(8,128)(2,1)S(1)} %get-tuple-element.58), channel_id=1, source_target_pairs={{0,16},{4,20},{8,24},{12,28},{16,0},{20,4},{24,8},{28,12},{1,17},{... | collective-permute-start | bytes 1376264 | tf_op jit(solution)/shard_map/ppermute | solution.py:22
  7.1 1.5 collective-permute-start.4
  9.4 1.6 collective-permute-start
  13.3 1.3 fusion.94
  14.8 1.4 constant_dynamic-slice_fusion.1
  16.2 13.8 %collective-permute-done = bf16[896,256]{1,0:T(8,128)(2,1)S(1)} collective-permute-done((bf16[896,256]{1,0:T(8,128)(2,1)}, bf16[896,256]{1,0:T(8,128)(2,1)S(1)}, u32[]{:S(2)}, u32[]{:S(2)}) %collective-permute-start) | collective-permute-done | bytes 458784 | tf_op jit(solution)/shard_map/ppermute | solution.py:22
  30.0 2.4 %collective-permute-start.2 = (bf16[896,256]{1,0:T(8,128)(2,1)}, bf16[896,256]{1,0:T(8,128)(2,1)S(1)}, u32[]{:S(2)}, u32[]{:S(2)}) collective-permute-start(bf16[896,256]{1,0:T(8,128)(2,1)} %pad_maximum_fusion.3), channel_id=1, source_target_pairs={{0,24},{4,28},{8,16},{12,20},{16,8},{20,12},{24,0},{28,4},{1,25},{... | collective-permute-start | bytes 1376264 | tf_op jit(solution)/shard_map/ppermute | solution.py:22
  33.0 1.5 collective-permute-start.18
  34.5 1.3 fusion.92
  36.4 1.3 fusion.82
  37.8 1.5 convolution_add_fusion.2
  39.3 11.5 %collective-permute-done.18 = bf16[896,128]{1,0:T(8,128)(2,1)S(1)} collective-permute-done((bf16[896,128]{1,0:T(8,128)(2,1)S(1)}, bf16[896,128]{1,0:T(8,128)(2,1)S(1)}, u32[]{:S(2)}, u32[]{:S(2)}) %collective-permute-start.18) | collective-permute-done | bytes 229408 | tf_op jit(solution)/shard_map/ppermute | solution.py:22
  52.6 2.7 %collective-permute-start.17 = (bf16[896,128]{1,0:T(8,128)(2,1)S(1)}, bf16[896,128]{1,0:T(8,128)(2,1)S(1)}, u32[]{:S(2)}, u32[]{:S(2)}) collective-permute-start(bf16[896,128]{1,0:T(8,128)(2,1)S(1)} %copy-done.9), channel_id=1, source_target_pairs={{0,24},{4,28},{8,16},{12,20},{16,8},{20,12},{24,0},{28,4},{1,25},{... | collective-permute-start | bytes 688136 | tf_op jit(solution)/shard_map/ppermute | solution.py:22
  55.4 2.5 %collective-permute-done.5 = bf16[896,256]{1,0:T(8,128)(2,1)S(1)} collective-permute-done((bf16[896,256]{1,0:T(8,128)(2,1)S(1)}, bf16[896,256]{1,0:T(8,128)(2,1)S(1)}, u32[]{:S(2)}, u32[]{:S(2)}) %collective-permute-start.5) | collective-permute-done | bytes 458784 | tf_op jit(solution)/shard_map/ppermute | solution.py:22
  57.9 1.5 collective-permute-start.7
  61.6 3.0 %collective-permute-done.25 = bf16[256,128]{1,0:T(8,128)(2,1)S(1)} collective-permute-done((bf16[256,128]{1,0:T(8,128)(2,1)S(1)}, bf16[256,128]{1,0:T(8,128)(2,1)S(1)}, u32[]{:S(2)}, u32[]{:S(2)}) %collective-permute-start.25) | collective-permute-done | bytes 65568 | tf_op jit(solution)/shard_map/ppermute | solution.py:22
  65.2 1.6 collective-permute-start.9
  67.8 8.2 %collective-permute-done.16 = bf16[896,128]{1,0:T(8,128)(2,1)S(1)} collective-permute-done((bf16[896,128]{1,0:T(8,128)(2,1)S(1)}, bf16[896,128]{1,0:T(8,128)(2,1)S(1)}, u32[]{:S(2)}, u32[]{:S(2)}) %collective-permute-start.16) | collective-permute-done | bytes 229408 | tf_op jit(solution)/shard_map/ppermute | solution.py:22
  78.7 3.6 %collective-permute-done.11 = bf16[256,896]{1,0:T(8,128)(2,1)S(1)} collective-permute-done((bf16[256,896]{1,0:T(8,128)(2,1)S(1)}, bf16[256,896]{1,0:T(8,128)(2,1)S(1)}, u32[]{:S(2)}, u32[]{:S(2)}) %collective-permute-start.11) | collective-permute-done | bytes 458784 | tf_op jit(solution)/shard_map/ppermute | solution.py:22
  84.8 8.0 %collective-permute-done.20 = bf16[896,128]{1,0:T(8,128)(2,1)S(1)} collective-permute-done((bf16[896,128]{1,0:T(8,128)(2,1)S(1)}, bf16[896,128]{1,0:T(8,128)(2,1)S(1)}, u32[]{:S(2)}, u32[]{:S(2)}) %collective-permute-start.20) | collective-permute-done | bytes 229408 | tf_op jit(solution)/shard_map/ppermute | solution.py:22
  99.5 1.7 collective-permute-start.29
  101.1 1.6 collective-permute-start.30
  102.8 1.3 collective-permute-start.31
  105.2 1.5 collective-permute-start.26
  108.3 2.4 %collective-permute-done.26.refs_5_ = bf16[512,128]{1,0:T(8,128)(2,1)S(1)} collective-permute-done((bf16[512,128]{1,0:T(8,128)(2,1)S(1)}, bf16[512,128]{1,0:T(8,128)(2,1)S(1)}, u32[]{:S(2)}, u32[]{:S(2)}) %collective-permute-start.26) | collective-permute-done | bytes 131104 | tf_op jit(solution)/shard_map/ppermute | solution.py:22
  110.7 1.3 collective-permute-start.28
  112.0 1.7 collective-permute-start.22
  113.7 1.3 collective-permute-start.23
  115.0 1.5 collective-permute-start.24
  116.5 4.4 %shard_map.46 = (bf16[512,128]{1,0:T(8,128)(2,1)S(1)}, f32[8,512]{1,0:T(8,128)S(1)}) custom-call(s32[2,8]{1,0:T(2,128)S(1)} %get-tuple-element.63.limit_ref, bf16[512,128]{1,0:T(8,128)(2,1)S(1)} %pad_maximum_fusion.6.q_ref.refs_0_, bf16[512,128]{1,0:T(8,128)(2,1)S(1)} %pad_maximum_fusion.7.grad_ref.refs_4_, ...), custom_call_target="tpu_custom_call" | custom-call | flops 1342177280 | bytes 4194304 | tf_op jit(solution)/shard_map/pallas_call | solution.py:287
  121.4 2.3 %collective-permute-done.28.refs_7_ = bf16[512,128]{1,0:T(8,128)(2,1)S(1)} collective-permute-done((bf16[512,128]{1,0:T(8,128)(2,1)S(1)}, bf16[512,128]{1,0:T(8,128)(2,1)S(1)}, u32[]{:S(2)}, u32[]{:S(2)}) %collective-permute-start.28) | collective-permute-done | bytes 131104 | tf_op jit(solution)/shard_map/ppermute | solution.py:22
  123.7 1.3 collective-permute-start.33
  125.0 1.3 collective-permute-start.34
  126.3 3.0 %collective-permute-done.23.refs_2_ = bf16[512,128]{1,0:T(8,128)(2,1)S(1)} collective-permute-done((bf16[512,128]{1,0:T(8,128)(2,1)S(1)}, bf16[512,128]{1,0:T(8,128)(2,1)S(1)}, u32[]{:S(2)}, u32[]{:S(2)}) %collective-permute-start.23) | collective-permute-done | bytes 131104 | tf_op jit(solution)/shard_map/ppermute | solution.py:22
  129.3 2.4 %collective-permute-done.24.refs_3_ = bf16[512,128]{1,0:T(8,128)(2,1)S(1)} collective-permute-done((bf16[512,128]{1,0:T(8,128)(2,1)S(1)}, bf16[512,128]{1,0:T(8,128)(2,1)S(1)}, u32[]{:S(2)}, u32[]{:S(2)}) %collective-permute-start.24) | collective-permute-done | bytes 131104 | tf_op jit(solution)/shard_map/ppermute | solution.py:22
  131.7 3.0 %collective-permute-done.33.refs_10_ = f32[8,512]{1,0:T(8,128)S(1)} collective-permute-done((f32[8,512]{1,0:T(8,128)S(1)}, f32[8,512]{1,0:T(8,128)S(1)}, u32[]{:S(2)}, u32[]{:S(2)}) %collective-permute-start.33) | collective-permute-done | bytes 16416 | tf_op jit(solution)/shard_map/ppermute | solution.py:22
  134.6 3.7 %shard_map.47 = bf16[512,256]{1,0:T(8,128)(2,1)S(1)} custom-call(s32[2,8]{1,0:T(2,128)S(1)} %get-tuple-element.62.limit_ref, bf16[512,256]{1,0:T(8,128)(2,1)S(1)} %pad_maximum_fusion.5.refs_0_.kv_ref, bf16[512,128]{1,0:T(8,128)(2,1)S(1)} %pad_maximum_fusion.6.q_ref.refs_0_, bf16[512,128]{1,0:T(8,128)(2,1)S(1)} %collective-permute-done.22.refs_1_, ...), custom_call_target="tpu_custom_call" | custom-call | flops 1342177280 | bytes 4194304 | tf_op jit(solution)/shard_map/pallas_call | solution.py:297
  138.4 2.4 %convolution_convert_fusion = bf16[512,1792]{1,0:T(8,128)(2,1)} fusion(s32[]{:T(128)S(6)} %select_n.258, bf16[7168,256]{1,0:T(8,128)(2,1)S(1)} %constant_dynamic-update-slice_fusion.4, bf16[7168,128]{1,0:T(8,128)(2,1)S(1)} %constant_dynamic-update-slice_fusion.12, bf16[512,128]{1,0:T(8,128)(2,1)S(1)} %get-tuple-element.44, bf16[512,256]{1,0:T(8,128)(2,1)S(1)} %shard_map.47), kind=kOutput, calls=%fused_computation.12 | convolution fusion | flops 709099520 | bytes 7733252 | tf_op jit(solution)/shard_map/dot_general | solution.py:52
  140.8 3.6 %convolution_convert_fusion.1 = bf16[512,1792]{1,0:T(8,128)(2,1)} fusion(s32[]{:T(128)S(6)} %select_n.256, bf16[7168,256]{1,0:T(8,128)(2,1)} %copy-done.2, bf16[7168,128]{1,0:T(8,128)(2,1)S(1)} %constant_dynamic-update-slice_fusion.12, bf16[512,128]{1,0:T(8,128)(2,1)S(1)} %get-tuple-element.44, bf16[512,256]{1,0:T(8,128)(2,1)S(1)} %shard_map.47), kind=kOutput, calls=%fused_computation.13 | convolution fusion | flops 709099520 | bytes 7733252 | tf_op jit(solution)/shard_map/dot_general | solution.py:52
  144.9 4.8 %fusion.140 = (bf16[512,1792]{1,0:T(8,128)(2,1)S(1)}, f32[512,1792]{1,0:T(8,128)}) fusion(bf16[512,1792]{1,0:T(8,128)(2,1)} %collective-permute-done.36, s32[]{:T(128)S(6)} %select_n.257, bf16[7168,256]{1,0:T(8,128)(2,1)} %copy-done.2, bf16[7168,128]{1,0:T(8,128)(2,1)S(1)} %constant_dynamic-update-slice_fusion.12, ...), kind=kOutput, calls=%fused_computation.221 | convolution fusion | flops 710934528 | bytes 13238276 | tf_op jit(solution)/shard_map/dot_general | solution.py:52
  150.9 8.5 %collective-permute-start.37 = (bf16[256,896]{1,0:T(8,128)(2,1)}, bf16[256,896]{1,0:T(8,128)(2,1)S(1)}, u32[]{:S(2)}, u32[]{:S(2)}) collective-permute-start(bf16[256,896]{1,0:T(8,128)(2,1)} %get-tuple-element.51), channel_id=1, source_target_pairs={{0,8},{4,12},{8,0},{12,4},{16,24},{20,28},{24,16},{28,20},{1,9},{5... | collective-permute-start | bytes 1376264 | tf_op jit(solution)/shard_map/ppermute | solution.py:22
  160.2 2.9 %convert_add_fusion.1 = f32[512,1792]{1,0:T(8,128)S(1)} fusion(bf16[512,1792]{1,0:T(8,128)(2,1)} %collective-permute-done.35, s32[]{:T(128)S(6)} %select_n.255, bf16[7168,256]{1,0:T(8,128)(2,1)} %copy-done.2, bf16[7168,128]{1,0:T(8,128)(2,1)S(1)} %constant_dynamic-update-slice_fusion.12, bf16[512,128]{1,0:T(8,128)(2,1)S(1)} %get-tuple-element.44, ...), kind=kOutput, calls=%fused_computation.11 | convolution fusion | flops 710017024 | bytes 11403268 | tf_op jit(solution)/shard_map/dot_general | solution.py:52
  164.6 7.3 %collective-permute-start.42 = (bf16[256,896]{1,0:T(8,128)(2,1)S(1)}, bf16[256,896]{1,0:T(8,128)(2,1)S(1)}, u32[]{:S(2)}, u32[]{:S(2)}) collective-permute-start(bf16[256,896]{1,0:T(8,128)(2,1)S(1)} %fusion.34), channel_id=1, source_target_pairs={{0,8},{4,12},{8,0},{12,4},{16,24},{20,28},{24,16},{28,20},{1,9},{5... | collective-permute-start | bytes 1376264 | tf_op jit(solution)/shard_map/ppermute | solution.py:22
  173.2 1.4 collective-permute-start.38
  174.5 6.3 %collective-permute-done.39 = bf16[256,896]{1,0:T(8,128)(2,1)S(1)} collective-permute-done((bf16[256,896]{1,0:T(8,128)(2,1)}, bf16[256,896]{1,0:T(8,128)(2,1)S(1)}, u32[]{:S(2)}, u32[]{:S(2)}) %collective-permute-start.39) | collective-permute-done | bytes 458784 | tf_op jit(solution)/shard_map/ppermute | solution.py:22
  180.8 9.0 %collective-permute-done.42 = bf16[256,896]{1,0:T(8,128)(2,1)S(1)} collective-permute-done((bf16[256,896]{1,0:T(8,128)(2,1)S(1)}, bf16[256,896]{1,0:T(8,128)(2,1)S(1)}, u32[]{:S(2)}, u32[]{:S(2)}) %collective-permute-start.42) | collective-permute-done | bytes 458784 | tf_op jit(solution)/shard_map/ppermute | solution.py:22
  189.8 1.8 select_convert_fusion.1
  (147 shorter events, 31.9 us)
Async XLA Ops:
  2.2 12.4 %copy-start.7 = (bf16[896,128]{1,0:T(8,128)(2,1)}, bf16[896,128]{1,0:T(8,128)(2,1)S(1)}, u32[]{:S(2)}) copy-start(bf16[896,128]{1,0:T(8,128)(2,1)S(1)} %get-tuple-element.56) | copy-start | bytes 688132
  3.1 27.0 %collective-permute-start.1 = (bf16[896,256]{1,0:T(8,128)(2,1)S(1)}, bf16[896,256]{1,0:T(8,128)(2,1)S(1)}, u32[]{:S(2)}, u32[]{:S(2)}) collective-permute-start(bf16[896,256]{1,0:T(8,128)(2,1)S(1)} %get-tuple-element.58), channel_id=1, source_target_pairs={{0,16},{4,20},{8,24},{12,28},{16,0},{20,4},{24,8},{28,12},{1,17},{... | collective-permute-start | bytes 1376264 | tf_op jit(solution)/shard_map/ppermute | solution.py:22
  7.1 28.7 %collective-permute-start.4 = (bf16[896,256]{1,0:T(8,128)(2,1)S(1)}, bf16[896,256]{1,0:T(8,128)(2,1)S(1)}, u32[]{:S(2)}, u32[]{:S(2)}) collective-permute-start(bf16[896,256]{1,0:T(8,128)(2,1)S(1)} %get-tuple-element.58), channel_id=1, source_target_pairs={{0,4},{4,0},{8,12},{12,8},{16,20},{20,16},{24,28},{28,24},{1,5},{5... | collective-permute-start | bytes 1376264 | tf_op jit(solution)/shard_map/ppermute | solution.py:22
  9.4 20.6 %collective-permute-start = (bf16[896,256]{1,0:T(8,128)(2,1)}, bf16[896,256]{1,0:T(8,128)(2,1)S(1)}, u32[]{:S(2)}, u32[]{:S(2)}) collective-permute-start(bf16[896,256]{1,0:T(8,128)(2,1)} %pad_maximum_fusion.3), channel_id=1, source_target_pairs={{0,8},{4,12},{8,0},{12,4},{16,24},{20,28},{24,16},{28,20},{1,9},{5... | collective-permute-start | bytes 1376264 | tf_op jit(solution)/shard_map/ppermute | solution.py:22
  14.8 22.9 %copy-start.1 = (bf16[7168,256]{1,0:T(8,128)(2,1)S(1)}, bf16[7168,256]{1,0:T(8,128)(2,1)}, u32[]{:S(2)}) copy-start(bf16[7168,256]{1,0:T(8,128)(2,1)} %get-tuple-element.59) | copy-start | bytes 11010052
  30.0 21.1 %collective-permute-start.3 = (bf16[256,896]{1,0:T(8,128)(2,1)S(1)}, bf16[256,896]{1,0:T(8,128)(2,1)S(1)}, u32[]{:S(2)}, u32[]{:S(2)}) collective-permute-start(bf16[256,896]{1,0:T(8,128)(2,1)S(1)} %get-tuple-element.30), channel_id=1, source_target_pairs={{0,8},{4,12},{8,0},{12,4},{16,24},{20,28},{24,16},{28,20},{1,9},{5... | collective-permute-start | bytes 1376264 | tf_op jit(solution)/shard_map/ppermute | solution.py:22
  30.0 21.8 %collective-permute-start.2 = (bf16[896,256]{1,0:T(8,128)(2,1)}, bf16[896,256]{1,0:T(8,128)(2,1)S(1)}, u32[]{:S(2)}, u32[]{:S(2)}) collective-permute-start(bf16[896,256]{1,0:T(8,128)(2,1)} %pad_maximum_fusion.3), channel_id=1, source_target_pairs={{0,24},{4,28},{8,16},{12,20},{16,8},{20,12},{24,0},{28,4},{1,25},{... | collective-permute-start | bytes 1376264 | tf_op jit(solution)/shard_map/ppermute | solution.py:22
  32.4 27.7 %collective-permute-start.6 = (bf16[896,256]{1,0:T(8,128)(2,1)S(1)}, bf16[896,256]{1,0:T(8,128)(2,1)S(1)}, u32[]{:S(2)}, u32[]{:S(2)}) collective-permute-start(bf16[896,256]{1,0:T(8,128)(2,1)S(1)} %collective-permute-done.1), channel_id=1, source_target_pairs={{0,4},{4,0},{8,12},{12,8},{16,20},{20,16},{24,28},{28,24},{1,5},{5... | collective-permute-start | bytes 1376264 | tf_op jit(solution)/shard_map/ppermute | solution.py:22
  33.0 17.8 %collective-permute-start.18 = (bf16[896,128]{1,0:T(8,128)(2,1)S(1)}, bf16[896,128]{1,0:T(8,128)(2,1)S(1)}, u32[]{:S(2)}, u32[]{:S(2)}) collective-permute-start(bf16[896,128]{1,0:T(8,128)(2,1)S(1)} %get-tuple-element.40), channel_id=1, source_target_pairs={{0,4},{4,0},{8,12},{12,8},{16,20},{20,16},{24,28},{28,24},{1,5},{5... | collective-permute-start | bytes 688136 | tf_op jit(solution)/shard_map/ppermute | solution.py:22
  35.8 22.2 %collective-permute-start.5 = (bf16[896,256]{1,0:T(8,128)(2,1)S(1)}, bf16[896,256]{1,0:T(8,128)(2,1)S(1)}, u32[]{:S(2)}, u32[]{:S(2)}) collective-permute-start(bf16[896,256]{1,0:T(8,128)(2,1)S(1)} %collective-permute-done), channel_id=1, source_target_pairs={{0,4},{4,0},{8,12},{12,8},{16,20},{20,16},{24,28},{28,24},{1,5},{5... | collective-permute-start | bytes 1376264 | tf_op jit(solution)/shard_map/ppermute | solution.py:22
  37.7 13.1 %copy-start.3 = (bf16[256,7168]{1,0:T(8,128)(2,1)S(1)}, bf16[256,7168]{1,0:T(8,128)(2,1)}, u32[]{:S(2)}) copy-start(bf16[256,7168]{1,0:T(8,128)(2,1)} %param.4) | copy-start | bytes 11010052
  37.8 14.1 %copy-start.9 = (bf16[896,128]{1,0:T(8,128)(2,1)S(1)}, bf16[896,128]{1,0:T(8,128)(2,1)}, u32[]{:S(2)}) copy-start(bf16[896,128]{1,0:T(8,128)(2,1)} %get-tuple-element.39) | copy-start | bytes 688132
  51.8 13.3 %collective-permute-start.15 = (bf16[896,128]{1,0:T(8,128)(2,1)S(1)}, bf16[896,128]{1,0:T(8,128)(2,1)S(1)}, u32[]{:S(2)}, u32[]{:S(2)}) collective-permute-start(bf16[896,128]{1,0:T(8,128)(2,1)S(1)} %copy-done.9), channel_id=1, source_target_pairs={{0,8},{4,12},{8,0},{12,4},{16,24},{20,28},{24,16},{28,20},{1,9},{5... | collective-permute-start | bytes 688136 | tf_op jit(solution)/shard_map/ppermute | solution.py:22
  52.6 14.1 %collective-permute-start.17 = (bf16[896,128]{1,0:T(8,128)(2,1)S(1)}, bf16[896,128]{1,0:T(8,128)(2,1)S(1)}, u32[]{:S(2)}, u32[]{:S(2)}) collective-permute-start(bf16[896,128]{1,0:T(8,128)(2,1)S(1)} %copy-done.9), channel_id=1, source_target_pairs={{0,24},{4,28},{8,16},{12,20},{16,8},{20,12},{24,0},{28,4},{1,25},{... | collective-permute-start | bytes 688136 | tf_op jit(solution)/shard_map/ppermute | solution.py:22
  55.4 27.3 %collective-permute-start.8 = (bf16[256,896]{1,0:T(8,128)(2,1)S(1)}, bf16[256,896]{1,0:T(8,128)(2,1)S(1)}, u32[]{:S(2)}, u32[]{:S(2)}) collective-permute-start(bf16[256,896]{1,0:T(8,128)(2,1)S(1)} %collective-permute-done.3), channel_id=1, source_target_pairs={{0,1},{1,0},{2,3},{3,2},{4,5},{5,4},{6,7},{7,6},{8,9},{9,8},{10,11... | collective-permute-start | bytes 1376264 | tf_op jit(solution)/shard_map/ppermute | solution.py:22
  57.9 24.8 %collective-permute-start.7 = (bf16[896,256]{1,0:T(8,128)(2,1)S(1)}, bf16[896,256]{1,0:T(8,128)(2,1)S(1)}, u32[]{:S(2)}, u32[]{:S(2)}) collective-permute-start(bf16[896,256]{1,0:T(8,128)(2,1)S(1)} %collective-permute-done.2), channel_id=1, source_target_pairs={{0,4},{4,0},{8,12},{12,8},{16,20},{20,16},{24,28},{28,24},{1,5},{5... | collective-permute-start | bytes 1376264 | tf_op jit(solution)/shard_map/ppermute | solution.py:22
  60.3 4.3 %collective-permute-start.25 = (bf16[256,128]{1,0:T(8,128)(2,1)S(1)}, bf16[256,128]{1,0:T(8,128)(2,1)S(1)}, u32[]{:S(2)}, u32[]{:S(2)}) collective-permute-start(bf16[256,128]{1,0:T(8,128)(2,1)S(1)} %copy-done.11), channel_id=1, source_target_pairs={{0,8},{4,12},{8,0},{12,4},{16,24},{20,28},{24,16},{28,20},{1,9},{5... | collective-permute-start | bytes 196616 | tf_op jit(solution)/shard_map/ppermute | solution.py:22
  64.6 11.4 %collective-permute-start.16 = (bf16[896,128]{1,0:T(8,128)(2,1)S(1)}, bf16[896,128]{1,0:T(8,128)(2,1)S(1)}, u32[]{:S(2)}, u32[]{:S(2)}) collective-permute-start(bf16[896,128]{1,0:T(8,128)(2,1)S(1)} %get-tuple-element.40), channel_id=1, source_target_pairs={{0,16},{4,20},{8,24},{12,28},{16,0},{20,4},{24,8},{28,12},{1,17},{... | collective-permute-start | bytes 688136 | tf_op jit(solution)/shard_map/ppermute | solution.py:22
  65.2 12.2 %collective-permute-start.9 = (bf16[256,896]{1,0:T(8,128)(2,1)S(1)}, bf16[256,896]{1,0:T(8,128)(2,1)S(1)}, u32[]{:S(2)}, u32[]{:S(2)}) collective-permute-start(bf16[256,896]{1,0:T(8,128)(2,1)S(1)} %collective-permute-done.3), channel_id=1, source_target_pairs={{0,2},{1,3},{2,0},{3,1},{4,6},{5,7},{6,4},{7,5},{8,10},{9,11},{10,... | collective-permute-start | bytes 1376264 | tf_op jit(solution)/shard_map/ppermute | solution.py:22
  66.8 15.5 %collective-permute-start.11 = (bf16[256,896]{1,0:T(8,128)(2,1)S(1)}, bf16[256,896]{1,0:T(8,128)(2,1)S(1)}, u32[]{:S(2)}, u32[]{:S(2)}) collective-permute-start(bf16[256,896]{1,0:T(8,128)(2,1)S(1)} %get-tuple-element.37), channel_id=1, source_target_pairs={{0,8},{4,12},{8,0},{12,4},{16,24},{20,28},{24,16},{28,20},{1,9},{5... | collective-permute-start | bytes 1376264 | tf_op jit(solution)/shard_map/ppermute | solution.py:22
  76.0 8.5 %collective-permute-start.21 = (bf16[896,128]{1,0:T(8,128)(2,1)S(1)}, bf16[896,128]{1,0:T(8,128)(2,1)S(1)}, u32[]{:S(2)}, u32[]{:S(2)}) collective-permute-start(bf16[896,128]{1,0:T(8,128)(2,1)S(1)} %collective-permute-done.17), channel_id=1, source_target_pairs={{0,4},{4,0},{8,12},{12,8},{16,20},{20,16},{24,28},{28,24},{1,5},{5... | collective-permute-start | bytes 688136 | tf_op jit(solution)/shard_map/ppermute | solution.py:22
  77.4 15.7 %collective-permute-start.19 = (bf16[896,128]{1,0:T(8,128)(2,1)S(1)}, bf16[896,128]{1,0:T(8,128)(2,1)S(1)}, u32[]{:S(2)}, u32[]{:S(2)}) collective-permute-start(bf16[896,128]{1,0:T(8,128)(2,1)S(1)} %collective-permute-done.15), channel_id=1, source_target_pairs={{0,4},{4,0},{8,12},{12,8},{16,20},{20,16},{24,28},{28,24},{1,5},{5... | collective-permute-start | bytes 688136 | tf_op jit(solution)/shard_map/ppermute | solution.py:22
  82.2 10.6 %collective-permute-start.20 = (bf16[896,128]{1,0:T(8,128)(2,1)S(1)}, bf16[896,128]{1,0:T(8,128)(2,1)S(1)}, u32[]{:S(2)}, u32[]{:S(2)}) collective-permute-start(bf16[896,128]{1,0:T(8,128)(2,1)S(1)} %collective-permute-done.16), channel_id=1, source_target_pairs={{0,4},{4,0},{8,12},{12,8},{16,20},{20,16},{24,28},{28,24},{1,5},{5... | collective-permute-start | bytes 688136 | tf_op jit(solution)/shard_map/ppermute | solution.py:22
  82.6 11.6 %collective-permute-start.10 = (bf16[256,896]{1,0:T(8,128)(2,1)S(1)}, bf16[256,896]{1,0:T(8,128)(2,1)S(1)}, u32[]{:S(2)}, u32[]{:S(2)}) collective-permute-start(bf16[256,896]{1,0:T(8,128)(2,1)S(1)} %collective-permute-done.9), channel_id=1, source_target_pairs={{0,1},{1,0},{2,3},{3,2},{4,5},{5,4},{6,7},{7,6},{8,9},{9,8},{10,11... | collective-permute-start | bytes 1376264 | tf_op jit(solution)/shard_map/ppermute | solution.py:22
  82.8 13.0 %collective-permute-start.13 = (bf16[256,896]{1,0:T(8,128)(2,1)S(1)}, bf16[256,896]{1,0:T(8,128)(2,1)S(1)}, u32[]{:S(2)}, u32[]{:S(2)}) collective-permute-start(bf16[256,896]{1,0:T(8,128)(2,1)S(1)} %collective-permute-done.11), channel_id=1, source_target_pairs={{0,2},{1,3},{2,0},{3,1},{4,6},{5,7},{6,4},{7,5},{8,10},{9,11},{10,... | collective-permute-start | bytes 1376264 | tf_op jit(solution)/shard_map/ppermute | solution.py:22
  84.5 11.8 %collective-permute-start.12 = (bf16[256,896]{1,0:T(8,128)(2,1)S(1)}, bf16[256,896]{1,0:T(8,128)(2,1)S(1)}, u32[]{:S(2)}, u32[]{:S(2)}) collective-permute-start(bf16[256,896]{1,0:T(8,128)(2,1)S(1)} %collective-permute-done.11), channel_id=1, source_target_pairs={{0,1},{1,0},{2,3},{3,2},{4,5},{5,4},{6,7},{7,6},{8,9},{9,8},{10,11... | collective-permute-start | bytes 1376264 | tf_op jit(solution)/shard_map/ppermute | solution.py:22
  93.9 44.5 %copy-start.2 = (bf16[7168,256]{1,0:T(8,128)(2,1)}, bf16[7168,256]{1,0:T(8,128)(2,1)S(1)}, u32[]{:S(2)}) copy-start(bf16[7168,256]{1,0:T(8,128)(2,1)S(1)} %constant_dynamic-update-slice_fusion.4) | copy-start | bytes 11010052
  95.8 1.8 collective-permute-start.14
  99.5 12.5 %collective-permute-start.29 = (bf16[512,256]{1,0:T(8,128)(2,1)S(1)}, bf16[512,256]{1,0:T(8,128)(2,1)S(1)}, u32[]{:S(2)}, u32[]{:S(2)}) collective-permute-start(bf16[512,256]{1,0:T(8,128)(2,1)S(1)} %pad_maximum_fusion.5.refs_0_.kv_ref), channel_id=1, source_target_pairs={{0,4},{4,0},{8,12},{12,8},{16,20},{20,16},{24,28},{28,24},{1,5},{5... | collective-permute-start | bytes 786440 | tf_op jit(solution)/shard_map/ppermute | solution.py:22
  101.1 12.6 %collective-permute-start.30 = (bf16[512,256]{1,0:T(8,128)(2,1)S(1)}, bf16[512,256]{1,0:T(8,128)(2,1)S(1)}, u32[]{:S(2)}, u32[]{:S(2)}) collective-permute-start(bf16[512,256]{1,0:T(8,128)(2,1)S(1)} %pad_maximum_fusion.5.refs_0_.kv_ref), channel_id=1, source_target_pairs={{0,16},{4,20},{8,24},{12,28},{1,17},{5,21},{9,25},{13,29},{2,18},{... | collective-permute-start | bytes 786440 | tf_op jit(solution)/shard_map/ppermute | solution.py:22
  102.8 12.2 %collective-permute-start.31 = (bf16[512,256]{1,0:T(8,128)(2,1)S(1)}, bf16[512,256]{1,0:T(8,128)(2,1)S(1)}, u32[]{:S(2)}, u32[]{:S(2)}) collective-permute-start(bf16[512,256]{1,0:T(8,128)(2,1)S(1)} %pad_maximum_fusion.5.refs_0_.kv_ref), channel_id=1, source_target_pairs={{0,20},{4,16},{8,28},{12,24},{1,21},{5,17},{9,29},{13,25},{2,22},{... | collective-permute-start | bytes 786440 | tf_op jit(solution)/shard_map/ppermute | solution.py:22
  105.2 5.5 %collective-permute-start.26 = (bf16[512,128]{1,0:T(8,128)(2,1)S(1)}, bf16[512,128]{1,0:T(8,128)(2,1)S(1)}, u32[]{:S(2)}, u32[]{:S(2)}) collective-permute-start(bf16[512,128]{1,0:T(8,128)(2,1)S(1)} %pad_maximum_fusion.7.grad_ref.refs_4_), channel_id=1, source_target_pairs={{0,4},{4,0},{8,12},{12,8},{16,20},{20,16},{24,28},{28,24},{1,5},{5... | collective-permute-start | bytes 393224 | tf_op jit(solution)/shard_map/ppermute | solution.py:22
  106.7 14.2 %collective-permute-start.27 = (bf16[512,128]{1,0:T(8,128)(2,1)S(1)}, bf16[512,128]{1,0:T(8,128)(2,1)S(1)}, u32[]{:S(2)}, u32[]{:S(2)}) collective-permute-start(bf16[512,128]{1,0:T(8,128)(2,1)S(1)} %pad_maximum_fusion.7.grad_ref.refs_4_), channel_id=1, source_target_pairs={{16,0},{20,4},{24,8},{28,12},{17,1},{21,5},{25,9},{29,13},{18,2},{... | collective-permute-start | bytes 393224 | tf_op jit(solution)/shard_map/ppermute | solution.py:22
  110.7 13.0 %collective-permute-start.28 = (bf16[512,128]{1,0:T(8,128)(2,1)S(1)}, bf16[512,128]{1,0:T(8,128)(2,1)S(1)}, u32[]{:S(2)}, u32[]{:S(2)}) collective-permute-start(bf16[512,128]{1,0:T(8,128)(2,1)S(1)} %pad_maximum_fusion.7.grad_ref.refs_4_), channel_id=1, source_target_pairs={{16,4},{20,0},{24,12},{28,8},{17,5},{21,1},{25,13},{29,9},{18,6},{... | collective-permute-start | bytes 393224 | tf_op jit(solution)/shard_map/ppermute | solution.py:22
  112.0 13.0 %collective-permute-start.22 = (bf16[512,128]{1,0:T(8,128)(2,1)S(1)}, bf16[512,128]{1,0:T(8,128)(2,1)S(1)}, u32[]{:S(2)}, u32[]{:S(2)}) collective-permute-start(bf16[512,128]{1,0:T(8,128)(2,1)S(1)} %pad_maximum_fusion.6.q_ref.refs_0_), channel_id=1, source_target_pairs={{0,4},{4,0},{8,12},{12,8},{16,20},{20,16},{24,28},{28,24},{1,5},{5... | collective-permute-start | bytes 393224 | tf_op jit(solution)/shard_map/ppermute | solution.py:22
  113.7 15.6 %collective-permute-start.23 = (bf16[512,128]{1,0:T(8,128)(2,1)S(1)}, bf16[512,128]{1,0:T(8,128)(2,1)S(1)}, u32[]{:S(2)}, u32[]{:S(2)}) collective-permute-start(bf16[512,128]{1,0:T(8,128)(2,1)S(1)} %pad_maximum_fusion.6.q_ref.refs_0_), channel_id=1, source_target_pairs={{16,0},{20,4},{24,8},{28,12},{17,1},{21,5},{25,9},{29,13},{18,2},{... | collective-permute-start | bytes 393224 | tf_op jit(solution)/shard_map/ppermute | solution.py:22
  115.0 16.7 %collective-permute-start.24 = (bf16[512,128]{1,0:T(8,128)(2,1)S(1)}, bf16[512,128]{1,0:T(8,128)(2,1)S(1)}, u32[]{:S(2)}, u32[]{:S(2)}) collective-permute-start(bf16[512,128]{1,0:T(8,128)(2,1)S(1)} %pad_maximum_fusion.6.q_ref.refs_0_), channel_id=1, source_target_pairs={{16,4},{20,0},{24,12},{28,8},{17,5},{21,1},{25,13},{29,9},{18,6},{... | collective-permute-start | bytes 393224 | tf_op jit(solution)/shard_map/ppermute | solution.py:22
  120.9 10.7 %collective-permute-start.32 = (f32[8,512]{1,0:T(8,128)S(1)}, f32[8,512]{1,0:T(8,128)S(1)}, u32[]{:S(2)}, u32[]{:S(2)}) collective-permute-start(f32[8,512]{1,0:T(8,128)S(1)} %get-tuple-element.43.refs_8_), channel_id=1, source_target_pairs={{0,4},{4,0},{8,12},{12,8},{16,20},{20,16},{24,28},{28,24},{1,5},{5... | collective-permute-start | bytes 49160 | tf_op jit(solution)/shard_map/ppermute | solution.py:22
  123.7 10.9 %collective-permute-start.33 = (f32[8,512]{1,0:T(8,128)S(1)}, f32[8,512]{1,0:T(8,128)S(1)}, u32[]{:S(2)}, u32[]{:S(2)}) collective-permute-start(f32[8,512]{1,0:T(8,128)S(1)} %get-tuple-element.43.refs_8_), channel_id=1, source_target_pairs={{16,0},{20,4},{24,8},{28,12},{17,1},{21,5},{25,9},{29,13},{18,2},{... | collective-permute-start | bytes 49160 | tf_op jit(solution)/shard_map/ppermute | solution.py:22
  125.0 9.6 %collective-permute-start.34 = (f32[8,512]{1,0:T(8,128)S(1)}, f32[8,512]{1,0:T(8,128)S(1)}, u32[]{:S(2)}, u32[]{:S(2)}) collective-permute-start(f32[8,512]{1,0:T(8,128)S(1)} %get-tuple-element.43.refs_8_), channel_id=1, source_target_pairs={{16,4},{20,0},{24,12},{28,8},{17,5},{21,1},{25,13},{29,9},{18,6},{... | collective-permute-start | bytes 49160 | tf_op jit(solution)/shard_map/ppermute | solution.py:22
  140.8 4.1 %collective-permute-start.36 = (bf16[512,1792]{1,0:T(8,128)(2,1)}, bf16[512,1792]{1,0:T(8,128)(2,1)}, u32[]{:S(2)}, u32[]{:S(2)}) collective-permute-start(bf16[512,1792]{1,0:T(8,128)(2,1)} %convolution_convert_fusion), channel_id=1, source_target_pairs={{0,1},{1,0},{2,3},{3,2},{4,5},{5,4},{6,7},{7,6},{8,9},{9,8},{10,11... | collective-permute-start | bytes 5505032 | tf_op jit(solution)/shard_map/ppermute | solution.py:22
  144.4 15.8 %collective-permute-start.35 = (bf16[512,1792]{1,0:T(8,128)(2,1)}, bf16[512,1792]{1,0:T(8,128)(2,1)}, u32[]{:S(2)}, u32[]{:S(2)}) collective-permute-start(bf16[512,1792]{1,0:T(8,128)(2,1)} %convolution_convert_fusion.1), channel_id=1, source_target_pairs={{0,1},{1,0},{2,3},{3,2},{4,5},{5,4},{6,7},{7,6},{8,9},{9,8},{10,11... | collective-permute-start | bytes 5505032 | tf_op jit(solution)/shard_map/ppermute | solution.py:22
  150.9 13.6 %collective-permute-start.41 = (bf16[256,896]{1,0:T(8,128)(2,1)}, bf16[256,896]{1,0:T(8,128)(2,1)S(1)}, u32[]{:S(2)}, u32[]{:S(2)}) collective-permute-start(bf16[256,896]{1,0:T(8,128)(2,1)} %get-tuple-element.50), channel_id=1, source_target_pairs={{0,2},{1,3},{2,0},{3,1},{4,6},{5,7},{6,4},{7,5},{8,10},{9,11},{10,... | collective-permute-start | bytes 1376264 | tf_op jit(solution)/shard_map/ppermute | solution.py:22
  150.9 21.0 %collective-permute-start.37 = (bf16[256,896]{1,0:T(8,128)(2,1)}, bf16[256,896]{1,0:T(8,128)(2,1)S(1)}, u32[]{:S(2)}, u32[]{:S(2)}) collective-permute-start(bf16[256,896]{1,0:T(8,128)(2,1)} %get-tuple-element.51), channel_id=1, source_target_pairs={{0,8},{4,12},{8,0},{12,4},{16,24},{20,28},{24,16},{28,20},{1,9},{5... | collective-permute-start | bytes 1376264 | tf_op jit(solution)/shard_map/ppermute | solution.py:22
  159.4 15.1 %collective-permute-start.40 = (bf16[256,896]{1,0:T(8,128)(2,1)}, bf16[256,896]{1,0:T(8,128)(2,1)S(1)}, u32[]{:S(2)}, u32[]{:S(2)}) collective-permute-start(bf16[256,896]{1,0:T(8,128)(2,1)} %get-tuple-element.49), channel_id=1, source_target_pairs={{0,2},{1,3},{2,0},{3,1},{4,6},{5,7},{6,4},{7,5},{8,10},{9,11},{10,... | collective-permute-start | bytes 1376264 | tf_op jit(solution)/shard_map/ppermute | solution.py:22
  164.0 16.8 %collective-permute-start.39 = (bf16[256,896]{1,0:T(8,128)(2,1)}, bf16[256,896]{1,0:T(8,128)(2,1)S(1)}, u32[]{:S(2)}, u32[]{:S(2)}) collective-permute-start(bf16[256,896]{1,0:T(8,128)(2,1)} %slice.101), channel_id=1, source_target_pairs={{0,8},{4,12},{8,0},{12,4},{16,24},{20,28},{24,16},{28,20},{1,9},{5... | collective-permute-start | bytes 1376264 | tf_op jit(solution)/shard_map/ppermute | solution.py:22
  164.6 25.3 %collective-permute-start.42 = (bf16[256,896]{1,0:T(8,128)(2,1)S(1)}, bf16[256,896]{1,0:T(8,128)(2,1)S(1)}, u32[]{:S(2)}, u32[]{:S(2)}) collective-permute-start(bf16[256,896]{1,0:T(8,128)(2,1)S(1)} %fusion.34), channel_id=1, source_target_pairs={{0,8},{4,12},{8,0},{12,4},{16,24},{20,28},{24,16},{28,20},{1,9},{5... | collective-permute-start | bytes 1376264 | tf_op jit(solution)/shard_map/ppermute | solution.py:22
  173.2 16.7 %collective-permute-start.38 = (bf16[256,896]{1,0:T(8,128)(2,1)S(1)}, bf16[256,896]{1,0:T(8,128)(2,1)S(1)}, u32[]{:S(2)}, u32[]{:S(2)}) collective-permute-start(bf16[256,896]{1,0:T(8,128)(2,1)S(1)} %fusion.36), channel_id=1, source_target_pairs={{0,2},{1,3},{2,0},{3,1},{4,6},{5,7},{6,4},{7,5},{8,10},{9,11},{10,... | collective-permute-start | bytes 1376264 | tf_op jit(solution)/shard_map/ppermute | solution.py:22
  (7 other events, 45.9 us)

commit v3 on v1

v3 whole, which is shorter than its diff:
```python
import functools

import jax
import jax.numpy as jnp
from jax import lax
from jax.experimental import pallas as pl
from jax.experimental.pallas import tpu as pltpu
from jax.sharding import PartitionSpec as P

HD = 128
BLOCK = 512
FAR = 1 << 20
PAIR = 2
F32 = jnp.float32
BF16 = jnp.bfloat16
VMEM_LIMIT = 20 * 1024 * 1024


def swap(array, axis, size, distance, sender=lambda i: True):
    pairs = [(i, i ^ distance) for i in range(size) if sender(i)]
    return lax.ppermute(array, axis, pairs)


class Order:
    def __init__(self):
        self.held = {}

    def __getitem__(self, name):
        return self.held[name]

    def __setitem__(self, name, array):
        self.held[name] = array

    def after(self, names, *first):
        names = names.split() + list(first)
        tied = lax.optimization_barrier([self.held[n] for n in names])
        self.held.update(zip(names, tied))


def dot_nt(a, b):
    return lax.dot_general(a, b, (((1,), (1,)), ((), ())), preferred_element_type=F32)


def dot_nn(a, b):
    return lax.dot_general(a, b, (((1,), (0,)), ((), ())), preferred_element_type=F32)


def masked_scores(products, gap, limits, run):
    scaled = products * (HD ** -0.5)
    parts = [
        jnp.where(gap <= limit, scaled[:, i * run : (i + 1) * run], -jnp.inf)
        for i, limit in enumerate(limits)
    ]
    return jnp.concatenate(parts, axis=1)


def tile_gap(run, by):
    rows = lax.broadcasted_iota(jnp.int32, (run, run), by)
    return lax.broadcasted_iota(jnp.int32, (run, run), 1 - by) - rows


def query_scores(sets, run, half, limit_ref, q_ref, kv_refs):
    gap = tile_gap(run, 0)
    q = q_ref[half * run : (half + 1) * run]
    return [
        masked_scores(
            dot_nt(q, kv_refs[j][:, :HD]),
            gap,
            [limit_ref[half, 2 * j], limit_ref[half, 2 * j + 1]],
            run,
        )
        for j in range(sets)
    ]


def forward_kernel(sets, run, limit_ref, q_ref, grad_ref, *refs):
    kv_refs, (stat_ref, column_ref) = refs[:sets], refs[sets:]
    lane = lax.broadcasted_iota(jnp.int32, (run, HD), 1)
    for half in range(2):
        rows = pl.ds(half * run, run)
        scores = query_scores(sets, run, half, limit_ref, q_ref, kv_refs)
        highest = functools.reduce(
            jnp.maximum, [jnp.max(s, axis=1, keepdims=True) for s in scores]
        )
        expo = [jnp.exp(s - highest) for s in scores]
        inverse = 1.0 / sum(jnp.sum(e, axis=1, keepdims=True) for e in expo)
        attended = sum(
            dot_nn((e * inverse).astype(BF16), kv_refs[j][:, HD:]) for j, e in enumerate(expo)
        ).astype(BF16)
        delta = jnp.sum(
            grad_ref[rows, :].astype(F32) * attended.astype(F32), axis=1, keepdims=True
        )
        stats = jnp.where(
            lane == 0, highest, jnp.where(lane == 1, inverse, delta)
        )
        column_ref[rows, :] = stats
        stat_ref[:, rows] = jnp.transpose(stats)[:8]


def query_kernel(sets, run, limit_ref, q_ref, grad_ref, column_ref, *refs):
    kv_refs, dq_ref = refs[:sets], refs[sets]
    for half in range(2):
        rows = pl.ds(half * run, run)
        scores = query_scores(sets, run, half, limit_ref, q_ref, kv_refs)
        highest, inverse, delta = (column_ref[rows, i : i + 1] for i in range(3))
        grad = grad_ref[rows, :]
        dq = jnp.zeros((run, HD), F32)
        for j, s in enumerate(scores):
            probs = jnp.exp(s - highest) * inverse
            dprobs = dot_nt(grad, kv_refs[j][:, HD:])
            dscores = (probs * (dprobs - delta)).astype(BF16)
            dq += dot_nn(dscores, kv_refs[j][:, :HD])
        dq_ref[rows, :] = (dq * (HD ** -0.5)).astype(BF16)


def key_kernel(sets, run, limit_ref, kv_ref, *refs):
    q_refs, grad_refs, stat_refs = refs[:sets], refs[sets : 2 * sets], refs[2 * sets : 3 * sets]
    before, out_ref = refs[3 * sets : -1], refs[-1]
    gap = -tile_gap(run, 0)
    for half in range(2):
        rows = pl.ds(half * run, run)
        keys, values = kv_ref[rows, :HD], kv_ref[rows, HD:]
        dk = before[0][rows, :HD] if before else jnp.zeros((run, HD), F32)
        dv = before[0][rows, HD:] if before else jnp.zeros((run, HD), F32)
        for j in range(sets):
            q, grad, stat = q_refs[j][...], grad_refs[j][...], stat_refs[j]
            scores = masked_scores(
                dot_nt(keys, q),
                gap,
                [limit_ref[half, 2 * j], limit_ref[half, 2 * j + 1]],
                run,
            )
            probs = jnp.exp(scores - stat[0:1, :]) * stat[1:2, :]
            dprobs = dot_nt(values, grad)
            dscores = (probs * (dprobs - stat[2:3, :])).astype(BF16)
            dk += dot_nn(dscores, q) * (HD ** -0.5)
            dv += dot_nn(probs.astype(BF16), grad)
        out_ref[rows, :HD] = dk.astype(out_ref.dtype)
        out_ref[rows, HD:] = dv.astype(out_ref.dtype)


def project_kernel(groups, n_pieces, place_ref, own_ref, *refs):
    parts, pieces = refs[: len(groups)], refs[len(groups) : len(groups) + n_pieces]
    before, (out_ref, partner_ref) = refs[len(groups) + n_pieces : -2], refs[-2:]
    run = own_ref.shape[0]
    for ids, part_ref in zip(groups, parts):
        for i, e in enumerate(ids):
            partner_ref[e] = part_ref[i * run : (i + 1) * run]
    total = before[0][...] if before else None
    for i, piece_ref in enumerate(pieces):
        depth = piece_ref.shape[0]
        at = pl.multiple_of(place_ref[0, i], HD)
        rows = jnp.concatenate(
            [own_ref[:, pl.ds(at, depth)], partner_ref[place_ref[1, i]]], axis=0
        )
        term = dot_nn(rows, piece_ref[...])
        total = term if total is None else total + term
    out_ref[...] = total.astype(out_ref.dtype)


def local_call(kernel, out_shape, n_vmem, scratch=()):
    return pl.pallas_call(
        kernel,
        out_shape=out_shape,
        in_specs=[pl.BlockSpec(memory_space=pltpu.SMEM)]
        + [pl.BlockSpec(memory_space=pltpu.VMEM)] * n_vmem,
        out_specs=jax.tree.map(lambda _: pl.BlockSpec(memory_space=pltpu.VMEM), out_shape),
        scratch_shapes=scratch,
        compiler_params=pltpu.CompilerParams(vmem_limit_bytes=VMEM_LIMIT),
        cost_estimate=pl.CostEstimate(flops=1, bytes_accessed=1, transcendentals=0),
    )


def shards(n_ctx, n_f, inputs, w_qkv, selected, d_attn):
    run, width = inputs.shape
    depth = w_qkv.shape[0]
    per_f = width // n_f
    c = lax.axis_index("ctx")
    f = lax.axis_index("fsdp")
    mine = (c // PAIR) % 2
    over_ctx = functools.partial(swap, axis="ctx", size=n_ctx)
    over_f = functools.partial(swap, axis="fsdp", size=n_f)
    even = [d for d in range(n_ctx) if d % 2 == 0]
    group = [d for d in range(n_ctx) if not d & PAIR]
    sets = len(group)

    def head_of(array, which):
        return lax.dynamic_slice_in_dim(array, which * HD, HD, axis=array.ndim - 1)

    order = Order()
    near, *mids = even[1:]
    parity = c % 2
    bits = [1 << i for i in reversed(range(n_f.bit_length() - 1))]

    def kv_of(which):
        return jnp.concatenate([head_of(w_qkv[:, 1], which), head_of(w_qkv[:, 2], which)], axis=1)

    def q_of(which):
        return head_of(w_qkv[:, 0], which)

    step = depth if per_f > depth else per_f

    def part(which):
        start = f * per_f + (which * step if per_f > depth else 0)
        return lax.dynamic_slice_in_dim(inputs, start, step, axis=1)

    def start(name, array, distance, across=over_ctx):
        order[name] = across(array, distance=distance)

    def send(kind, *ds):
        for d in ds:
            start(f"{kind}{d}", order[kind + ("other" if d & PAIR else "0")], d)

    def relay(kind, *ds):
        for d in ds:
            start(f"{kind}{d ^ 1}", order[f"{kind}{d}"], 1)

    def spread(kind, groups):
        bit = bits[len(groups) - 1]
        held = [order[f"{kind}{i}"] for i in range(len(groups))]
        start(f"{kind}{len(groups)}", jnp.concatenate(held, axis=0) if held[1:] else held[0], bit, over_f)
        return groups + [[e ^ bit for ids in groups for e in ids]]

    def project(kind, ds, x_kind, groups, before=None):
        pieces = [order[f"{kind}{d}"] for d in ds]
        first = jnp.stack([(c ^ d) * depth for d in ds])
        place = jnp.stack([first, (first // per_f) ^ f]).astype(jnp.int32)
        held = [order[f"{x_kind}{i}"] for i in range(len(groups))]
        out = jax.ShapeDtypeStruct((2 * run, pieces[0].shape[1]), F32 if before is None else BF16)
        earlier = [] if before is None else [before]
        return local_call(
            functools.partial(project_kernel, groups, len(ds)),
            out,
            1 + len(held) + len(ds) + len(earlier),
            [pltpu.VMEM((n_f, run, step), BF16)],
        )(place, inputs, *held, *pieces, *earlier)

    def top(d):
        return 1 << (d.bit_length() - 1)

    def to_later(array, distance):
        ordered = top(distance) > PAIR
        return over_ctx(array, distance=distance, sender=lambda i: not (ordered and i & top(distance)))

    def to_earlier(array, distance):
        ordered = top(distance) > PAIR
        return over_ctx(array, distance=distance, sender=lambda i: not ordered or i & top(distance))

    odd = [d ^ 1 for d in even]
    others = group[:0:-1]
    far = mids[0]
    order["kv0"], order["kvother"] = kv_of(mine), kv_of(1 - mine)
    order["part_a"], order["part_b"] = part(parity), part(1 - parity)
    order["q0"], order["qother"] = q_of(mine), q_of(1 - mine)
    order["g0"], order["gother"] = head_of(d_attn, mine), head_of(d_attn, 1 - mine)
    send("kv", far, near)
    relay("kv", 0)
    start("a0", order["part_a"], PAIR)
    start("gpair", order["gother"], PAIR)
    order.after("q0", "kv1")
    relay("q", 0)
    order.after("kvother kv0 part_b", f"kv{far}", "a0", "gpair", "q1")
    groups_a = spread("a", [[0]])
    relay("kv", far, near)
    send("kv", *mids[1:])
    start("b0", order["part_b"], PAIR)
    for _ in bits[1:]:
        groups_a = spread("a", groups_a)
    order["grad"] = jnp.concatenate([order["g0"], order["gpair"]], axis=0)

    order.after("q0 qother", f"kv{mids[1]}", f"kv{far ^ 1}")
    relay("kv", *mids[1:])
    groups_b = spread("b", [[0]])
    send("q", *mids)
    order.after("qother", f"a{len(groups_a) - 1}")
    send("q", near)
    order["kv_even"] = project("kv", even, "a", groups_a)
    order.after("b0 b1", *[f"kv{d ^ 1}" for d in mids[1:]])
    for _ in bits[1:]:
        groups_b = spread("b", groups_b)
    last = ("b", groups_b) if per_f > depth else ("a", groups_a)
    order["kv"] = project("kv", odd, *last, order["kv_even"])

    for d in others[:-1]:
        start(f"keys{d}", order["kv"], d, to_later)
    moved = mids + [near]
    start("passed", jnp.concatenate([order[f"q{d}"] for d in moved], axis=0), 1)
    order.after("kv", "passed")
    start(f"keys{others[-1]}", order["kv"], others[-1], to_later)
    for i, d in enumerate(moved):
        order[f"q{d ^ 1}"] = order["passed"][i * depth : (i + 1) * depth]
    order["q_even"] = project("q", even, "a", groups_a)
    order.after("grad", "kv")
    for d in others:
        start(f"grad{d}", order["grad"], d, to_earlier)
    order["q"] = project("q", odd, *last, order["q_even"])
    order.after("q", *[f"grad{d}" for d in others[:-1]])
    for d in others:
        start(f"query{d}", order["q"], d, to_earlier)
    kv, q, grad = order["kv"], order["q"], order["grad"]
    kv_pieces = {d: order[f"kv{d}"] for d in range(n_ctx)}
    q_pieces = {d: order[f"q{d}"] for d in range(n_ctx)}
    kvs = [kv] + [order[f"keys{d}"] for d in group[1:]]
    grads = [grad] + [order[f"grad{d}"] for d in group[1:]]
    qs = [q] + [order[f"query{d}"] for d in group[1:]]

    runs = jnp.stack([c ^ d ^ p for d in group for p in (0, PAIR)])
    blocks = runs * run // BLOCK
    here = runs[:2]

    def limits(query_runs, key_runs, query_blocks, key_blocks):
        chosen = jnp.any(
            selected[query_blocks][:, :, None] == key_blocks[None, None, :], axis=1
        )
        ahead = query_runs[:, None] - key_runs[None, :]
        bound = jnp.where(ahead > 0, FAR, jnp.where(ahead == 0, 0, -FAR))
        return jnp.where(chosen, bound, -FAR).astype(jnp.int32)

    query_limits = limits(here, runs, blocks[:2], blocks)
    key_limits = limits(runs, here, blocks, blocks[:2]).T

    stat, column = local_call(
        functools.partial(forward_kernel, sets, run),
        (
            jax.ShapeDtypeStruct((8, 2 * run), F32),
            jax.ShapeDtypeStruct((2 * run, HD), F32),
        ),
        2 + sets,
    )(query_limits, q, grad, *kvs)
    stats = [stat] + [to_earlier(stat, distance=d) for d in group[1:]]
    dq = local_call(
        functools.partial(query_kernel, sets, run),
        jax.ShapeDtypeStruct((2 * run, HD), BF16),
        3 + sets,
    )(query_limits, q, grad, column, *kvs)
    close = 2
    dkv = local_call(
        functools.partial(key_kernel, close, run),
        jax.ShapeDtypeStruct((2 * run, 2 * HD), F32),
        1 + 3 * close,
    )(key_limits[:, : 2 * close], kv, *qs[:close], *grads[:close], *stats[:close])
    dkv = local_call(
        functools.partial(key_kernel, sets - close, run),
        jax.ShapeDtypeStruct((2 * run, 2 * HD), BF16),
        2 + 3 * (sets - close),
    )(key_limits[:, 2 * close :], kv, *qs[close:], *grads[close:], *stats[close:], dkv)

    all_grads = jnp.concatenate([dkv, dq], axis=1)
    if n_f != 4 or n_ctx != 2 * n_f:
        whole_w = jnp.zeros((width, 3 * HD), BF16)
        for d in kv_pieces:
            piece = jnp.concatenate([kv_pieces[d], q_pieces[d]], axis=1)
            whole_w = lax.dynamic_update_slice(whole_w, piece, ((c ^ d) * depth, 0))
        partial_out = dot_nt(all_grads, whole_w).astype(BF16)
        total = partial_out[:run].astype(F32) + over_ctx(partial_out[run:], distance=PAIR).astype(F32)
        return lax.psum_scatter(total.astype(BF16), "fsdp", scatter_dimension=1, tiled=True)

    stacked = jnp.concatenate(
        [
            jnp.concatenate([kv_pieces[d] for d in range(n_ctx)], axis=0),
            jnp.concatenate([q_pieces[d] for d in range(n_ctx)], axis=0),
        ],
        axis=1,
    )

    half = per_f // 2
    by_core = functools.partial(over_f, distance=1)
    by_x = functools.partial(over_f, distance=2)
    by_z = functools.partial(over_ctx, distance=PAIR)

    def term(which, e, start=0, size=per_f):
        at = ((f ^ e) ^ (c // 2)) * per_f + start
        rows = lax.dynamic_slice_in_dim(stacked, at, size, axis=0)
        return dot_nt(all_grads[which * run : (which + 1) * run], rows)

    def chip(which, e, *columns):
        return term(which, e, *columns) + by_core(term(which, e ^ 1, *columns).astype(BF16)).astype(F32)

    corner_x = by_x(chip(1, 2, 0, half).astype(BF16))
    corner_z = by_z(chip(1, 2, half, half).astype(BF16))
    for_x = chip(0, 2)
    from_x_a = by_x(for_x[:, :half].astype(BF16))
    for_z = chip(1, 0)
    from_z_b = by_z(for_z[:, half:].astype(BF16))
    here = chip(0, 0)
    from_z_a = by_z((for_z[:, :half] + corner_x.astype(F32)).astype(BF16))
    from_x_b = by_x((for_x[:, half:] + corner_z.astype(F32)).astype(BF16))

    def finish_kernel(swapped_ref, here_ref, x_a, x_b, z_a, z_b, out_ref):
        for i, (x_ref, z_ref) in enumerate(((x_a, z_a), (x_b, z_b))):
            total = here_ref[:, i * half : (i + 1) * half] + x_ref[...].astype(F32) + z_ref[...].astype(F32)
            at = pl.multiple_of((swapped_ref[0] ^ i) * half, HD)
            out_ref[:, pl.ds(at, half)] = total.astype(BF16)

    return local_call(
        finish_kernel, jax.ShapeDtypeStruct((run, per_f), BF16), 5
    )(parity.reshape(1).astype(jnp.int32), here, from_x_a, from_x_b, from_z_a, from_z_b)


def solution(mesh):
    placed = (P("ctx", None), P("ctx", None, "fsdp"), P(), P("ctx", "fsdp"))
    body = functools.partial(shards, mesh.shape["ctx"], mesh.shape["fsdp"])
    return jax.shard_map(
        body, mesh=mesh, in_specs=placed, out_specs=P("ctx", "fsdp"), check_vma=False
    )
```

time: 236 us -> 172 us (0.73)
  waiting for transfers between devices: 128 us -> 83.1 us
  local copies, waits for them, and re-layouts: 28.5 us -> 10.5 us
  Pallas kernels: 8.35 us -> 20.6 us
  matrix products: 16.9 us -> 5.89 us
    ppermute x39 -> x42, waiting for transfers between devices: 128 us -> 83.1 us  [swap(): return lax.ppermute(array, axis, pairs)]
    dynamic_update_slice x19 -> x0, local copies, waits for them, and re-layouts: 13.1 us -> none  [the longest x8 6.97 us: shards(): lax.dynamic_update_slice(whole_w, q_pieces[d], ((c ^ d) * depth, 2 * HD))]
    pallas_call x2 -> x9, Pallas kernels: 8.35 us -> 20.6 us  [the longest x4 8.63 us: project(): local_call(functools.partial(project_kernel, groups, len(ds)), out, 1 + l...]
    dot_general x16 -> x0, matrix products: 6.9 us -> none  [dot_nn(): lax.dot_general(a, b, (((1,), (0,)), ((), ())), preferred_element_type=F32)]
    concatenate x1 -> x2, local copies, waits for them, and re-layouts: 5.76 us -> 0.14 us  [the longest x1 0.11 us: shards(): jnp.concatenate([q_pieces[d] for d in range(n_ctx)], axis=0)]
    unnamed x4 -> x30, local copies, waits for them, and re-layouts: 0.01 us -> 4.53 us
    dot_general x4 -> x10, matrix products: 9.99 us -> 5.89 us  [dot_nt(): lax.dot_general(a, b, (((1,), (1,)), ((), ())), preferred_element_type=F32)]
    broadcast_in_dim x1 -> x0, local copies, waits for them, and re-layouts: 2.93 us -> none  [shards(): whole_w = jnp.zeros((width, 3 * HD), BF16)]
  transfers between devices with their start and end apart: 39 -> 42, of which waited for: 15 -> 17; matrix products, arithmetic and copies ran while one was open for 17% -> 10% of each run, Pallas kernels for 2% -> 10%
where the time goes in v3:
time: 172 us
  waiting for transfers between devices  83.1 us (48%)
  starting transfers between devices  47.9 us (28%)
  Pallas kernels  20.6 us (12%)
  local copies, waits for them, and re-layouts  10.5 us (6%)
  matrix products  5.89 us (3%)
  other arithmetic  3.1 us (2%)
    ppermute x42, waiting for transfers between devices, swap(): return lax.ppermute(array, axis, pairs)  83.1 us
    ppermute x42, starting transfers between devices, swap(): return lax.ppermute(array, axis, pairs)  47.9 us
    pallas_call x4, Pallas kernels, project(): local_call(functools.partial(project_kernel, groups, len(ds)), out, 1 + l...  8.63 us
    dot_general x10, matrix products, dot_nt(): lax.dot_general(a, b, (((1,), (1,)), ((), ())), preferred_element_type=F32)  5.89 us
    unnamed x30, local copies, waits for them, and re-layouts  4.53 us
  transfers between devices with their start and end apart: 42, of which 17 were waited for; matrix products, arithmetic and copies ran while one was open for 10% of the time, Pallas kernels for 10%

profile of v3, /device:TPU:0, one launch (start us, length us, event | category | flops | bytes accessed | tf_op | source)
XLA Modules:
  0.0 171.8 jit_solution(13208415519262205743)
XLA Ops:
  0.0 1.4 fusion.37
  1.7 3.0 %collective-permute-start.3 = (bf16[896,256]{1,0:T(8,128)(2,1)S(1)}, bf16[896,256]{1,0:T(8,128)(2,1)S(1)}, u32[]{:S(2)}, u32[]{:S(2)}) collective-permute-start(bf16[896,256]{1,0:T(8,128)(2,1)S(1)} %pad_maximum_fusion.4.refs_3_), channel_id=1, source_target_pairs={{0,4},{4,0},{8,12},{12,8},{16,20},{20,16},{24,28},{28,24},{1,5},{5... | collective-permute-start | bytes 1376264 | tf_op jit(solution)/shard_map/ppermute | solution.py:21
  4.7 2.6 %collective-permute-start = (bf16[896,256]{1,0:T(8,128)(2,1)S(1)}, bf16[896,256]{1,0:T(8,128)(2,1)}, u32[]{:S(2)}, u32[]{:S(2)}) collective-permute-start(bf16[896,256]{1,0:T(8,128)(2,1)S(1)} %pad_maximum_fusion.4.refs_3_), channel_id=1, source_target_pairs={{0,16},{4,20},{8,24},{12,28},{16,0},{20,4},{24,8},{28,12},{1,17},{... | collective-permute-start | bytes 1376264 | tf_op jit(solution)/shard_map/ppermute | solution.py:21
  7.3 1.6 collective-permute-start.2
  8.9 2.0 %constant_dynamic-slice_fusion.1 = (bf16[256,896]{1,0:T(8,128)(2,1)S(1)}, bf16[256,896]{1,0:T(8,128)(2,1)}) fusion(bf16[256,7168]{1,0:T(8,128)(2,1)} %own_ref.7, s32[]{:T(128)S(6)} %select_n.159, s32[]{:T(128)S(6)} %select_n.158), kind=kLoop, calls=%fused_computation.83 | loop fusion | bytes 1835016 | tf_op jit(solution)/shard_map/dynamic_slice | solution.py:205
  12.2 1.6 collective-permute-start.11
  15.2 1.7 %collective-permute-start.4 = (bf16[896,128]{1,0:T(8,128)(2,1)S(1)}, bf16[896,128]{1,0:T(8,128)(2,1)S(1)}, u32[]{:S(2)}, u32[]{:S(2)}) collective-permute-start(bf16[896,128]{1,0:T(8,128)(2,1)S(1)} %get-tuple-element.47.refs_3_), channel_id=1, source_target_pairs={{0,4},{4,0},{8,12},{12,8},{16,20},{20,16},{24,28},{28,24},{1,5},{5... | collective-permute-start | bytes 688136 | tf_op jit(solution)/shard_map/ppermute | solution.py:21
  17.2 2.5 %collective-permute-done.2 = bf16[256,128]{1,0:T(8,128)(2,1)S(1)} collective-permute-done((bf16[256,128]{1,0:T(8,128)(2,1)S(1)}, bf16[256,128]{1,0:T(8,128)(2,1)S(1)}, u32[]{:S(2)}, u32[]{:S(2)}) %collective-permute-start.2) | collective-permute-done | bytes 65568 | tf_op jit(solution)/shard_map/ppermute | solution.py:21
  19.7 13.4 %collective-permute-done.1.refs_0_ = bf16[256,896]{1,0:T(8,128)(2,1)S(1)} collective-permute-done((bf16[256,896]{1,0:T(8,128)(2,1)S(1)}, bf16[256,896]{1,0:T(8,128)(2,1)S(1)}, u32[]{:S(2)}, u32[]{:S(2)}) %collective-permute-start.1) | collective-permute-done | bytes 458784 | tf_op jit(solution)/shard_map/ppermute | solution.py:21
  33.1 1.6 collective-permute-start.13
  36.3 1.3 collective-permute-start.7
  38.1 3.6 %collective-permute-done.13.refs_1_ = bf16[256,896]{1,0:T(8,128)(2,1)S(1)} collective-permute-done((bf16[256,896]{1,0:T(8,128)(2,1)S(1)}, bf16[256,896]{1,0:T(8,128)(2,1)S(1)}, u32[]{:S(2)}, u32[]{:S(2)}) %collective-permute-start.13) | collective-permute-done | bytes 458784 | tf_op jit(solution)/shard_map/ppermute | solution.py:21
  42.9 16.8 %collective-permute-done.7.refs_6_ = bf16[896,256]{1,0:T(8,128)(2,1)} collective-permute-done((bf16[896,256]{1,0:T(8,128)(2,1)}, bf16[896,256]{1,0:T(8,128)(2,1)}, u32[]{:S(2)}, u32[]{:S(2)}) %collective-permute-start.7) | collective-permute-done | bytes 458784 | tf_op jit(solution)/shard_map/ppermute | solution.py:21
  60.6 1.5 collective-permute-start.6
  63.2 2.1 %collective-permute-start.16 = (bf16[896,128]{1,0:T(8,128)(2,1)S(1)}, bf16[896,128]{1,0:T(8,128)(2,1)S(1)}, u32[]{:S(2)}, u32[]{:S(2)}) collective-permute-start(bf16[896,128]{1,0:T(8,128)(2,1)S(1)} %copy-done.4), channel_id=1, source_target_pairs={{0,24},{4,28},{8,16},{12,20},{16,8},{20,12},{24,0},{28,4},{1,25},{... | collective-permute-start | bytes 688136 | tf_op jit(solution)/shard_map/ppermute | solution.py:21
  65.3 2.4 %collective-permute-start.17 = (bf16[896,128]{1,0:T(8,128)(2,1)S(1)}, bf16[896,128]{1,0:T(8,128)(2,1)S(1)}, u32[]{:S(2)}, u32[]{:S(2)}) collective-permute-start(bf16[896,128]{1,0:T(8,128)(2,1)S(1)} %copy-done.4), channel_id=1, source_target_pairs={{0,8},{4,12},{8,0},{12,4},{16,24},{20,28},{24,16},{28,20},{1,9},{5... | collective-permute-start | bytes 688136 | tf_op jit(solution)/shard_map/ppermute | solution.py:21
  67.7 3.2 %collective-permute-done.6.refs_1_ = bf16[256,896]{1,0:T(8,128)(2,1)S(1)} collective-permute-done((bf16[256,896]{1,0:T(8,128)(2,1)S(1)}, bf16[256,896]{1,0:T(8,128)(2,1)S(1)}, u32[]{:S(2)}, u32[]{:S(2)}) %collective-permute-start.6) | collective-permute-done | bytes 458784 | tf_op jit(solution)/shard_map/ppermute | solution.py:21
  70.9 1.5 collective-permute-start.12
  73.6 8.9 %collective-permute-done.15.refs_5_ = bf16[896,128]{1,0:T(8,128)(2,1)S(1)} collective-permute-done((bf16[896,128]{1,0:T(8,128)(2,1)S(1)}, bf16[896,128]{1,0:T(8,128)(2,1)S(1)}, u32[]{:S(2)}, u32[]{:S(2)}) %collective-permute-start.15) | collective-permute-done | bytes 229408 | tf_op jit(solution)/shard_map/ppermute | solution.py:21
  82.6 1.2 collective-permute-start.18
  86.0 2.7 %shard_map.46.refs_7_ = f32[512,256]{1,0:T(8,128)S(1)} custom-call(s32[2,4]{1,0:T(2,128)S(1)} %pad_add_fusion.1.place_ref, bf16[256,7168]{1,0:T(8,128)(2,1)S(1)} %copy-done.1, bf16[256,896]{1,0:T(8,128)(2,1)S(1)} %collective-permute-done.1.refs_0_, bf16[256,896]{1,0:T(8,128)(2,1)S(1)} %collective-permute-done.13.refs_1_, ...), custom_call_target="tpu_custom_call" | custom-call | flops 1 | bytes 1 | tf_op jit(solution)/shard_map/pallas_call | solution.py:231
  88.7 1.8 %shard_map.48.refs_7_ = f32[512,128]{1,0:T(8,128)S(1)} custom-call(s32[2,4]{1,0:T(2,128)S(1)} %pad_add_fusion.1.place_ref, bf16[256,7168]{1,0:T(8,128)(2,1)S(1)} %copy-done.1, bf16[256,896]{1,0:T(8,128)(2,1)S(1)} %collective-permute-done.1.refs_0_, bf16[256,896]{1,0:T(8,128)(2,1)S(1)} %collective-permute-done.13.refs_1_, ...), custom_call_target="tpu_custom_call" | custom-call | flops 1 | bytes 1 | tf_op jit(solution)/shard_map/pallas_call | solution.py:231
  90.5 2.4 %shard_map.47.refs_0_.kv_ref = bf16[512,256]{1,0:T(8,128)(2,1)S(1)} custom-call(s32[2,4]{1,0:T(2,128)S(1)} %pad_add_fusion.place_ref, bf16[256,7168]{1,0:T(8,128)(2,1)S(1)} %copy-done.1, bf16[256,896]{1,0:T(8,128)(2,1)S(1)} %collective-permute-done.5.refs_0_, bf16[256,896]{1,0:T(8,128)(2,1)S(1)} %collective-permute-done.6.refs_1_, ...), custom_call_target="tpu_custom_call" | custom-call | flops 1 | bytes 1 | tf_op jit(solution)/shard_map/pallas_call | solution.py:231
  92.9 1.9 %collective-permute-start.25 = (bf16[512,256]{1,0:T(8,128)(2,1)S(1)}, bf16[512,256]{1,0:T(8,128)(2,1)S(1)}, u32[]{:S(2)}, u32[]{:S(2)}) collective-permute-start(bf16[512,256]{1,0:T(8,128)(2,1)S(1)} %shard_map.47.refs_0_.kv_ref), channel_id=1, source_target_pairs={{0,20},{4,16},{8,28},{12,24},{1,21},{5,17},{9,29},{13,25},{2,22},{... | collective-permute-start | bytes 786440 | tf_op jit(solution)/shard_map/ppermute | solution.py:21
  94.8 1.3 collective-permute-start.24
  96.1 1.6 collective-permute-done.18
  97.7 1.3 collective-permute-start.20
  99.0 1.3 collective-permute-start.19
  100.3 1.7 collective-permute-start.23
  102.2 1.8 %shard_map.49.q_ref.refs_0_ = bf16[512,128]{1,0:T(8,128)(2,1)S(1)} custom-call(s32[2,4]{1,0:T(2,128)S(1)} %pad_add_fusion.place_ref, bf16[256,7168]{1,0:T(8,128)(2,1)S(1)} %copy-done.1, bf16[256,896]{1,0:T(8,128)(2,1)S(1)} %collective-permute-done.5.refs_0_, bf16[256,896]{1,0:T(8,128)(2,1)S(1)} %collective-permute-done.6.refs_1_, ...), custom_call_target="tpu_custom_call" | custom-call | flops 1 | bytes 1 | tf_op jit(solution)/shard_map/pallas_call | solution.py:231
  104.0 6.1 %collective-permute-done.20.refs_2_ = bf16[512,128]{1,0:T(8,128)(2,1)S(1)} collective-permute-done((bf16[512,128]{1,0:T(8,128)(2,1)S(1)}, bf16[512,128]{1,0:T(8,128)(2,1)S(1)}, u32[]{:S(2)}, u32[]{:S(2)}) %collective-permute-start.20) | collective-permute-done | bytes 131104 | tf_op jit(solution)/shard_map/ppermute | solution.py:21
  110.1 1.5 collective-permute-start.29
  114.2 1.3 collective-permute-start.22
  115.5 1.3 collective-permute-start.21
  116.8 2.9 %shard_map.50 = (f32[8,512]{1,0:T(8,128)S(1)}, f32[512,128]{1,0:T(8,128)S(1)}) custom-call(s32[2,8]{1,0:T(2,128)S(1)} %get-tuple-element.80.limit_ref, bf16[512,128]{1,0:T(8,128)(2,1)S(1)} %shard_map.49.q_ref.refs_0_, bf16[512,128]{1,0:T(8,128)(2,1)S(1)} %pad_maximum_fusion.6.grad_ref.refs_2_, bf16[512,256]{1,0:T(8,128)(2,1)S(1)} %shard_map.47.refs_0_.kv_ref, ...), custom_call_target="tpu_custom_call" | custom-call | flops 1 | bytes 1 | tf_op jit(solution)/shard_map/pallas_call | solution.py:322
  119.7 1.7 %collective-permute-start.30 = (f32[8,512]{1,0:T(8,128)S(1)}, f32[8,512]{1,0:T(8,128)S(1)}, u32[]{:S(2)}, u32[]{:S(2)}) collective-permute-start(f32[8,512]{1,0:T(8,128)S(1)} %get-tuple-element.57.refs_4_), channel_id=1, source_target_pairs={{0,4},{4,0},{8,12},{12,8},{16,20},{20,16},{24,28},{28,24},{1,5},{5... | collective-permute-start | bytes 49160 | tf_op jit(solution)/shard_map/ppermute | solution.py:21
  121.4 1.3 collective-permute-start.27
  122.7 1.5 collective-permute-start.26
  124.4 3.2 %shard_map.53 = bf16[512,128]{1,0:T(8,128)(2,1)S(1)} custom-call(s32[2,8]{1,0:T(2,128)S(1)} %get-tuple-element.80.limit_ref, bf16[512,128]{1,0:T(8,128)(2,1)S(1)} %shard_map.49.q_ref.refs_0_, bf16[512,128]{1,0:T(8,128)(2,1)S(1)} %pad_maximum_fusion.6.grad_ref.refs_2_, f32[512,128]{1,0:T(8,128)S(1)} %get-tuple-element.58.column_ref, ...), custom_call_target="tpu_custom_call" | custom-call | flops 1 | bytes 1 | tf_op jit(solution)/shard_map/pallas_call | solution.py:331
  127.6 2.3 %shard_map.51.refs_6_ = f32[512,256]{1,0:T(8,128)S(1)} custom-call(s32[2,4]{1,0:T(2,128)S(1)} %get-tuple-element.78.limit_ref, bf16[512,256]{1,0:T(8,128)(2,1)S(1)} %shard_map.47.refs_0_.kv_ref, bf16[512,128]{1,0:T(8,128)(2,1)S(1)} %shard_map.49.q_ref.refs_0_, bf16[512,128]{1,0:T(8,128)(2,1)S(1)} %collective-permute-done.28.refs_1_, ...), custom_call_target="tpu_custom_call" | custom-call | flops 1 | bytes 1 | tf_op jit(solution)/shard_map/pallas_call | solution.py:337
  130.0 2.3 %shard_map.52 = bf16[512,256]{1,0:T(8,128)(2,1)S(1)} custom-call(s32[2,4]{1,0:T(2,128)S(1)} %get-tuple-element.79.limit_ref, bf16[512,256]{1,0:T(8,128)(2,1)S(1)} %shard_map.47.refs_0_.kv_ref, bf16[512,128]{1,0:T(8,128)(2,1)S(1)} %collective-permute-done.21.refs_0_, bf16[512,128]{1,0:T(8,128)(2,1)S(1)} %collective-permute-done.22.refs_1_, ...), custom_call_target="tpu_custom_call" | custom-call | flops 1 | bytes 1 | tf_op jit(solution)/shard_map/pallas_call | solution.py:342
  139.7 1.5 collective-permute-start.33
  141.9 1.5 collective-permute-start.41
  143.4 8.3 %collective-permute-done.35 = bf16[256,896]{1,0:T(8,128)(2,1)S(1)} collective-permute-done((bf16[256,896]{1,0:T(8,128)(2,1)S(1)}, bf16[256,896]{1,0:T(8,128)(2,1)S(1)}, u32[]{:S(2)}, u32[]{:S(2)}) %collective-permute-start.35) | collective-permute-done | bytes 458784 | tf_op jit(solution)/shard_map/ppermute | solution.py:21
  151.8 1.5 collective-permute-start.36
  154.8 5.6 %collective-permute-done.33.x_a = bf16[256,896]{1,0:T(8,128)(2,1)S(1)} collective-permute-done((bf16[256,896]{1,0:T(8,128)(2,1)S(1)}, bf16[256,896]{1,0:T(8,128)(2,1)S(1)}, u32[]{:S(2)}, u32[]{:S(2)}) %collective-permute-start.33) | collective-permute-done | bytes 458784 | tf_op jit(solution)/shard_map/ppermute | solution.py:21
  161.5 8.2 %collective-permute-done.36.x_b = bf16[256,896]{1,0:T(8,128)(2,1)S(1)} collective-permute-done((bf16[256,896]{1,0:T(8,128)(2,1)S(1)}, bf16[256,896]{1,0:T(8,128)(2,1)S(1)}, u32[]{:S(2)}, u32[]{:S(2)}) %collective-permute-start.36) | collective-permute-done | bytes 458784 | tf_op jit(solution)/shard_map/ppermute | solution.py:21
  170.6 1.2 shard_map.54
  (125 shorter events, 26.5 us)
Async XLA Ops:
  0.0 34.8 %copy-start = (s32[4,4]{1,0:T(4,128)S(1)}, s32[4,4]{1,0:T(4,128)}, u32[]{:S(2)}) copy-start(s32[4,4]{1,0:T(4,128)} %param.6) | copy-start | bytes 196
  1.4 5.9 %copy-start.5 = (bf16[256,256]{1,0:T(8,128)(2,1)S(1)}, bf16[256,256]{1,0:T(8,128)(2,1)}, u32[]{:S(2)}) copy-start(bf16[256,256]{1,0:T(8,128)(2,1)} %param.7) | copy-start | bytes 393220
  1.7 13.6 %collective-permute-start.3 = (bf16[896,256]{1,0:T(8,128)(2,1)S(1)}, bf16[896,256]{1,0:T(8,128)(2,1)S(1)}, u32[]{:S(2)}, u32[]{:S(2)}) collective-permute-start(bf16[896,256]{1,0:T(8,128)(2,1)S(1)} %pad_maximum_fusion.4.refs_3_), channel_id=1, source_target_pairs={{0,4},{4,0},{8,12},{12,8},{16,20},{20,16},{24,28},{28,24},{1,5},{5... | collective-permute-start | bytes 1376264 | tf_op jit(solution)/shard_map/ppermute | solution.py:21
  4.7 28.4 %collective-permute-start = (bf16[896,256]{1,0:T(8,128)(2,1)S(1)}, bf16[896,256]{1,0:T(8,128)(2,1)}, u32[]{:S(2)}, u32[]{:S(2)}) collective-permute-start(bf16[896,256]{1,0:T(8,128)(2,1)S(1)} %pad_maximum_fusion.4.refs_3_), channel_id=1, source_target_pairs={{0,16},{4,20},{8,24},{12,28},{16,0},{20,4},{24,8},{28,12},{1,17},{... | collective-permute-start | bytes 1376264 | tf_op jit(solution)/shard_map/ppermute | solution.py:21
  7.3 12.4 %collective-permute-start.2 = (bf16[256,128]{1,0:T(8,128)(2,1)S(1)}, bf16[256,128]{1,0:T(8,128)(2,1)S(1)}, u32[]{:S(2)}, u32[]{:S(2)}) collective-permute-start(bf16[256,128]{1,0:T(8,128)(2,1)S(1)} %get-tuple-element.77), channel_id=1, source_target_pairs={{0,8},{4,12},{8,0},{12,4},{16,24},{20,28},{24,16},{28,20},{1,9},{5... | collective-permute-start | bytes 196616 | tf_op jit(solution)/shard_map/ppermute | solution.py:21
  10.9 22.2 %collective-permute-start.1 = (bf16[256,896]{1,0:T(8,128)(2,1)S(1)}, bf16[256,896]{1,0:T(8,128)(2,1)S(1)}, u32[]{:S(2)}, u32[]{:S(2)}) collective-permute-start(bf16[256,896]{1,0:T(8,128)(2,1)S(1)} %get-tuple-element.59), channel_id=1, source_target_pairs={{0,8},{4,12},{8,0},{12,4},{16,24},{20,28},{24,16},{28,20},{1,9},{5... | collective-permute-start | bytes 1376264 | tf_op jit(solution)/shard_map/ppermute | solution.py:21
  12.2 49.9 %collective-permute-start.11 = (bf16[896,256]{1,0:T(8,128)(2,1)}, bf16[896,256]{1,0:T(8,128)(2,1)}, u32[]{:S(2)}, u32[]{:S(2)}) collective-permute-start(bf16[896,256]{1,0:T(8,128)(2,1)} %pad_maximum_fusion.3), channel_id=1, source_target_pairs={{0,8},{4,12},{8,0},{12,4},{16,24},{20,28},{24,16},{28,20},{1,9},{5... | collective-permute-start | bytes 1376264 | tf_op jit(solution)/shard_map/ppermute | solution.py:21
  15.2 17.9 %collective-permute-start.4 = (bf16[896,128]{1,0:T(8,128)(2,1)S(1)}, bf16[896,128]{1,0:T(8,128)(2,1)S(1)}, u32[]{:S(2)}, u32[]{:S(2)}) collective-permute-start(bf16[896,128]{1,0:T(8,128)(2,1)S(1)} %get-tuple-element.47.refs_3_), channel_id=1, source_target_pairs={{0,4},{4,0},{8,12},{12,8},{16,20},{20,16},{24,28},{28,24},{1,5},{5... | collective-permute-start | bytes 688136 | tf_op jit(solution)/shard_map/ppermute | solution.py:21
  19.7 22.0 %copy-start.6 = (bf16[256,128]{1,0:T(8,128)(2,1)}, bf16[256,128]{1,0:T(8,128)(2,1)S(1)}, u32[]{:S(2)}) copy-start(bf16[256,128]{1,0:T(8,128)(2,1)S(1)} %collective-permute-done.2) | copy-start | bytes 196612
  33.1 8.5 %collective-permute-start.13 = (bf16[256,896]{1,0:T(8,128)(2,1)S(1)}, bf16[256,896]{1,0:T(8,128)(2,1)S(1)}, u32[]{:S(2)}, u32[]{:S(2)}) collective-permute-start(bf16[256,896]{1,0:T(8,128)(2,1)S(1)} %collective-permute-done.1.refs_0_), channel_id=1, source_target_pairs={{0,2},{1,3},{2,0},{3,1},{4,6},{5,7},{6,4},{7,5},{8,10},{9,11},{10,... | collective-permute-start | bytes 1376264 | tf_op jit(solution)/shard_map/ppermute | solution.py:21
  36.2 24.4 %collective-permute-start.5 = (bf16[256,896]{1,0:T(8,128)(2,1)}, bf16[256,896]{1,0:T(8,128)(2,1)S(1)}, u32[]{:S(2)}, u32[]{:S(2)}) collective-permute-start(bf16[256,896]{1,0:T(8,128)(2,1)} %get-tuple-element.34), channel_id=1, source_target_pairs={{0,8},{4,12},{8,0},{12,4},{16,24},{20,28},{24,16},{28,20},{1,9},{5... | collective-permute-start | bytes 1376264 | tf_op jit(solution)/shard_map/ppermute | solution.py:21
  36.3 23.4 %collective-permute-start.7 = (bf16[896,256]{1,0:T(8,128)(2,1)}, bf16[896,256]{1,0:T(8,128)(2,1)}, u32[]{:S(2)}, u32[]{:S(2)}) collective-permute-start(bf16[896,256]{1,0:T(8,128)(2,1)} %pad_maximum_fusion.3), channel_id=1, source_target_pairs={{0,24},{4,28},{8,16},{12,20},{16,8},{20,12},{24,0},{28,4},{1,25},{... | collective-permute-start | bytes 1376264 | tf_op jit(solution)/shard_map/ppermute | solution.py:21
  37.6 22.1 %collective-permute-start.8 = (bf16[896,256]{1,0:T(8,128)(2,1)}, bf16[896,256]{1,0:T(8,128)(2,1)}, u32[]{:S(2)}, u32[]{:S(2)}) collective-permute-start(bf16[896,256]{1,0:T(8,128)(2,1)} %collective-permute-done.refs_5_), channel_id=1, source_target_pairs={{0,4},{4,0},{8,12},{12,8},{16,20},{20,16},{24,28},{28,24},{1,5},{5... | collective-permute-start | bytes 1376264 | tf_op jit(solution)/shard_map/ppermute | solution.py:21
  42.7 22.6 %collective-permute-start.14 = (bf16[512,896]{1,0:T(8,128)(2,1)}, bf16[512,896]{1,0:T(8,128)(2,1)S(1)}, u32[]{:S(2)}, u32[]{:S(2)}) collective-permute-start(bf16[512,896]{1,0:T(8,128)(2,1)} %pad_maximum_fusion.1), channel_id=1, source_target_pairs={{0,1},{1,0},{2,3},{3,2},{4,5},{5,4},{6,7},{7,6},{8,9},{9,8},{10,11... | collective-permute-start | bytes 2752520 | tf_op jit(solution)/shard_map/ppermute | solution.py:21
  42.8 20.4 %copy-start.4 = (bf16[896,128]{1,0:T(8,128)(2,1)S(1)}, bf16[896,128]{1,0:T(8,128)(2,1)}, u32[]{:S(2)}) copy-start(bf16[896,128]{1,0:T(8,128)(2,1)} %get-tuple-element.48) | copy-start | bytes 688132
  42.8 24.9 %copy-start.7 = (bf16[256,128]{1,0:T(8,128)(2,1)S(1)}, bf16[256,128]{1,0:T(8,128)(2,1)}, u32[]{:S(2)}) copy-start(bf16[256,128]{1,0:T(8,128)(2,1)} %copy-done.6) | copy-start | bytes 196612
  59.7 12.8 %collective-permute-start.9 = (bf16[896,256]{1,0:T(8,128)(2,1)}, bf16[896,256]{1,0:T(8,128)(2,1)S(1)}, u32[]{:S(2)}, u32[]{:S(2)}) collective-permute-start(bf16[896,256]{1,0:T(8,128)(2,1)} %collective-permute-done.7.refs_6_), channel_id=1, source_target_pairs={{0,4},{4,0},{8,12},{12,8},{16,20},{20,16},{24,28},{28,24},{1,5},{5... | collective-permute-start | bytes 1376264 | tf_op jit(solution)/shard_map/ppermute | solution.py:21
  60.6 10.3 %collective-permute-start.6 = (bf16[256,896]{1,0:T(8,128)(2,1)S(1)}, bf16[256,896]{1,0:T(8,128)(2,1)S(1)}, u32[]{:S(2)}, u32[]{:S(2)}) collective-permute-start(bf16[256,896]{1,0:T(8,128)(2,1)S(1)} %collective-permute-done.5.refs_0_), channel_id=1, source_target_pairs={{0,2},{1,3},{2,0},{3,1},{4,6},{5,7},{6,4},{7,5},{8,10},{9,11},{10,... | collective-permute-start | bytes 1376264 | tf_op jit(solution)/shard_map/ppermute | solution.py:21
  63.2 10.4 %collective-permute-start.16 = (bf16[896,128]{1,0:T(8,128)(2,1)S(1)}, bf16[896,128]{1,0:T(8,128)(2,1)S(1)}, u32[]{:S(2)}, u32[]{:S(2)}) collective-permute-start(bf16[896,128]{1,0:T(8,128)(2,1)S(1)} %copy-done.4), channel_id=1, source_target_pairs={{0,24},{4,28},{8,16},{12,20},{16,8},{20,12},{24,0},{28,4},{1,25},{... | collective-permute-start | bytes 688136 | tf_op jit(solution)/shard_map/ppermute | solution.py:21
  65.3 17.2 %collective-permute-start.15 = (bf16[896,128]{1,0:T(8,128)(2,1)S(1)}, bf16[896,128]{1,0:T(8,128)(2,1)S(1)}, u32[]{:S(2)}, u32[]{:S(2)}) collective-permute-start(bf16[896,128]{1,0:T(8,128)(2,1)S(1)} %get-tuple-element.47.refs_3_), channel_id=1, source_target_pairs={{0,16},{4,20},{8,24},{12,28},{16,0},{20,4},{24,8},{28,12},{1,17},{... | collective-permute-start | bytes 688136 | tf_op jit(solution)/shard_map/ppermute | solution.py:21
  65.3 17.2 %collective-permute-start.17 = (bf16[896,128]{1,0:T(8,128)(2,1)S(1)}, bf16[896,128]{1,0:T(8,128)(2,1)S(1)}, u32[]{:S(2)}, u32[]{:S(2)}) collective-permute-start(bf16[896,128]{1,0:T(8,128)(2,1)S(1)} %copy-done.4), channel_id=1, source_target_pairs={{0,8},{4,12},{8,0},{12,4},{16,24},{20,28},{24,16},{28,20},{1,9},{5... | collective-permute-start | bytes 688136 | tf_op jit(solution)/shard_map/ppermute | solution.py:21
  70.9 12.9 %collective-permute-start.12 = (bf16[896,256]{1,0:T(8,128)(2,1)}, bf16[896,256]{1,0:T(8,128)(2,1)S(1)}, u32[]{:S(2)}, u32[]{:S(2)}) collective-permute-start(bf16[896,256]{1,0:T(8,128)(2,1)} %collective-permute-done.11.refs_4_), channel_id=1, source_target_pairs={{0,4},{4,0},{8,12},{12,8},{16,20},{20,16},{24,28},{28,24},{1,5},{5... | collective-permute-start | bytes 1376264 | tf_op jit(solution)/shard_map/ppermute | solution.py:21
  72.5 12.4 %copy-start.3 = (bf16[896,128]{1,0:T(8,128)(2,1)S(1)}, bf16[896,128]{1,0:T(8,128)(2,1)}, u32[]{:S(2)}) copy-start(bf16[896,128]{1,0:T(8,128)(2,1)} %copy-done.2) | copy-start | bytes 688132
  72.5 18.0 %collective-permute-start.10 = (bf16[512,896]{1,0:T(8,128)(2,1)S(1)}, bf16[512,896]{1,0:T(8,128)(2,1)S(1)}, u32[]{:S(2)}, u32[]{:S(2)}) collective-permute-start(bf16[512,896]{1,0:T(8,128)(2,1)S(1)} %pad_maximum_fusion), channel_id=1, source_target_pairs={{0,1},{1,0},{2,3},{3,2},{4,5},{5,4},{6,7},{7,6},{8,9},{9,8},{10,11... | collective-permute-start | bytes 2752520 | tf_op jit(solution)/shard_map/ppermute | solution.py:21
  82.6 15.1 %collective-permute-start.18 = (bf16[2688,128]{1,0:T(8,128)(2,1)S(1)}, bf16[2688,128]{1,0:T(8,128)(2,1)S(1)}, u32[]{:S(2)}, u32[]{:S(2)}) collective-permute-start(bf16[2688,128]{1,0:T(8,128)(2,1)S(1)} %pad_maximum_fusion.2), channel_id=1, source_target_pairs={{0,4},{4,0},{8,12},{12,8},{16,20},{20,16},{24,28},{28,24},{1,5},{5... | collective-permute-start | bytes 2064392 | tf_op jit(solution)/shard_map/ppermute | solution.py:21
  92.9 21.3 %collective-permute-start.25 = (bf16[512,256]{1,0:T(8,128)(2,1)S(1)}, bf16[512,256]{1,0:T(8,128)(2,1)S(1)}, u32[]{:S(2)}, u32[]{:S(2)}) collective-permute-start(bf16[512,256]{1,0:T(8,128)(2,1)S(1)} %shard_map.47.refs_0_.kv_ref), channel_id=1, source_target_pairs={{0,20},{4,16},{8,28},{12,24},{1,21},{5,17},{9,29},{13,25},{2,22},{... | collective-permute-start | bytes 786440 | tf_op jit(solution)/shard_map/ppermute | solution.py:21
  94.8 20.7 %collective-permute-start.24 = (bf16[512,256]{1,0:T(8,128)(2,1)S(1)}, bf16[512,256]{1,0:T(8,128)(2,1)S(1)}, u32[]{:S(2)}, u32[]{:S(2)}) collective-permute-start(bf16[512,256]{1,0:T(8,128)(2,1)S(1)} %shard_map.47.refs_0_.kv_ref), channel_id=1, source_target_pairs={{0,16},{4,20},{8,24},{12,28},{1,17},{5,21},{9,25},{13,29},{2,18},{... | collective-permute-start | bytes 786440 | tf_op jit(solution)/shard_map/ppermute | solution.py:21
  97.7 12.4 %collective-permute-start.20 = (bf16[512,128]{1,0:T(8,128)(2,1)S(1)}, bf16[512,128]{1,0:T(8,128)(2,1)S(1)}, u32[]{:S(2)}, u32[]{:S(2)}) collective-permute-start(bf16[512,128]{1,0:T(8,128)(2,1)S(1)} %pad_maximum_fusion.6.grad_ref.refs_2_), channel_id=1, source_target_pairs={{16,0},{20,4},{24,8},{28,12},{17,1},{21,5},{25,9},{29,13},{18,2},{... | collective-permute-start | bytes 393224 | tf_op jit(solution)/shard_map/ppermute | solution.py:21
  99.0 13.8 %collective-permute-start.19 = (bf16[512,128]{1,0:T(8,128)(2,1)S(1)}, bf16[512,128]{1,0:T(8,128)(2,1)S(1)}, u32[]{:S(2)}, u32[]{:S(2)}) collective-permute-start(bf16[512,128]{1,0:T(8,128)(2,1)S(1)} %pad_maximum_fusion.6.grad_ref.refs_2_), channel_id=1, source_target_pairs={{16,4},{20,0},{24,12},{28,8},{17,5},{21,1},{25,13},{29,9},{18,6},{... | collective-permute-start | bytes 393224 | tf_op jit(solution)/shard_map/ppermute | solution.py:21
  100.3 16.5 %collective-permute-start.23 = (bf16[512,256]{1,0:T(8,128)(2,1)S(1)}, bf16[512,256]{1,0:T(8,128)(2,1)S(1)}, u32[]{:S(2)}, u32[]{:S(2)}) collective-permute-start(bf16[512,256]{1,0:T(8,128)(2,1)S(1)} %shard_map.47.refs_0_.kv_ref), channel_id=1, source_target_pairs={{0,4},{4,0},{8,12},{12,8},{16,20},{20,16},{24,28},{28,24},{1,5},{5... | collective-permute-start | bytes 786440 | tf_op jit(solution)/shard_map/ppermute | solution.py:21
  110.1 11.3 %collective-permute-start.29 = (bf16[512,128]{1,0:T(8,128)(2,1)S(1)}, bf16[512,128]{1,0:T(8,128)(2,1)S(1)}, u32[]{:S(2)}, u32[]{:S(2)}) collective-permute-start(bf16[512,128]{1,0:T(8,128)(2,1)S(1)} %pad_maximum_fusion.6.grad_ref.refs_2_), channel_id=1, source_target_pairs={{0,4},{4,0},{8,12},{12,8},{16,20},{20,16},{24,28},{28,24},{1,5},{5... | collective-permute-start | bytes 393224 | tf_op jit(solution)/shard_map/ppermute | solution.py:21
  112.7 10.0 %collective-permute-start.28 = (bf16[512,128]{1,0:T(8,128)(2,1)S(1)}, bf16[512,128]{1,0:T(8,128)(2,1)S(1)}, u32[]{:S(2)}, u32[]{:S(2)}) collective-permute-start(bf16[512,128]{1,0:T(8,128)(2,1)S(1)} %shard_map.49.q_ref.refs_0_), channel_id=1, source_target_pairs={{0,4},{4,0},{8,12},{12,8},{16,20},{20,16},{24,28},{28,24},{1,5},{5... | collective-permute-start | bytes 393224 | tf_op jit(solution)/shard_map/ppermute | solution.py:21
  114.2 15.8 %collective-permute-start.22 = (bf16[512,128]{1,0:T(8,128)(2,1)S(1)}, bf16[512,128]{1,0:T(8,128)(2,1)S(1)}, u32[]{:S(2)}, u32[]{:S(2)}) collective-permute-start(bf16[512,128]{1,0:T(8,128)(2,1)S(1)} %shard_map.49.q_ref.refs_0_), channel_id=1, source_target_pairs={{16,4},{20,0},{24,12},{28,8},{17,5},{21,1},{25,13},{29,9},{18,6},{... | collective-permute-start | bytes 393224 | tf_op jit(solution)/shard_map/ppermute | solution.py:21
  115.5 14.5 %collective-permute-start.21 = (bf16[512,128]{1,0:T(8,128)(2,1)S(1)}, bf16[512,128]{1,0:T(8,128)(2,1)S(1)}, u32[]{:S(2)}, u32[]{:S(2)}) collective-permute-start(bf16[512,128]{1,0:T(8,128)(2,1)S(1)} %shard_map.49.q_ref.refs_0_), channel_id=1, source_target_pairs={{16,0},{20,4},{24,8},{28,12},{17,1},{21,5},{25,9},{29,13},{18,2},{... | collective-permute-start | bytes 393224 | tf_op jit(solution)/shard_map/ppermute | solution.py:21
  119.7 7.9 %collective-permute-start.30 = (f32[8,512]{1,0:T(8,128)S(1)}, f32[8,512]{1,0:T(8,128)S(1)}, u32[]{:S(2)}, u32[]{:S(2)}) collective-permute-start(f32[8,512]{1,0:T(8,128)S(1)} %get-tuple-element.57.refs_4_), channel_id=1, source_target_pairs={{0,4},{4,0},{8,12},{12,8},{16,20},{20,16},{24,28},{28,24},{1,5},{5... | collective-permute-start | bytes 49160 | tf_op jit(solution)/shard_map/ppermute | solution.py:21
  121.4 8.5 %collective-permute-start.27 = (f32[8,512]{1,0:T(8,128)S(1)}, f32[8,512]{1,0:T(8,128)S(1)}, u32[]{:S(2)}, u32[]{:S(2)}) collective-permute-start(f32[8,512]{1,0:T(8,128)S(1)} %get-tuple-element.57.refs_4_), channel_id=1, source_target_pairs={{16,4},{20,0},{24,12},{28,8},{17,5},{21,1},{25,13},{29,9},{18,6},{... | collective-permute-start | bytes 49160 | tf_op jit(solution)/shard_map/ppermute | solution.py:21
  122.7 7.2 %collective-permute-start.26 = (f32[8,512]{1,0:T(8,128)S(1)}, f32[8,512]{1,0:T(8,128)S(1)}, u32[]{:S(2)}, u32[]{:S(2)}) collective-permute-start(f32[8,512]{1,0:T(8,128)S(1)} %get-tuple-element.57.refs_4_), channel_id=1, source_target_pairs={{16,0},{20,4},{24,8},{28,12},{17,1},{21,5},{25,9},{29,13},{18,2},{... | collective-permute-start | bytes 49160 | tf_op jit(solution)/shard_map/ppermute | solution.py:21
  133.3 3.4 %collective-permute-start.38 = (bf16[256,896]{1,0:T(8,128)(2,1)S(1)}, bf16[256,896]{1,0:T(8,128)(2,1)S(1)}, u32[]{:S(2)}, u32[]{:S(2)}) collective-permute-start(bf16[256,896]{1,0:T(8,128)(2,1)S(1)} %convolution_convert_fusion.3), channel_id=1, source_target_pairs={{0,1},{1,0},{2,3},{3,2},{4,5},{5,4},{6,7},{7,6},{8,9},{9,8},{10,11... | collective-permute-start | bytes 1376264 | tf_op jit(solution)/shard_map/ppermute | solution.py:21
  133.4 4.4 %collective-permute-start.34 = (bf16[256,896]{1,0:T(8,128)(2,1)S(1)}, bf16[256,896]{1,0:T(8,128)(2,1)S(1)}, u32[]{:S(2)}, u32[]{:S(2)}) collective-permute-start(bf16[256,896]{1,0:T(8,128)(2,1)S(1)} %convolution_convert_fusion.4), channel_id=1, source_target_pairs={{0,1},{1,0},{2,3},{3,2},{4,5},{5,4},{6,7},{7,6},{8,9},{9,8},{10,11... | collective-permute-start | bytes 1376264 | tf_op jit(solution)/shard_map/ppermute | solution.py:21
  134.5 4.4 %collective-permute-start.32 = (bf16[256,1792]{1,0:T(8,128)(2,1)S(1)}, bf16[256,1792]{1,0:T(8,128)(2,1)S(1)}, u32[]{:S(2)}, u32[]{:S(2)}) collective-permute-start(bf16[256,1792]{1,0:T(8,128)(2,1)S(1)} %convolution_convert_fusion.1), channel_id=1, source_target_pairs={{0,1},{1,0},{2,3},{3,2},{4,5},{5,4},{6,7},{7,6},{8,9},{9,8},{10,11... | collective-permute-start | bytes 2752520 | tf_op jit(solution)/shard_map/ppermute | solution.py:21
  135.3 5.9 %collective-permute-start.37 = (bf16[256,1792]{1,0:T(8,128)(2,1)S(1)}, bf16[256,1792]{1,0:T(8,128)(2,1)S(1)}, u32[]{:S(2)}, u32[]{:S(2)}) collective-permute-start(bf16[256,1792]{1,0:T(8,128)(2,1)S(1)} %convolution_convert_fusion), channel_id=1, source_target_pairs={{0,1},{1,0},{2,3},{3,2},{4,5},{5,4},{6,7},{7,6},{8,9},{9,8},{10,11... | collective-permute-start | bytes 2752520 | tf_op jit(solution)/shard_map/ppermute | solution.py:21
  136.5 17.6 %collective-permute-start.31 = (bf16[256,1792]{1,0:T(8,128)(2,1)S(1)}, bf16[256,1792]{1,0:T(8,128)(2,1)S(1)}, u32[]{:S(2)}, u32[]{:S(2)}) collective-permute-start(bf16[256,1792]{1,0:T(8,128)(2,1)S(1)} %convolution_convert_fusion.2), channel_id=1, source_target_pairs={{0,1},{1,0},{2,3},{3,2},{4,5},{5,4},{6,7},{7,6},{8,9},{9,8},{10,11... | collective-permute-start | bytes 2752520 | tf_op jit(solution)/shard_map/ppermute | solution.py:21
  137.1 16.2 %collective-permute-start.39 = (bf16[256,896]{1,0:T(8,128)(2,1)S(1)}, bf16[256,896]{1,0:T(8,128)(2,1)S(1)}, u32[]{:S(2)}, u32[]{:S(2)}) collective-permute-start(bf16[256,896]{1,0:T(8,128)(2,1)S(1)} %fusion.7), channel_id=1, source_target_pairs={{0,2},{1,3},{2,0},{3,1},{4,6},{5,7},{6,4},{7,5},{8,10},{9,11},{10,... | collective-permute-start | bytes 1376264 | tf_op jit(solution)/shard_map/ppermute | solution.py:21
  138.3 13.4 %collective-permute-start.35 = (bf16[256,896]{1,0:T(8,128)(2,1)S(1)}, bf16[256,896]{1,0:T(8,128)(2,1)S(1)}, u32[]{:S(2)}, u32[]{:S(2)}) collective-permute-start(bf16[256,896]{1,0:T(8,128)(2,1)S(1)} %fusion.6), channel_id=1, source_target_pairs={{0,8},{4,12},{8,0},{12,4},{16,24},{20,28},{24,16},{28,20},{1,9},{5... | collective-permute-start | bytes 1376264 | tf_op jit(solution)/shard_map/ppermute | solution.py:21
  139.7 20.7 %collective-permute-start.33 = (bf16[256,896]{1,0:T(8,128)(2,1)S(1)}, bf16[256,896]{1,0:T(8,128)(2,1)S(1)}, u32[]{:S(2)}, u32[]{:S(2)}) collective-permute-start(bf16[256,896]{1,0:T(8,128)(2,1)S(1)} %slice.105), channel_id=1, source_target_pairs={{0,2},{1,3},{2,0},{3,1},{4,6},{5,7},{6,4},{7,5},{8,10},{9,11},{10,... | collective-permute-start | bytes 1376264 | tf_op jit(solution)/shard_map/ppermute | solution.py:21
  141.9 19.6 %collective-permute-start.41 = (bf16[256,896]{1,0:T(8,128)(2,1)S(1)}, bf16[256,896]{1,0:T(8,128)(2,1)S(1)}, u32[]{:S(2)}, u32[]{:S(2)}) collective-permute-start(bf16[256,896]{1,0:T(8,128)(2,1)S(1)} %slice.104), channel_id=1, source_target_pairs={{0,8},{4,12},{8,0},{12,4},{16,24},{20,28},{24,16},{28,20},{1,9},{5... | collective-permute-start | bytes 1376264 | tf_op jit(solution)/shard_map/ppermute | solution.py:21
  151.8 17.9 %collective-permute-start.36 = (bf16[256,896]{1,0:T(8,128)(2,1)S(1)}, bf16[256,896]{1,0:T(8,128)(2,1)S(1)}, u32[]{:S(2)}, u32[]{:S(2)}) collective-permute-start(bf16[256,896]{1,0:T(8,128)(2,1)S(1)} %fusion.9), channel_id=1, source_target_pairs={{0,2},{1,3},{2,0},{3,1},{4,6},{5,7},{6,4},{7,5},{8,10},{9,11},{10,... | collective-permute-start | bytes 1376264 | tf_op jit(solution)/shard_map/ppermute | solution.py:21
  153.4 17.2 %collective-permute-start.40 = (bf16[256,896]{1,0:T(8,128)(2,1)S(1)}, bf16[256,896]{1,0:T(8,128)(2,1)S(1)}, u32[]{:S(2)}, u32[]{:S(2)}) collective-permute-start(bf16[256,896]{1,0:T(8,128)(2,1)S(1)} %fusion.8), channel_id=1, source_target_pairs={{0,8},{4,12},{8,0},{12,4},{16,24},{20,28},{24,16},{28,20},{1,9},{5... | collective-permute-start | bytes 1376264 | tf_op jit(solution)/shard_map/ppermute | solution.py:21
  (2 other events, 6.4 us)

commit v4 on v3

--- a/solution.py
+++ b/solution.py
@@ -115,28 +115,25 @@
 
 def key_kernel(sets, run, limit_ref, kv_ref, *refs):
     q_refs, grad_refs, stat_refs = refs[:sets], refs[sets : 2 * sets], refs[2 * sets : 3 * sets]
-    before, out_ref = refs[3 * sets : -1], refs[-1]
+    before, (out_ref, total_ref) = refs[3 * sets : -2], refs[-2:]
     gap = -tile_gap(run, 0)
+    total_ref[...] = before[0][...] if before else jnp.zeros_like(total_ref)
     for half in range(2):
         rows = pl.ds(half * run, run)
-        keys, values = kv_ref[rows, :HD], kv_ref[rows, HD:]
-        dk = before[0][rows, :HD] if before else jnp.zeros((run, HD), F32)
-        dv = before[0][rows, HD:] if before else jnp.zeros((run, HD), F32)
         for j in range(sets):
-            q, grad, stat = q_refs[j][...], grad_refs[j][...], stat_refs[j]
-            scores = masked_scores(
-                dot_nt(keys, q),
-                gap,
-                [limit_ref[half, 2 * j], limit_ref[half, 2 * j + 1]],
-                run,
-            )
-            probs = jnp.exp(scores - stat[0:1, :]) * stat[1:2, :]
-            dprobs = dot_nt(values, grad)
-            dscores = (probs * (dprobs - stat[2:3, :])).astype(BF16)
-            dk += dot_nn(dscores, q) * (HD ** -0.5)
-            dv += dot_nn(probs.astype(BF16), grad)
-        out_ref[rows, :HD] = dk.astype(out_ref.dtype)
-        out_ref[rows, HD:] = dv.astype(out_ref.dtype)
+            limits = [limit_ref[half, 2 * j], limit_ref[half, 2 * j + 1]]
+
+            @pl.when(jnp.maximum(*limits) > -FAR)
+            def add(rows=rows, j=j, limits=limits):
+                q, grad, stat = q_refs[j][...], grad_refs[j][...], stat_refs[j]
+                scores = masked_scores(dot_nt(kv_ref[rows, :HD], q), gap, limits, run)
+                probs = jnp.exp(scores - stat[0:1, :]) * stat[1:2, :]
+                dprobs = dot_nt(kv_ref[rows, HD:], grad)
+                dscores = (probs * (dprobs - stat[2:3, :])).astype(BF16)
+                total_ref[rows, :HD] += dot_nn(dscores, q) * (HD ** -0.5)
+                total_ref[rows, HD:] += dot_nn(probs.astype(BF16), grad)
+
+    out_ref[...] = total_ref[...].astype(out_ref.dtype)
 
 
 def project_kernel(groups, n_pieces, place_ref, own_ref, *refs):
@@ -259,7 +256,8 @@
     start("gpair", order["gother"], PAIR)
     order.after("q0", "kv1")
     relay("q", 0)
-    order.after("kvother kv0 part_b", f"kv{far}", "a0", "gpair", "q1")
+    order.after("kvother kv0", f"kv{far}")
+    order.after("part_b", "a0", "gpair", "q1")
     groups_a = spread("a", [[0]])
     relay("kv", far, near)
     send("kv", *mids[1:])
@@ -269,34 +267,38 @@
     order["grad"] = jnp.concatenate([order["g0"], order["gpair"]], axis=0)
 
     order.after("q0 qother", f"kv{mids[1]}", f"kv{far ^ 1}")
+    order.after(f"kv{mids[1]}", f"kv{near ^ 1}")
     relay("kv", *mids[1:])
     groups_b = spread("b", [[0]])
     send("q", *mids)
-    order.after("qother", f"a{len(groups_a) - 1}")
+    order["kv_even"] = project("kv", even, "a", groups_a)
+    order.after("qother", "kv_even")
     send("q", near)
-    order["kv_even"] = project("kv", even, "a", groups_a)
     order.after("b0 b1", *[f"kv{d ^ 1}" for d in mids[1:]])
     for _ in bits[1:]:
         groups_b = spread("b", groups_b)
     last = ("b", groups_b) if per_f > depth else ("a", groups_a)
     order["kv"] = project("kv", odd, *last, order["kv_even"])
 
+    moved = mids + [near]
+    start("passed", jnp.concatenate([order[f"q{d}"] for d in moved], axis=0), 1)
     for d in others[:-1]:
         start(f"keys{d}", order["kv"], d, to_later)
-    moved = mids + [near]
-    start("passed", jnp.concatenate([order[f"q{d}"] for d in moved], axis=0), 1)
-    order.after("kv", "passed")
+    order.after("grad", "kv")
+    for d in others[:-1]:
+        start(f"grad{d}", order["grad"], d, to_earlier)
+    order.after("kv grad", "passed", *[f"grad{d}" for d in others[:-1]])
     start(f"keys{others[-1]}", order["kv"], others[-1], to_later)
     for i, d in enumerate(moved):
         order[f"q{d ^ 1}"] = order["passed"][i * depth : (i + 1) * depth]
+    order.after("q0", *[f"grad{d}" for d in others[:-1]])
     order["q_even"] = project("q", even, "a", groups_a)
-    order.after("grad", "kv")
-    for d in others:
-        start(f"grad{d}", order["grad"], d, to_earlier)
     order["q"] = project("q", odd, *last, order["q_even"])
     order.after("q", *[f"grad{d}" for d in others[:-1]])
-    for d in others:
+    for d in others[:-1]:
         start(f"query{d}", order["q"], d, to_earlier)
+    start("both", jnp.concatenate([order["q"], order["grad"]], axis=1), others[-1])
+    order[f"query{others[-1]}"], order[f"grad{others[-1]}"] = order["both"][:, :HD], order["both"][:, HD:]
     kv, q, grad = order["kv"], order["q"], order["grad"]
     kv_pieces = {d: order[f"kv{d}"] for d in range(n_ctx)}
     q_pieces = {d: order[f"q{d}"] for d in range(n_ctx)}
@@ -327,7 +329,8 @@
         ),
         2 + sets,
     )(query_limits, q, grad, *kvs)
-    stats = [stat] + [to_earlier(stat, distance=d) for d in group[1:]]
+    moved_stats = {d: to_earlier(stat, distance=d) for d in others}
+    stats = [stat] + [moved_stats[d] for d in group[1:]]
     dq = local_call(
         functools.partial(query_kernel, sets, run),
         jax.ShapeDtypeStruct((2 * run, HD), BF16),
@@ -338,11 +341,13 @@
         functools.partial(key_kernel, close, run),
         jax.ShapeDtypeStruct((2 * run, 2 * HD), F32),
         1 + 3 * close,
+        [pltpu.VMEM((2 * run, 2 * HD), F32)],
     )(key_limits[:, : 2 * close], kv, *qs[:close], *grads[:close], *stats[:close])
     dkv = local_call(
         functools.partial(key_kernel, sets - close, run),
         jax.ShapeDtypeStruct((2 * run, 2 * HD), BF16),
         2 + 3 * (sets - close),
+        [pltpu.VMEM((2 * run, 2 * HD), F32)],
     )(key_limits[:, 2 * close :], kv, *qs[close:], *grads[close:], *stats[close:], dkv)
 
     all_grads = jnp.concatenate([dkv, dq], axis=1)

time: 172 us -> 169 us (0.983)
  local copies, waits for them, and re-layouts: 10.5 us -> 6.58 us
  starting transfers between devices: 47.9 us -> 50.4 us
    unnamed x30 -> x20, local copies, waits for them, and re-layouts: 4.53 us -> 0.45 us
    ppermute x42 -> x41, starting transfers between devices: 47.9 us -> 50.4 us  [swap(): return lax.ppermute(array, axis, pairs)]
    ppermute x42 -> x41, waiting for transfers between devices: 83.1 us -> 81.5 us  [swap(): return lax.ppermute(array, axis, pairs)]
  transfers between devices with their start and end apart: 42 -> 41, of which waited for: 17 -> 15; matrix products, arithmetic and copies ran while one was open for 10% -> 8% of each run, Pallas kernels for 10% -> 10%
where the time goes in v4:
time: 169 us
  waiting for transfers between devices  81.5 us (48%)
  starting transfers between devices  50.4 us (30%)
  Pallas kernels  20.7 us (12%)
  local copies, waits for them, and re-layouts  6.58 us (4%)
  matrix products  5.88 us (3%)
  other arithmetic  3.08 us (2%)
    ppermute x41, waiting for transfers between devices, swap(): return lax.ppermute(array, axis, pairs)  81.5 us
    ppermute x41, starting transfers between devices, swap(): return lax.ppermute(array, axis, pairs)  50.4 us
    pallas_call x4, Pallas kernels, project(): local_call(functools.partial(project_kernel, groups, len(ds)), out, 1 + l...  7.4 us
    dot_general x10, matrix products, dot_nt(): lax.dot_general(a, b, (((1,), (1,)), ((), ())), preferred_element_type=F32)  5.88 us
  transfers between devices with their start and end apart: 41, of which 15 were waited for; matrix products, arithmetic and copies ran while one was open for 8% of the time, Pallas kernels for 10%

profile of v4, /device:TPU:0, one launch (start us, length us, event | category | flops | bytes accessed | tf_op | source)
XLA Modules:
  0.0 168.8 jit_solution(16774056438024152287)
XLA Ops:
  0.0 1.4 fusion.37
  1.7 4.1 %collective-permute-start.6 = (bf16[896,256]{1,0:T(8,128)(2,1)S(1)}, bf16[896,256]{1,0:T(8,128)(2,1)S(1)}, u32[]{:S(2)}, u32[]{:S(2)}) collective-permute-start(bf16[896,256]{1,0:T(8,128)(2,1)S(1)} %pad_maximum_fusion.3.refs_3_), channel_id=1, source_target_pairs={{0,16},{4,20},{8,24},{12,28},{16,0},{20,4},{24,8},{28,12},{1,17},{... | collective-permute-start | bytes 1376264 | tf_op jit(solution)/shard_map/ppermute | solution.py:21
  5.8 1.5 collective-permute-start.2
  7.9 1.6 collective-permute-start.1
  9.5 2.2 %constant_dynamic-slice_fusion.1 = (bf16[256,896]{1,0:T(8,128)(2,1)}, bf16[256,896]{1,0:T(8,128)(2,1)}) fusion(bf16[256,7168]{1,0:T(8,128)(2,1)} %own_ref.7, s32[]{:T(128)S(6)} %select_n.158, s32[]{:T(128)S(6)} %select_n.157), kind=kLoop, calls=%fused_computation.84 | loop fusion | bytes 1835016 | tf_op jit(solution)/shard_map/dynamic_slice | solution.py:202
  13.0 1.6 collective-permute-start.9
  14.8 2.9 %collective-permute-done.2.refs_3_ = bf16[896,256]{1,0:T(8,128)(2,1)S(1)} collective-permute-done((bf16[896,256]{1,0:T(8,128)(2,1)S(1)}, bf16[896,256]{1,0:T(8,128)(2,1)S(1)}, u32[]{:S(2)}, u32[]{:S(2)}) %collective-permute-start.2) | collective-permute-done | bytes 458784 | tf_op jit(solution)/shard_map/ppermute | solution.py:21
  17.7 1.5 collective-permute-start.3
  19.4 14.6 %collective-permute-done.refs_0_ = bf16[256,896]{1,0:T(8,128)(2,1)S(1)} collective-permute-done((bf16[256,896]{1,0:T(8,128)(2,1)}, bf16[256,896]{1,0:T(8,128)(2,1)S(1)}, u32[]{:S(2)}, u32[]{:S(2)}) %collective-permute-start) | collective-permute-done | bytes 458784 | tf_op jit(solution)/shard_map/ppermute | solution.py:21
  34.0 1.5 collective-permute-start.13
  37.1 1.3 collective-permute-start.7
  38.9 12.7 %collective-permute-done.9.refs_4_ = bf16[896,256]{1,0:T(8,128)(2,1)S(1)} collective-permute-done((bf16[896,256]{1,0:T(8,128)(2,1)}, bf16[896,256]{1,0:T(8,128)(2,1)S(1)}, u32[]{:S(2)}, u32[]{:S(2)}) %collective-permute-start.9) | collective-permute-done | bytes 458784 | tf_op jit(solution)/shard_map/ppermute | solution.py:21
  52.6 9.7 %collective-permute-done.10.refs_4_ = bf16[896,256]{1,0:T(8,128)(2,1)S(1)} collective-permute-done((bf16[896,256]{1,0:T(8,128)(2,1)S(1)}, bf16[896,256]{1,0:T(8,128)(2,1)S(1)}, u32[]{:S(2)}, u32[]{:S(2)}) %collective-permute-start.10) | collective-permute-done | bytes 458784 | tf_op jit(solution)/shard_map/ppermute | solution.py:21
  62.9 1.5 collective-permute-start.5
  64.5 1.1 collective-permute-start.16
  66.1 5.9 %collective-permute-done.11.refs_6_ = bf16[896,256]{1,0:T(8,128)(2,1)S(1)} collective-permute-done((bf16[896,256]{1,0:T(8,128)(2,1)S(1)}, bf16[896,256]{1,0:T(8,128)(2,1)S(1)}, u32[]{:S(2)}, u32[]{:S(2)}) %collective-permute-start.11) | collective-permute-done | bytes 458784 | tf_op jit(solution)/shard_map/ppermute | solution.py:21
  72.0 1.9 %shard_map.46.refs_7_ = f32[512,256]{1,0:T(8,128)S(1)} custom-call(s32[2,4]{1,0:T(2,128)S(1)} %pad_add_fusion.1.place_ref, bf16[256,7168]{1,0:T(8,128)(2,1)S(1)} %copy-done.1, bf16[256,896]{1,0:T(8,128)(2,1)S(1)} %collective-permute-done.refs_0_, bf16[256,896]{1,0:T(8,128)(2,1)S(1)} %collective-permute-done.13.refs_1_, ...), custom_call_target="tpu_custom_call" | custom-call | flops 1 | bytes 1 | tf_op jit(solution)/shard_map/pallas_call | solution.py:228
  74.7 8.6 %collective-permute-done.15.refs_5_ = bf16[896,128]{1,0:T(8,128)(2,1)S(1)} collective-permute-done((bf16[896,128]{1,0:T(8,128)(2,1)S(1)}, bf16[896,128]{1,0:T(8,128)(2,1)S(1)}, u32[]{:S(2)}, u32[]{:S(2)}) %collective-permute-start.15) | collective-permute-done | bytes 229408 | tf_op jit(solution)/shard_map/ppermute | solution.py:21
  84.2 1.6 collective-permute-start.18
  86.8 1.9 %shard_map.47.refs_0_.kv_ref = bf16[512,256]{1,0:T(8,128)(2,1)S(1)} custom-call(s32[2,4]{1,0:T(2,128)S(1)} %pad_add_fusion.place_ref, bf16[256,7168]{1,0:T(8,128)(2,1)S(1)} %copy-done.1, bf16[256,896]{1,0:T(8,128)(2,1)S(1)} %collective-permute-done.4.refs_0_, bf16[256,896]{1,0:T(8,128)(2,1)S(1)} %collective-permute-done.5.refs_1_, ...), custom_call_target="tpu_custom_call" | custom-call | flops 1 | bytes 1 | tf_op jit(solution)/shard_map/pallas_call | solution.py:228
  88.7 1.3 collective-permute-start.20
  90.0 1.3 collective-permute-start.19
  91.4 6.4 %collective-permute-start.25 = (bf16[512,256]{1,0:T(8,128)(2,1)S(1)}, bf16[512,256]{1,0:T(8,128)(2,1)S(1)}, u32[]{:S(2)}, u32[]{:S(2)}) collective-permute-start(bf16[512,256]{1,0:T(8,128)(2,1)S(1)} %shard_map.47.refs_0_.kv_ref), channel_id=1, source_target_pairs={{0,20},{4,16},{8,28},{12,24},{1,21},{5,17},{9,29},{13,25},{2,22},{... | collective-permute-start | bytes 786440 | tf_op jit(solution)/shard_map/ppermute | solution.py:21
  97.7 1.3 collective-permute-start.24
  99.1 1.7 collective-permute-done.19.refs_3_
  100.7 1.0 collective-permute-done.18
  101.8 2.4 %collective-permute-start.23 = (bf16[512,256]{1,0:T(8,128)(2,1)S(1)}, bf16[512,256]{1,0:T(8,128)(2,1)S(1)}, u32[]{:S(2)}, u32[]{:S(2)}) collective-permute-start(bf16[512,256]{1,0:T(8,128)(2,1)S(1)} %shard_map.47.refs_0_.kv_ref), channel_id=1, source_target_pairs={{0,4},{4,0},{8,12},{12,8},{16,20},{20,16},{24,28},{28,24},{1,5},{5... | collective-permute-start | bytes 786440 | tf_op jit(solution)/shard_map/ppermute | solution.py:21
  104.5 1.8 %shard_map.48.refs_7_ = f32[512,128]{1,0:T(8,128)S(1)} custom-call(s32[2,4]{1,0:T(2,128)S(1)} %pad_add_fusion.1.place_ref, bf16[256,7168]{1,0:T(8,128)(2,1)S(1)} %copy-done.1, bf16[256,896]{1,0:T(8,128)(2,1)S(1)} %collective-permute-done.refs_0_, bf16[256,896]{1,0:T(8,128)(2,1)S(1)} %collective-permute-done.13.refs_1_, ...), custom_call_target="tpu_custom_call" | custom-call | flops 1 | bytes 1 | tf_op jit(solution)/shard_map/pallas_call | solution.py:228
  106.3 1.8 %shard_map.49.q_ref.refs_0_ = bf16[512,128]{1,0:T(8,128)(2,1)S(1)} custom-call(s32[2,4]{1,0:T(2,128)S(1)} %pad_add_fusion.place_ref, bf16[256,7168]{1,0:T(8,128)(2,1)S(1)} %copy-done.1, bf16[256,896]{1,0:T(8,128)(2,1)S(1)} %collective-permute-done.4.refs_0_, bf16[256,896]{1,0:T(8,128)(2,1)S(1)} %collective-permute-done.5.refs_1_, ...), custom_call_target="tpu_custom_call" | custom-call | flops 1 | bytes 1 | tf_op jit(solution)/shard_map/pallas_call | solution.py:228
  108.1 1.3 collective-permute-start.22
  109.7 1.3 collective-permute-start.21
  111.7 2.9 %shard_map.50 = (f32[8,512]{1,0:T(8,128)S(1)}, f32[512,128]{1,0:T(8,128)S(1)}) custom-call(s32[2,8]{1,0:T(2,128)S(1)} %get-tuple-element.98.limit_ref, bf16[512,128]{1,0:T(8,128)(2,1)S(1)} %shard_map.49.q_ref.refs_0_, bf16[512,128]{1,0:T(8,128)(2,1)S(1)} %pad_maximum_fusion.7.grad_ref.refs_2_, bf16[512,256]{1,0:T(8,128)(2,1)S(1)} %shard_map.47.refs_0_.kv_ref, ...), custom_call_target="tpu_custom_call" | custom-call | flops 1 | bytes 1 | tf_op jit(solution)/shard_map/pallas_call | solution.py:324
  114.7 2.5 %collective-permute-start.29 = (f32[8,512]{1,0:T(8,128)S(1)}, f32[8,512]{1,0:T(8,128)S(1)}, u32[]{:S(2)}, u32[]{:S(2)}) collective-permute-start(f32[8,512]{1,0:T(8,128)S(1)} %get-tuple-element.73.refs_4_), channel_id=1, source_target_pairs={{0,4},{4,0},{8,12},{12,8},{16,20},{20,16},{24,28},{28,24},{1,5},{5... | collective-permute-start | bytes 49160 | tf_op jit(solution)/shard_map/ppermute | solution.py:21
  117.2 1.3 collective-permute-start.27
  118.5 1.5 collective-permute-start.26
  120.0 3.2 %shard_map.53 = bf16[512,128]{1,0:T(8,128)(2,1)S(1)} custom-call(s32[2,8]{1,0:T(2,128)S(1)} %get-tuple-element.98.limit_ref, bf16[512,128]{1,0:T(8,128)(2,1)S(1)} %shard_map.49.q_ref.refs_0_, bf16[512,128]{1,0:T(8,128)(2,1)S(1)} %pad_maximum_fusion.7.grad_ref.refs_2_, f32[512,128]{1,0:T(8,128)S(1)} %get-tuple-element.74.column_ref, ...), custom_call_target="tpu_custom_call" | custom-call | flops 1 | bytes 1 | tf_op jit(solution)/shard_map/pallas_call | solution.py:334
  123.2 2.8 %shard_map.51.refs_6_ = f32[512,256]{1,0:T(8,128)S(1)} custom-call(s32[2,4]{1,0:T(2,128)S(1)} %get-tuple-element.96.limit_ref, bf16[512,256]{1,0:T(8,128)(2,1)S(1)} %shard_map.47.refs_0_.kv_ref, bf16[512,128]{1,0:T(8,128)(2,1)S(1)} %shard_map.49.q_ref.refs_0_, bf16[512,128]{1,0:T(8,128)(2,1)S(1)} %get-tuple-element.93.refs_1_, ...), custom_call_target="tpu_custom_call" | custom-call | flops 1 | bytes 1 | tf_op jit(solution)/shard_map/pallas_call | solution.py:340
  126.1 3.1 %shard_map.52 = bf16[512,256]{1,0:T(8,128)(2,1)S(1)} custom-call(s32[2,4]{1,0:T(2,128)S(1)} %get-tuple-element.97.limit_ref, bf16[512,256]{1,0:T(8,128)(2,1)S(1)} %shard_map.47.refs_0_.kv_ref, bf16[512,128]{1,0:T(8,128)(2,1)S(1)} %collective-permute-done.21.refs_0_, bf16[512,128]{1,0:T(8,128)(2,1)S(1)} %collective-permute-done.22.refs_1_, ...), custom_call_target="tpu_custom_call" | custom-call | flops 1 | bytes 1 | tf_op jit(solution)/shard_map/pallas_call | solution.py:346
  134.8 2.4 %collective-permute-start.34 = (bf16[256,896]{1,0:T(8,128)(2,1)S(1)}, bf16[256,896]{1,0:T(8,128)(2,1)S(1)}, u32[]{:S(2)}, u32[]{:S(2)}) collective-permute-start(bf16[256,896]{1,0:T(8,128)(2,1)S(1)} %fusion.6), channel_id=1, source_target_pairs={{0,8},{4,12},{8,0},{12,4},{16,24},{20,28},{24,16},{28,20},{1,9},{5... | collective-permute-start | bytes 1376264 | tf_op jit(solution)/shard_map/ppermute | solution.py:21
  137.8 1.6 collective-permute-start.32
  140.3 8.1 %collective-permute-done.34 = bf16[256,896]{1,0:T(8,128)(2,1)S(1)} collective-permute-done((bf16[256,896]{1,0:T(8,128)(2,1)S(1)}, bf16[256,896]{1,0:T(8,128)(2,1)S(1)}, u32[]{:S(2)}, u32[]{:S(2)}) %collective-permute-start.34) | collective-permute-done | bytes 458784 | tf_op jit(solution)/shard_map/ppermute | solution.py:21
  148.5 1.7 %collective-permute-start.35 = (bf16[256,896]{1,0:T(8,128)(2,1)S(1)}, bf16[256,896]{1,0:T(8,128)(2,1)S(1)}, u32[]{:S(2)}, u32[]{:S(2)}) collective-permute-start(bf16[256,896]{1,0:T(8,128)(2,1)S(1)} %fusion.9), channel_id=1, source_target_pairs={{0,2},{1,3},{2,0},{3,1},{4,6},{5,7},{6,4},{7,5},{8,10},{9,11},{10,... | collective-permute-start | bytes 1376264 | tf_op jit(solution)/shard_map/ppermute | solution.py:21
  150.3 2.0 %collective-permute-start.39 = (bf16[256,896]{1,0:T(8,128)(2,1)S(1)}, bf16[256,896]{1,0:T(8,128)(2,1)S(1)}, u32[]{:S(2)}, u32[]{:S(2)}) collective-permute-start(bf16[256,896]{1,0:T(8,128)(2,1)S(1)} %fusion.8), channel_id=1, source_target_pairs={{0,8},{4,12},{8,0},{12,4},{16,24},{20,28},{24,16},{28,20},{1,9},{5... | collective-permute-start | bytes 1376264 | tf_op jit(solution)/shard_map/ppermute | solution.py:21
  153.0 4.3 %collective-permute-done.32.x_a = bf16[256,896]{1,0:T(8,128)(2,1)S(1)} collective-permute-done((bf16[256,896]{1,0:T(8,128)(2,1)S(1)}, bf16[256,896]{1,0:T(8,128)(2,1)S(1)}, u32[]{:S(2)}, u32[]{:S(2)}) %collective-permute-start.32) | collective-permute-done | bytes 458784 | tf_op jit(solution)/shard_map/ppermute | solution.py:21
  157.3 1.0 collective-permute-done.40.z_b
  158.2 8.4 %collective-permute-done.35.x_b = bf16[256,896]{1,0:T(8,128)(2,1)S(1)} collective-permute-done((bf16[256,896]{1,0:T(8,128)(2,1)S(1)}, bf16[256,896]{1,0:T(8,128)(2,1)S(1)}, u32[]{:S(2)}, u32[]{:S(2)}) %collective-permute-start.35) | collective-permute-done | bytes 458784 | tf_op jit(solution)/shard_map/ppermute | solution.py:21
  166.7 1.0 collective-permute-done.39.z_a
  167.6 1.2 shard_map.54
  (115 shorter events, 18.6 us)
Async XLA Ops:
  0.0 35.7 %copy-start = (s32[4,4]{1,0:T(4,128)S(1)}, s32[4,4]{1,0:T(4,128)}, u32[]{:S(2)}) copy-start(s32[4,4]{1,0:T(4,128)} %param.6) | copy-start | bytes 196
  1.4 5.9 %copy-start.2 = (bf16[256,256]{1,0:T(8,128)(2,1)S(1)}, bf16[256,256]{1,0:T(8,128)(2,1)}, u32[]{:S(2)}) copy-start(bf16[256,256]{1,0:T(8,128)(2,1)} %param.7) | copy-start | bytes 393220
  1.7 35.4 %collective-permute-start.6 = (bf16[896,256]{1,0:T(8,128)(2,1)S(1)}, bf16[896,256]{1,0:T(8,128)(2,1)S(1)}, u32[]{:S(2)}, u32[]{:S(2)}) collective-permute-start(bf16[896,256]{1,0:T(8,128)(2,1)S(1)} %pad_maximum_fusion.3.refs_3_), channel_id=1, source_target_pairs={{0,16},{4,20},{8,24},{12,28},{16,0},{20,4},{24,8},{28,12},{1,17},{... | collective-permute-start | bytes 1376264 | tf_op jit(solution)/shard_map/ppermute | solution.py:21
  5.8 12.0 %collective-permute-start.2 = (bf16[896,256]{1,0:T(8,128)(2,1)S(1)}, bf16[896,256]{1,0:T(8,128)(2,1)S(1)}, u32[]{:S(2)}, u32[]{:S(2)}) collective-permute-start(bf16[896,256]{1,0:T(8,128)(2,1)S(1)} %pad_maximum_fusion.3.refs_3_), channel_id=1, source_target_pairs={{0,4},{4,0},{8,12},{12,8},{16,20},{20,16},{24,28},{28,24},{1,5},{5... | collective-permute-start | bytes 1376264 | tf_op jit(solution)/shard_map/ppermute | solution.py:21
  7.9 11.5 %collective-permute-start.1 = (bf16[256,128]{1,0:T(8,128)(2,1)}, bf16[256,128]{1,0:T(8,128)(2,1)}, u32[]{:S(2)}, u32[]{:S(2)}) collective-permute-start(bf16[256,128]{1,0:T(8,128)(2,1)} %get-tuple-element.95), channel_id=1, source_target_pairs={{0,8},{4,12},{8,0},{12,4},{16,24},{20,28},{24,16},{28,20},{1,9},{5... | collective-permute-start | bytes 196616 | tf_op jit(solution)/shard_map/ppermute | solution.py:21
  11.7 22.3 %collective-permute-start = (bf16[256,896]{1,0:T(8,128)(2,1)}, bf16[256,896]{1,0:T(8,128)(2,1)S(1)}, u32[]{:S(2)}, u32[]{:S(2)}) collective-permute-start(bf16[256,896]{1,0:T(8,128)(2,1)} %get-tuple-element.75), channel_id=1, source_target_pairs={{0,8},{4,12},{8,0},{12,4},{16,24},{20,28},{24,16},{28,20},{1,9},{5... | collective-permute-start | bytes 1376264 | tf_op jit(solution)/shard_map/ppermute | solution.py:21
  13.0 38.7 %collective-permute-start.9 = (bf16[896,256]{1,0:T(8,128)(2,1)}, bf16[896,256]{1,0:T(8,128)(2,1)S(1)}, u32[]{:S(2)}, u32[]{:S(2)}) collective-permute-start(bf16[896,256]{1,0:T(8,128)(2,1)} %pad_maximum_fusion.4), channel_id=1, source_target_pairs={{0,8},{4,12},{8,0},{12,4},{16,24},{20,28},{24,16},{28,20},{1,9},{5... | collective-permute-start | bytes 1376264 | tf_op jit(solution)/shard_map/ppermute | solution.py:21
  17.7 16.3 %collective-permute-start.3 = (bf16[896,128]{1,0:T(8,128)(2,1)S(1)}, bf16[896,128]{1,0:T(8,128)(2,1)S(1)}, u32[]{:S(2)}, u32[]{:S(2)}) collective-permute-start(bf16[896,128]{1,0:T(8,128)(2,1)S(1)} %get-tuple-element.66.refs_3_), channel_id=1, source_target_pairs={{0,4},{4,0},{8,12},{12,8},{16,20},{20,16},{24,28},{28,24},{1,5},{5... | collective-permute-start | bytes 688136 | tf_op jit(solution)/shard_map/ppermute | solution.py:21
  34.0 18.2 %collective-permute-start.13 = (bf16[256,896]{1,0:T(8,128)(2,1)S(1)}, bf16[256,896]{1,0:T(8,128)(2,1)S(1)}, u32[]{:S(2)}, u32[]{:S(2)}) collective-permute-start(bf16[256,896]{1,0:T(8,128)(2,1)S(1)} %collective-permute-done.refs_0_), channel_id=1, source_target_pairs={{0,2},{1,3},{2,0},{3,1},{4,6},{5,7},{6,4},{7,5},{8,10},{9,11},{10,... | collective-permute-start | bytes 1376264 | tf_op jit(solution)/shard_map/ppermute | solution.py:21
  37.1 34.9 %copy-start.1 = (bf16[256,7168]{1,0:T(8,128)(2,1)S(1)}, bf16[256,7168]{1,0:T(8,128)(2,1)}, u32[]{:S(2)}) copy-start(bf16[256,7168]{1,0:T(8,128)(2,1)} %own_ref.7) | copy-start | bytes 11010052
  37.1 15.5 %collective-permute-start.7 = (bf16[896,256]{1,0:T(8,128)(2,1)}, bf16[896,256]{1,0:T(8,128)(2,1)S(1)}, u32[]{:S(2)}, u32[]{:S(2)}) collective-permute-start(bf16[896,256]{1,0:T(8,128)(2,1)} %pad_maximum_fusion.4), channel_id=1, source_target_pairs={{0,24},{4,28},{8,16},{12,20},{16,8},{20,12},{24,0},{28,4},{1,25},{... | collective-permute-start | bytes 1376264 | tf_op jit(solution)/shard_map/ppermute | solution.py:21
  38.4 14.2 %collective-permute-start.8 = (bf16[896,256]{1,0:T(8,128)(2,1)S(1)}, bf16[896,256]{1,0:T(8,128)(2,1)S(1)}, u32[]{:S(2)}, u32[]{:S(2)}) collective-permute-start(bf16[896,256]{1,0:T(8,128)(2,1)S(1)} %collective-permute-done.6.refs_5_), channel_id=1, source_target_pairs={{0,4},{4,0},{8,12},{12,8},{16,20},{20,16},{24,28},{28,24},{1,5},{5... | collective-permute-start | bytes 1376264 | tf_op jit(solution)/shard_map/ppermute | solution.py:21
  51.6 10.7 %collective-permute-start.10 = (bf16[896,256]{1,0:T(8,128)(2,1)S(1)}, bf16[896,256]{1,0:T(8,128)(2,1)S(1)}, u32[]{:S(2)}, u32[]{:S(2)}) collective-permute-start(bf16[896,256]{1,0:T(8,128)(2,1)S(1)} %collective-permute-done.9.refs_4_), channel_id=1, source_target_pairs={{0,4},{4,0},{8,12},{12,8},{16,20},{20,16},{24,28},{28,24},{1,5},{5... | collective-permute-start | bytes 1376264 | tf_op jit(solution)/shard_map/ppermute | solution.py:21
  52.2 10.7 %collective-permute-start.4 = (bf16[256,896]{1,0:T(8,128)(2,1)}, bf16[256,896]{1,0:T(8,128)(2,1)S(1)}, u32[]{:S(2)}, u32[]{:S(2)}) collective-permute-start(bf16[256,896]{1,0:T(8,128)(2,1)} %get-tuple-element.42), channel_id=1, source_target_pairs={{0,8},{4,12},{8,0},{12,4},{16,24},{20,28},{24,16},{28,20},{1,9},{5... | collective-permute-start | bytes 1376264 | tf_op jit(solution)/shard_map/ppermute | solution.py:21
  52.3 19.7 %collective-permute-start.14 = (bf16[512,896]{1,0:T(8,128)(2,1)S(1)}, bf16[512,896]{1,0:T(8,128)(2,1)S(1)}, u32[]{:S(2)}, u32[]{:S(2)}) collective-permute-start(bf16[512,896]{1,0:T(8,128)(2,1)S(1)} %pad_maximum_fusion.1), channel_id=1, source_target_pairs={{0,1},{1,0},{2,3},{3,2},{4,5},{5,4},{6,7},{7,6},{8,9},{9,8},{10,11... | collective-permute-start | bytes 2752520 | tf_op jit(solution)/shard_map/ppermute | solution.py:21
  62.3 9.6 %collective-permute-start.11 = (bf16[896,256]{1,0:T(8,128)(2,1)S(1)}, bf16[896,256]{1,0:T(8,128)(2,1)S(1)}, u32[]{:S(2)}, u32[]{:S(2)}) collective-permute-start(bf16[896,256]{1,0:T(8,128)(2,1)S(1)} %collective-permute-done.7.refs_6_), channel_id=1, source_target_pairs={{0,4},{4,0},{8,12},{12,8},{16,20},{20,16},{24,28},{28,24},{1,5},{5... | collective-permute-start | bytes 1376264 | tf_op jit(solution)/shard_map/ppermute | solution.py:21
  62.9 9.1 %collective-permute-start.5 = (bf16[256,896]{1,0:T(8,128)(2,1)S(1)}, bf16[256,896]{1,0:T(8,128)(2,1)S(1)}, u32[]{:S(2)}, u32[]{:S(2)}) collective-permute-start(bf16[256,896]{1,0:T(8,128)(2,1)S(1)} %collective-permute-done.4.refs_0_), channel_id=1, source_target_pairs={{0,2},{1,3},{2,0},{3,1},{4,6},{5,7},{6,4},{7,5},{8,10},{9,11},{10,... | collective-permute-start | bytes 1376264 | tf_op jit(solution)/shard_map/ppermute | solution.py:21
  64.5 10.1 %collective-permute-start.16 = (bf16[896,128]{1,0:T(8,128)(2,1)S(1)}, bf16[896,128]{1,0:T(8,128)(2,1)S(1)}, u32[]{:S(2)}, u32[]{:S(2)}) collective-permute-start(bf16[896,128]{1,0:T(8,128)(2,1)S(1)} %get-tuple-element.60), channel_id=1, source_target_pairs={{0,24},{4,28},{8,16},{12,20},{16,8},{20,12},{24,0},{28,4},{1,25},{... | collective-permute-start | bytes 688136 | tf_op jit(solution)/shard_map/ppermute | solution.py:21
  65.7 17.6 %collective-permute-start.15 = (bf16[896,128]{1,0:T(8,128)(2,1)S(1)}, bf16[896,128]{1,0:T(8,128)(2,1)S(1)}, u32[]{:S(2)}, u32[]{:S(2)}) collective-permute-start(bf16[896,128]{1,0:T(8,128)(2,1)S(1)} %get-tuple-element.66.refs_3_), channel_id=1, source_target_pairs={{0,16},{4,20},{8,24},{12,28},{16,0},{20,4},{24,8},{28,12},{1,17},{... | collective-permute-start | bytes 688136 | tf_op jit(solution)/shard_map/ppermute | solution.py:21
  73.9 10.3 %collective-permute-start.17 = (bf16[896,128]{1,0:T(8,128)(2,1)S(1)}, bf16[896,128]{1,0:T(8,128)(2,1)S(1)}, u32[]{:S(2)}, u32[]{:S(2)}) collective-permute-start(bf16[896,128]{1,0:T(8,128)(2,1)S(1)} %get-tuple-element.60), channel_id=1, source_target_pairs={{0,8},{4,12},{8,0},{12,4},{16,24},{20,28},{24,16},{28,20},{1,9},{5... | collective-permute-start | bytes 688136 | tf_op jit(solution)/shard_map/ppermute | solution.py:21
  74.5 12.2 %collective-permute-start.12 = (bf16[512,896]{1,0:T(8,128)(2,1)S(1)}, bf16[512,896]{1,0:T(8,128)(2,1)S(1)}, u32[]{:S(2)}, u32[]{:S(2)}) collective-permute-start(bf16[512,896]{1,0:T(8,128)(2,1)S(1)} %pad_maximum_fusion), channel_id=1, source_target_pairs={{0,1},{1,0},{2,3},{3,2},{4,5},{5,4},{6,7},{7,6},{8,9},{9,8},{10,11... | collective-permute-start | bytes 2752520 | tf_op jit(solution)/shard_map/ppermute | solution.py:21
  84.2 17.6 %collective-permute-start.18 = (bf16[2688,128]{1,0:T(8,128)(2,1)S(1)}, bf16[2688,128]{1,0:T(8,128)(2,1)S(1)}, u32[]{:S(2)}, u32[]{:S(2)}) collective-permute-start(bf16[2688,128]{1,0:T(8,128)(2,1)S(1)} %pad_maximum_fusion.2), channel_id=1, source_target_pairs={{0,4},{4,0},{8,12},{12,8},{16,20},{20,16},{24,28},{28,24},{1,5},{5... | collective-permute-start | bytes 2064392 | tf_op jit(solution)/shard_map/ppermute | solution.py:21
  88.7 10.4 %collective-permute-start.20 = (bf16[512,128]{1,0:T(8,128)(2,1)S(1)}, bf16[512,128]{1,0:T(8,128)(2,1)S(1)}, u32[]{:S(2)}, u32[]{:S(2)}) collective-permute-start(bf16[512,128]{1,0:T(8,128)(2,1)S(1)} %pad_maximum_fusion.7.grad_ref.refs_2_), channel_id=1, source_target_pairs={{16,0},{20,4},{24,8},{28,12},{17,1},{21,5},{25,9},{29,13},{18,2},{... | collective-permute-start | bytes 393224 | tf_op jit(solution)/shard_map/ppermute | solution.py:21
  90.0 10.8 %collective-permute-start.19 = (bf16[512,128]{1,0:T(8,128)(2,1)S(1)}, bf16[512,128]{1,0:T(8,128)(2,1)S(1)}, u32[]{:S(2)}, u32[]{:S(2)}) collective-permute-start(bf16[512,128]{1,0:T(8,128)(2,1)S(1)} %pad_maximum_fusion.7.grad_ref.refs_2_), channel_id=1, source_target_pairs={{16,4},{20,0},{24,12},{28,8},{17,5},{21,1},{25,13},{29,9},{18,6},{... | collective-permute-start | bytes 393224 | tf_op jit(solution)/shard_map/ppermute | solution.py:21
  91.4 18.3 %collective-permute-start.25 = (bf16[512,256]{1,0:T(8,128)(2,1)S(1)}, bf16[512,256]{1,0:T(8,128)(2,1)S(1)}, u32[]{:S(2)}, u32[]{:S(2)}) collective-permute-start(bf16[512,256]{1,0:T(8,128)(2,1)S(1)} %shard_map.47.refs_0_.kv_ref), channel_id=1, source_target_pairs={{0,20},{4,16},{8,28},{12,24},{1,21},{5,17},{9,29},{13,25},{2,22},{... | collective-permute-start | bytes 786440 | tf_op jit(solution)/shard_map/ppermute | solution.py:21
  97.7 13.3 %collective-permute-start.24 = (bf16[512,256]{1,0:T(8,128)(2,1)S(1)}, bf16[512,256]{1,0:T(8,128)(2,1)S(1)}, u32[]{:S(2)}, u32[]{:S(2)}) collective-permute-start(bf16[512,256]{1,0:T(8,128)(2,1)S(1)} %shard_map.47.refs_0_.kv_ref), channel_id=1, source_target_pairs={{0,16},{4,20},{8,24},{12,28},{1,17},{5,21},{9,25},{13,29},{2,18},{... | collective-permute-start | bytes 786440 | tf_op jit(solution)/shard_map/ppermute | solution.py:21
  101.8 9.9 %collective-permute-start.23 = (bf16[512,256]{1,0:T(8,128)(2,1)S(1)}, bf16[512,256]{1,0:T(8,128)(2,1)S(1)}, u32[]{:S(2)}, u32[]{:S(2)}) collective-permute-start(bf16[512,256]{1,0:T(8,128)(2,1)S(1)} %shard_map.47.refs_0_.kv_ref), channel_id=1, source_target_pairs={{0,4},{4,0},{8,12},{12,8},{16,20},{20,16},{24,28},{28,24},{1,5},{5... | collective-permute-start | bytes 786440 | tf_op jit(solution)/shard_map/ppermute | solution.py:21
  108.1 18.0 %collective-permute-start.22 = (bf16[512,128]{1,0:T(8,128)(2,1)S(1)}, bf16[512,128]{1,0:T(8,128)(2,1)S(1)}, u32[]{:S(2)}, u32[]{:S(2)}) collective-permute-start(bf16[512,128]{1,0:T(8,128)(2,1)S(1)} %shard_map.49.q_ref.refs_0_), channel_id=1, source_target_pairs={{16,4},{20,0},{24,12},{28,8},{17,5},{21,1},{25,13},{29,9},{18,6},{... | collective-permute-start | bytes 393224 | tf_op jit(solution)/shard_map/ppermute | solution.py:21
  109.5 9.0 %collective-permute-start.28 = (bf16[512,256]{1,0:T(8,128)(2,1)S(1)}, bf16[512,256]{1,0:T(8,128)(2,1)S(1)}, u32[]{:S(2)}, u32[]{:S(2)}) collective-permute-start(bf16[512,256]{1,0:T(8,128)(2,1)S(1)} %pad_maximum_fusion.5), channel_id=1, source_target_pairs={{0,4},{4,0},{8,12},{12,8},{16,20},{20,16},{24,28},{28,24},{1,5},{5... | collective-permute-start | bytes 786440 | tf_op jit(solution)/shard_map/ppermute | solution.py:21
  109.7 16.4 %collective-permute-start.21 = (bf16[512,128]{1,0:T(8,128)(2,1)S(1)}, bf16[512,128]{1,0:T(8,128)(2,1)S(1)}, u32[]{:S(2)}, u32[]{:S(2)}) collective-permute-start(bf16[512,128]{1,0:T(8,128)(2,1)S(1)} %shard_map.49.q_ref.refs_0_), channel_id=1, source_target_pairs={{16,0},{20,4},{24,8},{28,12},{17,1},{21,5},{25,9},{29,13},{18,2},{... | collective-permute-start | bytes 393224 | tf_op jit(solution)/shard_map/ppermute | solution.py:21
  114.7 8.6 %collective-permute-start.29 = (f32[8,512]{1,0:T(8,128)S(1)}, f32[8,512]{1,0:T(8,128)S(1)}, u32[]{:S(2)}, u32[]{:S(2)}) collective-permute-start(f32[8,512]{1,0:T(8,128)S(1)} %get-tuple-element.73.refs_4_), channel_id=1, source_target_pairs={{0,4},{4,0},{8,12},{12,8},{16,20},{20,16},{24,28},{28,24},{1,5},{5... | collective-permute-start | bytes 49160 | tf_op jit(solution)/shard_map/ppermute | solution.py:21
  117.2 8.9 %collective-permute-start.27 = (f32[8,512]{1,0:T(8,128)S(1)}, f32[8,512]{1,0:T(8,128)S(1)}, u32[]{:S(2)}, u32[]{:S(2)}) collective-permute-start(f32[8,512]{1,0:T(8,128)S(1)} %get-tuple-element.73.refs_4_), channel_id=1, source_target_pairs={{16,4},{20,0},{24,12},{28,8},{17,5},{21,1},{25,13},{29,9},{18,6},{... | collective-permute-start | bytes 49160 | tf_op jit(solution)/shard_map/ppermute | solution.py:21
  118.5 7.7 %collective-permute-start.26 = (f32[8,512]{1,0:T(8,128)S(1)}, f32[8,512]{1,0:T(8,128)S(1)}, u32[]{:S(2)}, u32[]{:S(2)}) collective-permute-start(f32[8,512]{1,0:T(8,128)S(1)} %get-tuple-element.73.refs_4_), channel_id=1, source_target_pairs={{16,0},{20,4},{24,8},{28,12},{17,1},{21,5},{25,9},{29,13},{18,2},{... | collective-permute-start | bytes 49160 | tf_op jit(solution)/shard_map/ppermute | solution.py:21
  130.2 3.4 %collective-permute-start.37 = (bf16[256,896]{1,0:T(8,128)(2,1)S(1)}, bf16[256,896]{1,0:T(8,128)(2,1)S(1)}, u32[]{:S(2)}, u32[]{:S(2)}) collective-permute-start(bf16[256,896]{1,0:T(8,128)(2,1)S(1)} %convolution_convert_fusion.3), channel_id=1, source_target_pairs={{0,1},{1,0},{2,3},{3,2},{4,5},{5,4},{6,7},{7,6},{8,9},{9,8},{10,11... | collective-permute-start | bytes 1376264 | tf_op jit(solution)/shard_map/ppermute | solution.py:21
  130.3 4.0 %collective-permute-start.33 = (bf16[256,896]{1,0:T(8,128)(2,1)S(1)}, bf16[256,896]{1,0:T(8,128)(2,1)S(1)}, u32[]{:S(2)}, u32[]{:S(2)}) collective-permute-start(bf16[256,896]{1,0:T(8,128)(2,1)S(1)} %convolution_convert_fusion.4), channel_id=1, source_target_pairs={{0,1},{1,0},{2,3},{3,2},{4,5},{5,4},{6,7},{7,6},{8,9},{9,8},{10,11... | collective-permute-start | bytes 1376264 | tf_op jit(solution)/shard_map/ppermute | solution.py:21
  131.5 5.7 %collective-permute-start.31 = (bf16[256,1792]{1,0:T(8,128)(2,1)S(1)}, bf16[256,1792]{1,0:T(8,128)(2,1)S(1)}, u32[]{:S(2)}, u32[]{:S(2)}) collective-permute-start(bf16[256,1792]{1,0:T(8,128)(2,1)S(1)} %convolution_convert_fusion.1), channel_id=1, source_target_pairs={{0,1},{1,0},{2,3},{3,2},{4,5},{5,4},{6,7},{7,6},{8,9},{9,8},{10,11... | collective-permute-start | bytes 2752520 | tf_op jit(solution)/shard_map/ppermute | solution.py:21
  132.3 7.1 %collective-permute-start.36 = (bf16[256,1792]{1,0:T(8,128)(2,1)S(1)}, bf16[256,1792]{1,0:T(8,128)(2,1)S(1)}, u32[]{:S(2)}, u32[]{:S(2)}) collective-permute-start(bf16[256,1792]{1,0:T(8,128)(2,1)S(1)} %convolution_convert_fusion), channel_id=1, source_target_pairs={{0,1},{1,0},{2,3},{3,2},{4,5},{5,4},{6,7},{7,6},{8,9},{9,8},{10,11... | collective-permute-start | bytes 2752520 | tf_op jit(solution)/shard_map/ppermute | solution.py:21
  133.4 18.9 %collective-permute-start.30 = (bf16[256,1792]{1,0:T(8,128)(2,1)S(1)}, bf16[256,1792]{1,0:T(8,128)(2,1)S(1)}, u32[]{:S(2)}, u32[]{:S(2)}) collective-permute-start(bf16[256,1792]{1,0:T(8,128)(2,1)S(1)} %convolution_convert_fusion.2), channel_id=1, source_target_pairs={{0,1},{1,0},{2,3},{3,2},{4,5},{5,4},{6,7},{7,6},{8,9},{9,8},{10,11... | collective-permute-start | bytes 2752520 | tf_op jit(solution)/shard_map/ppermute | solution.py:21
  134.1 16.2 %collective-permute-start.38 = (bf16[256,896]{1,0:T(8,128)(2,1)S(1)}, bf16[256,896]{1,0:T(8,128)(2,1)S(1)}, u32[]{:S(2)}, u32[]{:S(2)}) collective-permute-start(bf16[256,896]{1,0:T(8,128)(2,1)S(1)} %fusion.7), channel_id=1, source_target_pairs={{0,2},{1,3},{2,0},{3,1},{4,6},{5,7},{6,4},{7,5},{8,10},{9,11},{10,... | collective-permute-start | bytes 1376264 | tf_op jit(solution)/shard_map/ppermute | solution.py:21
  134.8 13.6 %collective-permute-start.34 = (bf16[256,896]{1,0:T(8,128)(2,1)S(1)}, bf16[256,896]{1,0:T(8,128)(2,1)S(1)}, u32[]{:S(2)}, u32[]{:S(2)}) collective-permute-start(bf16[256,896]{1,0:T(8,128)(2,1)S(1)} %fusion.6), channel_id=1, source_target_pairs={{0,8},{4,12},{8,0},{12,4},{16,24},{20,28},{24,16},{28,20},{1,9},{5... | collective-permute-start | bytes 1376264 | tf_op jit(solution)/shard_map/ppermute | solution.py:21
  137.8 19.4 %collective-permute-start.32 = (bf16[256,896]{1,0:T(8,128)(2,1)S(1)}, bf16[256,896]{1,0:T(8,128)(2,1)S(1)}, u32[]{:S(2)}, u32[]{:S(2)}) collective-permute-start(bf16[256,896]{1,0:T(8,128)(2,1)S(1)} %slice.115), channel_id=1, source_target_pairs={{0,2},{1,3},{2,0},{3,1},{4,6},{5,7},{6,4},{7,5},{8,10},{9,11},{10,... | collective-permute-start | bytes 1376264 | tf_op jit(solution)/shard_map/ppermute | solution.py:21
  140.1 18.1 %collective-permute-start.40 = (bf16[256,896]{1,0:T(8,128)(2,1)S(1)}, bf16[256,896]{1,0:T(8,128)(2,1)S(1)}, u32[]{:S(2)}, u32[]{:S(2)}) collective-permute-start(bf16[256,896]{1,0:T(8,128)(2,1)S(1)} %slice.114), channel_id=1, source_target_pairs={{0,8},{4,12},{8,0},{12,4},{16,24},{20,28},{24,16},{28,20},{1,9},{5... | collective-permute-start | bytes 1376264 | tf_op jit(solution)/shard_map/ppermute | solution.py:21
  148.5 18.1 %collective-permute-start.35 = (bf16[256,896]{1,0:T(8,128)(2,1)S(1)}, bf16[256,896]{1,0:T(8,128)(2,1)S(1)}, u32[]{:S(2)}, u32[]{:S(2)}) collective-permute-start(bf16[256,896]{1,0:T(8,128)(2,1)S(1)} %fusion.9), channel_id=1, source_target_pairs={{0,2},{1,3},{2,0},{3,1},{4,6},{5,7},{6,4},{7,5},{8,10},{9,11},{10,... | collective-permute-start | bytes 1376264 | tf_op jit(solution)/shard_map/ppermute | solution.py:21
  150.3 17.3 %collective-permute-start.39 = (bf16[256,896]{1,0:T(8,128)(2,1)S(1)}, bf16[256,896]{1,0:T(8,128)(2,1)S(1)}, u32[]{:S(2)}, u32[]{:S(2)}) collective-permute-start(bf16[256,896]{1,0:T(8,128)(2,1)S(1)} %fusion.8), channel_id=1, source_target_pairs={{0,8},{4,12},{8,0},{12,4},{16,24},{20,28},{24,16},{28,20},{1,9},{5... | collective-permute-start | bytes 1376264 | tf_op jit(solution)/shard_map/ppermute | solution.py:21

commit v5 on v4

--- a/solution.py
+++ b/solution.py
@@ -329,7 +329,10 @@
         ),
         2 + sets,
     )(query_limits, q, grad, *kvs)
-    moved_stats = {d: to_earlier(stat, distance=d) for d in others}
+    moved_stats = {d: to_earlier(stat, distance=d) for d in others[:-1]}
+    near_stat, both = lax.optimization_barrier((stat, order["both"]))
+    moved_stats[others[-1]] = to_earlier(near_stat, distance=others[-1])
+    qs[1], grads[1] = both[:, :HD], both[:, HD:]
     stats = [stat] + [moved_stats[d] for d in group[1:]]
     dq = local_call(
         functools.partial(query_kernel, sets, run),

time: 169 us -> 169 us (level)
  no operation moved by 1% of the time
where the time goes in v5:
time: 169 us
  waiting for transfers between devices  81.5 us (48%)
  starting transfers between devices  50.4 us (30%)
  Pallas kernels  20.7 us (12%)
  local copies, waits for them, and re-layouts  6.58 us (4%)
  matrix products  5.88 us (3%)
  other arithmetic  3.08 us (2%)
    ppermute x41, waiting for transfers between devices, swap(): return lax.ppermute(array, axis, pairs)  81.5 us
    ppermute x41, starting transfers between devices, swap(): return lax.ppermute(array, axis, pairs)  50.4 us
    pallas_call x4, Pallas kernels, project(): local_call(functools.partial(project_kernel, groups, len(ds)), out, 1 + l...  7.4 us
    dot_general x10, matrix products, dot_nt(): lax.dot_general(a, b, (((1,), (1,)), ((), ())), preferred_element_type=F32)  5.88 us
  transfers between devices with their start and end apart: 41, of which 15 were waited for; matrix products, arithmetic and copies ran while one was open for 8% of the time, Pallas kernels for 10%

profile of v5, /device:TPU:0, one launch (start us, length us, event | category | flops | bytes accessed | tf_op | source)
XLA Modules:
  0.0 168.9 jit_solution(9465446068332744424)
XLA Ops:
  0.0 1.4 fusion.37
  1.7 4.1 %collective-permute-start.6 = (bf16[896,256]{1,0:T(8,128)(2,1)S(1)}, bf16[896,256]{1,0:T(8,128)(2,1)S(1)}, u32[]{:S(2)}, u32[]{:S(2)}) collective-permute-start(bf16[896,256]{1,0:T(8,128)(2,1)S(1)} %pad_maximum_fusion.3.refs_3_), channel_id=1, source_target_pairs={{0,16},{4,20},{8,24},{12,28},{16,0},{20,4},{24,8},{28,12},{1,17},{... | collective-permute-start | bytes 1376264 | tf_op jit(solution)/shard_map/ppermute | solution.py:21
  5.8 1.5 collective-permute-start.2
  7.9 1.6 collective-permute-start.1
  9.5 2.2 %constant_dynamic-slice_fusion.1 = (bf16[256,896]{1,0:T(8,128)(2,1)}, bf16[256,896]{1,0:T(8,128)(2,1)}) fusion(bf16[256,7168]{1,0:T(8,128)(2,1)} %own_ref.7, s32[]{:T(128)S(6)} %select_n.158, s32[]{:T(128)S(6)} %select_n.157), kind=kLoop, calls=%fused_computation.84 | loop fusion | bytes 1835016 | tf_op jit(solution)/shard_map/dynamic_slice | solution.py:202
  13.0 1.6 collective-permute-start.9
  14.8 2.9 %collective-permute-done.2.refs_3_ = bf16[896,256]{1,0:T(8,128)(2,1)S(1)} collective-permute-done((bf16[896,256]{1,0:T(8,128)(2,1)S(1)}, bf16[896,256]{1,0:T(8,128)(2,1)S(1)}, u32[]{:S(2)}, u32[]{:S(2)}) %collective-permute-start.2) | collective-permute-done | bytes 458784 | tf_op jit(solution)/shard_map/ppermute | solution.py:21
  17.7 1.5 collective-permute-start.3
  19.4 14.6 %collective-permute-done.refs_0_ = bf16[256,896]{1,0:T(8,128)(2,1)S(1)} collective-permute-done((bf16[256,896]{1,0:T(8,128)(2,1)}, bf16[256,896]{1,0:T(8,128)(2,1)S(1)}, u32[]{:S(2)}, u32[]{:S(2)}) %collective-permute-start) | collective-permute-done | bytes 458784 | tf_op jit(solution)/shard_map/ppermute | solution.py:21
  34.0 1.5 collective-permute-start.13
  37.1 1.3 collective-permute-start.7
  38.9 12.7 %collective-permute-done.9.refs_4_ = bf16[896,256]{1,0:T(8,128)(2,1)S(1)} collective-permute-done((bf16[896,256]{1,0:T(8,128)(2,1)}, bf16[896,256]{1,0:T(8,128)(2,1)S(1)}, u32[]{:S(2)}, u32[]{:S(2)}) %collective-permute-start.9) | collective-permute-done | bytes 458784 | tf_op jit(solution)/shard_map/ppermute | solution.py:21
  52.6 9.7 %collective-permute-done.10.refs_4_ = bf16[896,256]{1,0:T(8,128)(2,1)S(1)} collective-permute-done((bf16[896,256]{1,0:T(8,128)(2,1)S(1)}, bf16[896,256]{1,0:T(8,128)(2,1)S(1)}, u32[]{:S(2)}, u32[]{:S(2)}) %collective-permute-start.10) | collective-permute-done | bytes 458784 | tf_op jit(solution)/shard_map/ppermute | solution.py:21
  62.9 1.5 collective-permute-start.5
  64.5 1.1 collective-permute-start.16
  66.1 5.9 %collective-permute-done.11.refs_6_ = bf16[896,256]{1,0:T(8,128)(2,1)S(1)} collective-permute-done((bf16[896,256]{1,0:T(8,128)(2,1)S(1)}, bf16[896,256]{1,0:T(8,128)(2,1)S(1)}, u32[]{:S(2)}, u32[]{:S(2)}) %collective-permute-start.11) | collective-permute-done | bytes 458784 | tf_op jit(solution)/shard_map/ppermute | solution.py:21
  72.0 1.9 %shard_map.46.refs_7_ = f32[512,256]{1,0:T(8,128)S(1)} custom-call(s32[2,4]{1,0:T(2,128)S(1)} %pad_add_fusion.1.place_ref, bf16[256,7168]{1,0:T(8,128)(2,1)S(1)} %copy-done.1, bf16[256,896]{1,0:T(8,128)(2,1)S(1)} %collective-permute-done.refs_0_, bf16[256,896]{1,0:T(8,128)(2,1)S(1)} %collective-permute-done.13.refs_1_, ...), custom_call_target="tpu_custom_call" | custom-call | flops 1 | bytes 1 | tf_op jit(solution)/shard_map/pallas_call | solution.py:228
  74.7 8.6 %collective-permute-done.15.refs_5_ = bf16[896,128]{1,0:T(8,128)(2,1)S(1)} collective-permute-done((bf16[896,128]{1,0:T(8,128)(2,1)S(1)}, bf16[896,128]{1,0:T(8,128)(2,1)S(1)}, u32[]{:S(2)}, u32[]{:S(2)}) %collective-permute-start.15) | collective-permute-done | bytes 229408 | tf_op jit(solution)/shard_map/ppermute | solution.py:21
  84.2 1.6 collective-permute-start.18
  86.8 1.9 %shard_map.47.refs_0_.kv_ref = bf16[512,256]{1,0:T(8,128)(2,1)S(1)} custom-call(s32[2,4]{1,0:T(2,128)S(1)} %pad_add_fusion.place_ref, bf16[256,7168]{1,0:T(8,128)(2,1)S(1)} %copy-done.1, bf16[256,896]{1,0:T(8,128)(2,1)S(1)} %collective-permute-done.4.refs_0_, bf16[256,896]{1,0:T(8,128)(2,1)S(1)} %collective-permute-done.5.refs_1_, ...), custom_call_target="tpu_custom_call" | custom-call | flops 1 | bytes 1 | tf_op jit(solution)/shard_map/pallas_call | solution.py:228
  88.7 1.3 collective-permute-start.20
  90.0 1.3 collective-permute-start.19
  91.4 6.4 %collective-permute-start.25 = (bf16[512,256]{1,0:T(8,128)(2,1)S(1)}, bf16[512,256]{1,0:T(8,128)(2,1)S(1)}, u32[]{:S(2)}, u32[]{:S(2)}) collective-permute-start(bf16[512,256]{1,0:T(8,128)(2,1)S(1)} %shard_map.47.refs_0_.kv_ref), channel_id=1, source_target_pairs={{0,20},{4,16},{8,28},{12,24},{1,21},{5,17},{9,29},{13,25},{2,22},{... | collective-permute-start | bytes 786440 | tf_op jit(solution)/shard_map/ppermute | solution.py:21
  97.7 1.3 collective-permute-start.24
  99.1 1.7 collective-permute-done.19.refs_3_
  100.7 1.0 collective-permute-done.18
  101.8 2.4 %collective-permute-start.23 = (bf16[512,256]{1,0:T(8,128)(2,1)S(1)}, bf16[512,256]{1,0:T(8,128)(2,1)S(1)}, u32[]{:S(2)}, u32[]{:S(2)}) collective-permute-start(bf16[512,256]{1,0:T(8,128)(2,1)S(1)} %shard_map.47.refs_0_.kv_ref), channel_id=1, source_target_pairs={{0,4},{4,0},{8,12},{12,8},{16,20},{20,16},{24,28},{28,24},{1,5},{5... | collective-permute-start | bytes 786440 | tf_op jit(solution)/shard_map/ppermute | solution.py:21
  104.5 1.8 %shard_map.48.refs_7_ = f32[512,128]{1,0:T(8,128)S(1)} custom-call(s32[2,4]{1,0:T(2,128)S(1)} %pad_add_fusion.1.place_ref, bf16[256,7168]{1,0:T(8,128)(2,1)S(1)} %copy-done.1, bf16[256,896]{1,0:T(8,128)(2,1)S(1)} %collective-permute-done.refs_0_, bf16[256,896]{1,0:T(8,128)(2,1)S(1)} %collective-permute-done.13.refs_1_, ...), custom_call_target="tpu_custom_call" | custom-call | flops 1 | bytes 1 | tf_op jit(solution)/shard_map/pallas_call | solution.py:228
  106.3 1.8 %shard_map.49.q_ref.refs_0_ = bf16[512,128]{1,0:T(8,128)(2,1)S(1)} custom-call(s32[2,4]{1,0:T(2,128)S(1)} %pad_add_fusion.place_ref, bf16[256,7168]{1,0:T(8,128)(2,1)S(1)} %copy-done.1, bf16[256,896]{1,0:T(8,128)(2,1)S(1)} %collective-permute-done.4.refs_0_, bf16[256,896]{1,0:T(8,128)(2,1)S(1)} %collective-permute-done.5.refs_1_, ...), custom_call_target="tpu_custom_call" | custom-call | flops 1 | bytes 1 | tf_op jit(solution)/shard_map/pallas_call | solution.py:228
  108.1 1.3 collective-permute-start.22
  109.7 1.3 collective-permute-start.21
  111.7 2.9 %shard_map.50 = (f32[8,512]{1,0:T(8,128)S(1)}, f32[512,128]{1,0:T(8,128)S(1)}) custom-call(s32[2,8]{1,0:T(2,128)S(1)} %get-tuple-element.102.limit_ref, bf16[512,128]{1,0:T(8,128)(2,1)S(1)} %shard_map.49.q_ref.refs_0_, bf16[512,128]{1,0:T(8,128)(2,1)S(1)} %pad_maximum_fusion.7.grad_ref.refs_2_, bf16[512,256]{1,0:T(8,128)(2,1)S(1)} %shard_map.47.refs_0_.kv_ref, ...), custom_call_target="tpu_custom_call" | custom-call | flops 1 | bytes 1 | tf_op jit(solution)/shard_map/pallas_call | solution.py:324
  114.7 1.3 collective-permute-start.27
  115.9 1.5 collective-permute-start.26
  117.4 2.5 %collective-permute-start.29 = (f32[8,512]{1,0:T(8,128)S(1)}, f32[8,512]{1,0:T(8,128)S(1)}, u32[]{:S(2)}, u32[]{:S(2)}) collective-permute-start(f32[8,512]{1,0:T(8,128)S(1)} %get-tuple-element.77.refs_4_), channel_id=1, source_target_pairs={{0,4},{4,0},{8,12},{12,8},{16,20},{20,16},{24,28},{28,24},{1,5},{5... | collective-permute-start | bytes 49160 | tf_op jit(solution)/shard_map/ppermute | solution.py:21
  120.0 3.3 %shard_map.53 = bf16[512,128]{1,0:T(8,128)(2,1)S(1)} custom-call(s32[2,8]{1,0:T(2,128)S(1)} %get-tuple-element.102.limit_ref, bf16[512,128]{1,0:T(8,128)(2,1)S(1)} %shard_map.49.q_ref.refs_0_, bf16[512,128]{1,0:T(8,128)(2,1)S(1)} %pad_maximum_fusion.7.grad_ref.refs_2_, f32[512,128]{1,0:T(8,128)S(1)} %get-tuple-element.78.column_ref, ...), custom_call_target="tpu_custom_call" | custom-call | flops 1 | bytes 1 | tf_op jit(solution)/shard_map/pallas_call | solution.py:337
  123.3 2.8 %shard_map.51.refs_6_ = f32[512,256]{1,0:T(8,128)S(1)} custom-call(s32[2,4]{1,0:T(2,128)S(1)} %get-tuple-element.100.limit_ref, bf16[512,256]{1,0:T(8,128)(2,1)S(1)} %shard_map.47.refs_0_.kv_ref, bf16[512,128]{1,0:T(8,128)(2,1)S(1)} %shard_map.49.q_ref.refs_0_, bf16[512,128]{1,0:T(8,128)(2,1)S(1)} %get-tuple-element.97.refs_1_, ...), custom_call_target="tpu_custom_call" | custom-call | flops 1 | bytes 1 | tf_op jit(solution)/shard_map/pallas_call | solution.py:343
  126.2 3.1 %shard_map.52 = bf16[512,256]{1,0:T(8,128)(2,1)S(1)} custom-call(s32[2,4]{1,0:T(2,128)S(1)} %get-tuple-element.101.limit_ref, bf16[512,256]{1,0:T(8,128)(2,1)S(1)} %shard_map.47.refs_0_.kv_ref, bf16[512,128]{1,0:T(8,128)(2,1)S(1)} %collective-permute-done.21.refs_0_, bf16[512,128]{1,0:T(8,128)(2,1)S(1)} %collective-permute-done.22.refs_1_, ...), custom_call_target="tpu_custom_call" | custom-call | flops 1 | bytes 1 | tf_op jit(solution)/shard_map/pallas_call | solution.py:349
  134.7 2.5 %collective-permute-start.34 = (bf16[256,896]{1,0:T(8,128)(2,1)S(1)}, bf16[256,896]{1,0:T(8,128)(2,1)S(1)}, u32[]{:S(2)}, u32[]{:S(2)}) collective-permute-start(bf16[256,896]{1,0:T(8,128)(2,1)S(1)} %fusion.6), channel_id=1, source_target_pairs={{0,8},{4,12},{8,0},{12,4},{16,24},{20,28},{24,16},{28,20},{1,9},{5... | collective-permute-start | bytes 1376264 | tf_op jit(solution)/shard_map/ppermute | solution.py:21
  137.9 1.6 collective-permute-start.32
  140.4 8.1 %collective-permute-done.34 = bf16[256,896]{1,0:T(8,128)(2,1)S(1)} collective-permute-done((bf16[256,896]{1,0:T(8,128)(2,1)S(1)}, bf16[256,896]{1,0:T(8,128)(2,1)S(1)}, u32[]{:S(2)}, u32[]{:S(2)}) %collective-permute-start.34) | collective-permute-done | bytes 458784 | tf_op jit(solution)/shard_map/ppermute | solution.py:21
  148.6 1.7 %collective-permute-start.35 = (bf16[256,896]{1,0:T(8,128)(2,1)S(1)}, bf16[256,896]{1,0:T(8,128)(2,1)S(1)}, u32[]{:S(2)}, u32[]{:S(2)}) collective-permute-start(bf16[256,896]{1,0:T(8,128)(2,1)S(1)} %fusion.9), channel_id=1, source_target_pairs={{0,2},{1,3},{2,0},{3,1},{4,6},{5,7},{6,4},{7,5},{8,10},{9,11},{10,... | collective-permute-start | bytes 1376264 | tf_op jit(solution)/shard_map/ppermute | solution.py:21
  150.3 2.0 %collective-permute-start.39 = (bf16[256,896]{1,0:T(8,128)(2,1)S(1)}, bf16[256,896]{1,0:T(8,128)(2,1)S(1)}, u32[]{:S(2)}, u32[]{:S(2)}) collective-permute-start(bf16[256,896]{1,0:T(8,128)(2,1)S(1)} %fusion.8), channel_id=1, source_target_pairs={{0,8},{4,12},{8,0},{12,4},{16,24},{20,28},{24,16},{28,20},{1,9},{5... | collective-permute-start | bytes 1376264 | tf_op jit(solution)/shard_map/ppermute | solution.py:21
  153.0 4.3 %collective-permute-done.32.x_a = bf16[256,896]{1,0:T(8,128)(2,1)S(1)} collective-permute-done((bf16[256,896]{1,0:T(8,128)(2,1)S(1)}, bf16[256,896]{1,0:T(8,128)(2,1)S(1)}, u32[]{:S(2)}, u32[]{:S(2)}) %collective-permute-start.32) | collective-permute-done | bytes 458784 | tf_op jit(solution)/shard_map/ppermute | solution.py:21
  157.3 1.0 collective-permute-done.40.z_b
  158.3 8.4 %collective-permute-done.35.x_b = bf16[256,896]{1,0:T(8,128)(2,1)S(1)} collective-permute-done((bf16[256,896]{1,0:T(8,128)(2,1)S(1)}, bf16[256,896]{1,0:T(8,128)(2,1)S(1)}, u32[]{:S(2)}, u32[]{:S(2)}) %collective-permute-start.35) | collective-permute-done | bytes 458784 | tf_op jit(solution)/shard_map/ppermute | solution.py:21
  166.7 1.0 collective-permute-done.39.z_a
  167.7 1.2 shard_map.54
  (115 shorter events, 18.5 us)
Async XLA Ops:
  0.0 35.7 %copy-start = (s32[4,4]{1,0:T(4,128)S(1)}, s32[4,4]{1,0:T(4,128)}, u32[]{:S(2)}) copy-start(s32[4,4]{1,0:T(4,128)} %param.6) | copy-start | bytes 196
  1.4 5.9 %copy-start.2 = (bf16[256,256]{1,0:T(8,128)(2,1)S(1)}, bf16[256,256]{1,0:T(8,128)(2,1)}, u32[]{:S(2)}) copy-start(bf16[256,256]{1,0:T(8,128)(2,1)} %param.7) | copy-start | bytes 393220
  1.7 35.4 %collective-permute-start.6 = (bf16[896,256]{1,0:T(8,128)(2,1)S(1)}, bf16[896,256]{1,0:T(8,128)(2,1)S(1)}, u32[]{:S(2)}, u32[]{:S(2)}) collective-permute-start(bf16[896,256]{1,0:T(8,128)(2,1)S(1)} %pad_maximum_fusion.3.refs_3_), channel_id=1, source_target_pairs={{0,16},{4,20},{8,24},{12,28},{16,0},{20,4},{24,8},{28,12},{1,17},{... | collective-permute-start | bytes 1376264 | tf_op jit(solution)/shard_map/ppermute | solution.py:21
  5.8 12.0 %collective-permute-start.2 = (bf16[896,256]{1,0:T(8,128)(2,1)S(1)}, bf16[896,256]{1,0:T(8,128)(2,1)S(1)}, u32[]{:S(2)}, u32[]{:S(2)}) collective-permute-start(bf16[896,256]{1,0:T(8,128)(2,1)S(1)} %pad_maximum_fusion.3.refs_3_), channel_id=1, source_target_pairs={{0,4},{4,0},{8,12},{12,8},{16,20},{20,16},{24,28},{28,24},{1,5},{5... | collective-permute-start | bytes 1376264 | tf_op jit(solution)/shard_map/ppermute | solution.py:21
  7.9 11.5 %collective-permute-start.1 = (bf16[256,128]{1,0:T(8,128)(2,1)}, bf16[256,128]{1,0:T(8,128)(2,1)}, u32[]{:S(2)}, u32[]{:S(2)}) collective-permute-start(bf16[256,128]{1,0:T(8,128)(2,1)} %get-tuple-element.99), channel_id=1, source_target_pairs={{0,8},{4,12},{8,0},{12,4},{16,24},{20,28},{24,16},{28,20},{1,9},{5... | collective-permute-start | bytes 196616 | tf_op jit(solution)/shard_map/ppermute | solution.py:21
  11.7 22.3 %collective-permute-start = (bf16[256,896]{1,0:T(8,128)(2,1)}, bf16[256,896]{1,0:T(8,128)(2,1)S(1)}, u32[]{:S(2)}, u32[]{:S(2)}) collective-permute-start(bf16[256,896]{1,0:T(8,128)(2,1)} %get-tuple-element.79), channel_id=1, source_target_pairs={{0,8},{4,12},{8,0},{12,4},{16,24},{20,28},{24,16},{28,20},{1,9},{5... | collective-permute-start | bytes 1376264 | tf_op jit(solution)/shard_map/ppermute | solution.py:21
  13.0 38.7 %collective-permute-start.9 = (bf16[896,256]{1,0:T(8,128)(2,1)}, bf16[896,256]{1,0:T(8,128)(2,1)S(1)}, u32[]{:S(2)}, u32[]{:S(2)}) collective-permute-start(bf16[896,256]{1,0:T(8,128)(2,1)} %pad_maximum_fusion.4), channel_id=1, source_target_pairs={{0,8},{4,12},{8,0},{12,4},{16,24},{20,28},{24,16},{28,20},{1,9},{5... | collective-permute-start | bytes 1376264 | tf_op jit(solution)/shard_map/ppermute | solution.py:21
  17.7 16.3 %collective-permute-start.3 = (bf16[896,128]{1,0:T(8,128)(2,1)S(1)}, bf16[896,128]{1,0:T(8,128)(2,1)S(1)}, u32[]{:S(2)}, u32[]{:S(2)}) collective-permute-start(bf16[896,128]{1,0:T(8,128)(2,1)S(1)} %get-tuple-element.68.refs_3_), channel_id=1, source_target_pairs={{0,4},{4,0},{8,12},{12,8},{16,20},{20,16},{24,28},{28,24},{1,5},{5... | collective-permute-start | bytes 688136 | tf_op jit(solution)/shard_map/ppermute | solution.py:21
  34.0 18.2 %collective-permute-start.13 = (bf16[256,896]{1,0:T(8,128)(2,1)S(1)}, bf16[256,896]{1,0:T(8,128)(2,1)S(1)}, u32[]{:S(2)}, u32[]{:S(2)}) collective-permute-start(bf16[256,896]{1,0:T(8,128)(2,1)S(1)} %collective-permute-done.refs_0_), channel_id=1, source_target_pairs={{0,2},{1,3},{2,0},{3,1},{4,6},{5,7},{6,4},{7,5},{8,10},{9,11},{10,... | collective-permute-start | bytes 1376264 | tf_op jit(solution)/shard_map/ppermute | solution.py:21
  37.1 34.9 %copy-start.1 = (bf16[256,7168]{1,0:T(8,128)(2,1)S(1)}, bf16[256,7168]{1,0:T(8,128)(2,1)}, u32[]{:S(2)}) copy-start(bf16[256,7168]{1,0:T(8,128)(2,1)} %own_ref.7) | copy-start | bytes 11010052
  37.1 15.5 %collective-permute-start.7 = (bf16[896,256]{1,0:T(8,128)(2,1)}, bf16[896,256]{1,0:T(8,128)(2,1)S(1)}, u32[]{:S(2)}, u32[]{:S(2)}) collective-permute-start(bf16[896,256]{1,0:T(8,128)(2,1)} %pad_maximum_fusion.4), channel_id=1, source_target_pairs={{0,24},{4,28},{8,16},{12,20},{16,8},{20,12},{24,0},{28,4},{1,25},{... | collective-permute-start | bytes 1376264 | tf_op jit(solution)/shard_map/ppermute | solution.py:21
  38.4 14.2 %collective-permute-start.8 = (bf16[896,256]{1,0:T(8,128)(2,1)S(1)}, bf16[896,256]{1,0:T(8,128)(2,1)S(1)}, u32[]{:S(2)}, u32[]{:S(2)}) collective-permute-start(bf16[896,256]{1,0:T(8,128)(2,1)S(1)} %collective-permute-done.6.refs_5_), channel_id=1, source_target_pairs={{0,4},{4,0},{8,12},{12,8},{16,20},{20,16},{24,28},{28,24},{1,5},{5... | collective-permute-start | bytes 1376264 | tf_op jit(solution)/shard_map/ppermute | solution.py:21
  51.6 10.7 %collective-permute-start.10 = (bf16[896,256]{1,0:T(8,128)(2,1)S(1)}, bf16[896,256]{1,0:T(8,128)(2,1)S(1)}, u32[]{:S(2)}, u32[]{:S(2)}) collective-permute-start(bf16[896,256]{1,0:T(8,128)(2,1)S(1)} %collective-permute-done.9.refs_4_), channel_id=1, source_target_pairs={{0,4},{4,0},{8,12},{12,8},{16,20},{20,16},{24,28},{28,24},{1,5},{5... | collective-permute-start | bytes 1376264 | tf_op jit(solution)/shard_map/ppermute | solution.py:21
  52.2 10.7 %collective-permute-start.4 = (bf16[256,896]{1,0:T(8,128)(2,1)}, bf16[256,896]{1,0:T(8,128)(2,1)S(1)}, u32[]{:S(2)}, u32[]{:S(2)}) collective-permute-start(bf16[256,896]{1,0:T(8,128)(2,1)} %get-tuple-element.44), channel_id=1, source_target_pairs={{0,8},{4,12},{8,0},{12,4},{16,24},{20,28},{24,16},{28,20},{1,9},{5... | collective-permute-start | bytes 1376264 | tf_op jit(solution)/shard_map/ppermute | solution.py:21
  52.3 19.7 %collective-permute-start.14 = (bf16[512,896]{1,0:T(8,128)(2,1)S(1)}, bf16[512,896]{1,0:T(8,128)(2,1)S(1)}, u32[]{:S(2)}, u32[]{:S(2)}) collective-permute-start(bf16[512,896]{1,0:T(8,128)(2,1)S(1)} %pad_maximum_fusion.1), channel_id=1, source_target_pairs={{0,1},{1,0},{2,3},{3,2},{4,5},{5,4},{6,7},{7,6},{8,9},{9,8},{10,11... | collective-permute-start | bytes 2752520 | tf_op jit(solution)/shard_map/ppermute | solution.py:21
  62.3 9.6 %collective-permute-start.11 = (bf16[896,256]{1,0:T(8,128)(2,1)S(1)}, bf16[896,256]{1,0:T(8,128)(2,1)S(1)}, u32[]{:S(2)}, u32[]{:S(2)}) collective-permute-start(bf16[896,256]{1,0:T(8,128)(2,1)S(1)} %collective-permute-done.7.refs_6_), channel_id=1, source_target_pairs={{0,4},{4,0},{8,12},{12,8},{16,20},{20,16},{24,28},{28,24},{1,5},{5... | collective-permute-start | bytes 1376264 | tf_op jit(solution)/shard_map/ppermute | solution.py:21
  62.9 9.1 %collective-permute-start.5 = (bf16[256,896]{1,0:T(8,128)(2,1)S(1)}, bf16[256,896]{1,0:T(8,128)(2,1)S(1)}, u32[]{:S(2)}, u32[]{:S(2)}) collective-permute-start(bf16[256,896]{1,0:T(8,128)(2,1)S(1)} %collective-permute-done.4.refs_0_), channel_id=1, source_target_pairs={{0,2},{1,3},{2,0},{3,1},{4,6},{5,7},{6,4},{7,5},{8,10},{9,11},{10,... | collective-permute-start | bytes 1376264 | tf_op jit(solution)/shard_map/ppermute | solution.py:21
  64.5 10.1 %collective-permute-start.16 = (bf16[896,128]{1,0:T(8,128)(2,1)S(1)}, bf16[896,128]{1,0:T(8,128)(2,1)S(1)}, u32[]{:S(2)}, u32[]{:S(2)}) collective-permute-start(bf16[896,128]{1,0:T(8,128)(2,1)S(1)} %get-tuple-element.62), channel_id=1, source_target_pairs={{0,24},{4,28},{8,16},{12,20},{16,8},{20,12},{24,0},{28,4},{1,25},{... | collective-permute-start | bytes 688136 | tf_op jit(solution)/shard_map/ppermute | solution.py:21
  65.7 17.6 %collective-permute-start.15 = (bf16[896,128]{1,0:T(8,128)(2,1)S(1)}, bf16[896,128]{1,0:T(8,128)(2,1)S(1)}, u32[]{:S(2)}, u32[]{:S(2)}) collective-permute-start(bf16[896,128]{1,0:T(8,128)(2,1)S(1)} %get-tuple-element.68.refs_3_), channel_id=1, source_target_pairs={{0,16},{4,20},{8,24},{12,28},{16,0},{20,4},{24,8},{28,12},{1,17},{... | collective-permute-start | bytes 688136 | tf_op jit(solution)/shard_map/ppermute | solution.py:21
  73.9 10.3 %collective-permute-start.17 = (bf16[896,128]{1,0:T(8,128)(2,1)S(1)}, bf16[896,128]{1,0:T(8,128)(2,1)S(1)}, u32[]{:S(2)}, u32[]{:S(2)}) collective-permute-start(bf16[896,128]{1,0:T(8,128)(2,1)S(1)} %get-tuple-element.62), channel_id=1, source_target_pairs={{0,8},{4,12},{8,0},{12,4},{16,24},{20,28},{24,16},{28,20},{1,9},{5... | collective-permute-start | bytes 688136 | tf_op jit(solution)/shard_map/ppermute | solution.py:21
  74.5 12.2 %collective-permute-start.12 = (bf16[512,896]{1,0:T(8,128)(2,1)S(1)}, bf16[512,896]{1,0:T(8,128)(2,1)S(1)}, u32[]{:S(2)}, u32[]{:S(2)}) collective-permute-start(bf16[512,896]{1,0:T(8,128)(2,1)S(1)} %pad_maximum_fusion), channel_id=1, source_target_pairs={{0,1},{1,0},{2,3},{3,2},{4,5},{5,4},{6,7},{7,6},{8,9},{9,8},{10,11... | collective-permute-start | bytes 2752520 | tf_op jit(solution)/shard_map/ppermute | solution.py:21
  84.2 17.6 %collective-permute-start.18 = (bf16[2688,128]{1,0:T(8,128)(2,1)S(1)}, bf16[2688,128]{1,0:T(8,128)(2,1)S(1)}, u32[]{:S(2)}, u32[]{:S(2)}) collective-permute-start(bf16[2688,128]{1,0:T(8,128)(2,1)S(1)} %pad_maximum_fusion.2), channel_id=1, source_target_pairs={{0,4},{4,0},{8,12},{12,8},{16,20},{20,16},{24,28},{28,24},{1,5},{5... | collective-permute-start | bytes 2064392 | tf_op jit(solution)/shard_map/ppermute | solution.py:21
  88.7 10.4 %collective-permute-start.20 = (bf16[512,128]{1,0:T(8,128)(2,1)S(1)}, bf16[512,128]{1,0:T(8,128)(2,1)S(1)}, u32[]{:S(2)}, u32[]{:S(2)}) collective-permute-start(bf16[512,128]{1,0:T(8,128)(2,1)S(1)} %pad_maximum_fusion.7.grad_ref.refs_2_), channel_id=1, source_target_pairs={{16,0},{20,4},{24,8},{28,12},{17,1},{21,5},{25,9},{29,13},{18,2},{... | collective-permute-start | bytes 393224 | tf_op jit(solution)/shard_map/ppermute | solution.py:21
  90.0 10.8 %collective-permute-start.19 = (bf16[512,128]{1,0:T(8,128)(2,1)S(1)}, bf16[512,128]{1,0:T(8,128)(2,1)S(1)}, u32[]{:S(2)}, u32[]{:S(2)}) collective-permute-start(bf16[512,128]{1,0:T(8,128)(2,1)S(1)} %pad_maximum_fusion.7.grad_ref.refs_2_), channel_id=1, source_target_pairs={{16,4},{20,0},{24,12},{28,8},{17,5},{21,1},{25,13},{29,9},{18,6},{... | collective-permute-start | bytes 393224 | tf_op jit(solution)/shard_map/ppermute | solution.py:21
  91.4 18.3 %collective-permute-start.25 = (bf16[512,256]{1,0:T(8,128)(2,1)S(1)}, bf16[512,256]{1,0:T(8,128)(2,1)S(1)}, u32[]{:S(2)}, u32[]{:S(2)}) collective-permute-start(bf16[512,256]{1,0:T(8,128)(2,1)S(1)} %shard_map.47.refs_0_.kv_ref), channel_id=1, source_target_pairs={{0,20},{4,16},{8,28},{12,24},{1,21},{5,17},{9,29},{13,25},{2,22},{... | collective-permute-start | bytes 786440 | tf_op jit(solution)/shard_map/ppermute | solution.py:21
  97.7 13.3 %collective-permute-start.24 = (bf16[512,256]{1,0:T(8,128)(2,1)S(1)}, bf16[512,256]{1,0:T(8,128)(2,1)S(1)}, u32[]{:S(2)}, u32[]{:S(2)}) collective-permute-start(bf16[512,256]{1,0:T(8,128)(2,1)S(1)} %shard_map.47.refs_0_.kv_ref), channel_id=1, source_target_pairs={{0,16},{4,20},{8,24},{12,28},{1,17},{5,21},{9,25},{13,29},{2,18},{... | collective-permute-start | bytes 786440 | tf_op jit(solution)/shard_map/ppermute | solution.py:21
  101.8 9.9 %collective-permute-start.23 = (bf16[512,256]{1,0:T(8,128)(2,1)S(1)}, bf16[512,256]{1,0:T(8,128)(2,1)S(1)}, u32[]{:S(2)}, u32[]{:S(2)}) collective-permute-start(bf16[512,256]{1,0:T(8,128)(2,1)S(1)} %shard_map.47.refs_0_.kv_ref), channel_id=1, source_target_pairs={{0,4},{4,0},{8,12},{12,8},{16,20},{20,16},{24,28},{28,24},{1,5},{5... | collective-permute-start | bytes 786440 | tf_op jit(solution)/shard_map/ppermute | solution.py:21
  108.1 18.0 %collective-permute-start.22 = (bf16[512,128]{1,0:T(8,128)(2,1)S(1)}, bf16[512,128]{1,0:T(8,128)(2,1)S(1)}, u32[]{:S(2)}, u32[]{:S(2)}) collective-permute-start(bf16[512,128]{1,0:T(8,128)(2,1)S(1)} %shard_map.49.q_ref.refs_0_), channel_id=1, source_target_pairs={{16,4},{20,0},{24,12},{28,8},{17,5},{21,1},{25,13},{29,9},{18,6},{... | collective-permute-start | bytes 393224 | tf_op jit(solution)/shard_map/ppermute | solution.py:21
  109.5 8.0 %collective-permute-start.28 = (bf16[512,256]{1,0:T(8,128)(2,1)S(1)}, bf16[512,256]{1,0:T(8,128)(2,1)S(1)}, u32[]{:S(2)}, u32[]{:S(2)}) collective-permute-start(bf16[512,256]{1,0:T(8,128)(2,1)S(1)} %pad_maximum_fusion.5), channel_id=1, source_target_pairs={{0,4},{4,0},{8,12},{12,8},{16,20},{20,16},{24,28},{28,24},{1,5},{5... | collective-permute-start | bytes 786440 | tf_op jit(solution)/shard_map/ppermute | solution.py:21
  109.7 16.4 %collective-permute-start.21 = (bf16[512,128]{1,0:T(8,128)(2,1)S(1)}, bf16[512,128]{1,0:T(8,128)(2,1)S(1)}, u32[]{:S(2)}, u32[]{:S(2)}) collective-permute-start(bf16[512,128]{1,0:T(8,128)(2,1)S(1)} %shard_map.49.q_ref.refs_0_), channel_id=1, source_target_pairs={{16,0},{20,4},{24,8},{28,12},{17,1},{21,5},{25,9},{29,13},{18,2},{... | collective-permute-start | bytes 393224 | tf_op jit(solution)/shard_map/ppermute | solution.py:21
  114.7 11.5 %collective-permute-start.27 = (f32[8,512]{1,0:T(8,128)S(1)}, f32[8,512]{1,0:T(8,128)S(1)}, u32[]{:S(2)}, u32[]{:S(2)}) collective-permute-start(f32[8,512]{1,0:T(8,128)S(1)} %get-tuple-element.77.refs_4_), channel_id=1, source_target_pairs={{16,4},{20,0},{24,12},{28,8},{17,5},{21,1},{25,13},{29,9},{18,6},{... | collective-permute-start | bytes 49160 | tf_op jit(solution)/shard_map/ppermute | solution.py:21
  115.9 10.2 %collective-permute-start.26 = (f32[8,512]{1,0:T(8,128)S(1)}, f32[8,512]{1,0:T(8,128)S(1)}, u32[]{:S(2)}, u32[]{:S(2)}) collective-permute-start(f32[8,512]{1,0:T(8,128)S(1)} %get-tuple-element.77.refs_4_), channel_id=1, source_target_pairs={{16,0},{20,4},{24,8},{28,12},{17,1},{21,5},{25,9},{29,13},{18,2},{... | collective-permute-start | bytes 49160 | tf_op jit(solution)/shard_map/ppermute | solution.py:21
  117.4 5.8 %collective-permute-start.29 = (f32[8,512]{1,0:T(8,128)S(1)}, f32[8,512]{1,0:T(8,128)S(1)}, u32[]{:S(2)}, u32[]{:S(2)}) collective-permute-start(f32[8,512]{1,0:T(8,128)S(1)} %get-tuple-element.77.refs_4_), channel_id=1, source_target_pairs={{0,4},{4,0},{8,12},{12,8},{16,20},{20,16},{24,28},{28,24},{1,5},{5... | collective-permute-start | bytes 49160 | tf_op jit(solution)/shard_map/ppermute | solution.py:21
  130.2 3.4 %collective-permute-start.37 = (bf16[256,896]{1,0:T(8,128)(2,1)S(1)}, bf16[256,896]{1,0:T(8,128)(2,1)S(1)}, u32[]{:S(2)}, u32[]{:S(2)}) collective-permute-start(bf16[256,896]{1,0:T(8,128)(2,1)S(1)} %convolution_convert_fusion.3), channel_id=1, source_target_pairs={{0,1},{1,0},{2,3},{3,2},{4,5},{5,4},{6,7},{7,6},{8,9},{9,8},{10,11... | collective-permute-start | bytes 1376264 | tf_op jit(solution)/shard_map/ppermute | solution.py:21
  130.3 3.9 %collective-permute-start.33 = (bf16[256,896]{1,0:T(8,128)(2,1)S(1)}, bf16[256,896]{1,0:T(8,128)(2,1)S(1)}, u32[]{:S(2)}, u32[]{:S(2)}) collective-permute-start(bf16[256,896]{1,0:T(8,128)(2,1)S(1)} %convolution_convert_fusion.4), channel_id=1, source_target_pairs={{0,1},{1,0},{2,3},{3,2},{4,5},{5,4},{6,7},{7,6},{8,9},{9,8},{10,11... | collective-permute-start | bytes 1376264 | tf_op jit(solution)/shard_map/ppermute | solution.py:21
  131.5 5.7 %collective-permute-start.31 = (bf16[256,1792]{1,0:T(8,128)(2,1)S(1)}, bf16[256,1792]{1,0:T(8,128)(2,1)S(1)}, u32[]{:S(2)}, u32[]{:S(2)}) collective-permute-start(bf16[256,1792]{1,0:T(8,128)(2,1)S(1)} %convolution_convert_fusion.1), channel_id=1, source_target_pairs={{0,1},{1,0},{2,3},{3,2},{4,5},{5,4},{6,7},{7,6},{8,9},{9,8},{10,11... | collective-permute-start | bytes 2752520 | tf_op jit(solution)/shard_map/ppermute | solution.py:21
  132.3 7.1 %collective-permute-start.36 = (bf16[256,1792]{1,0:T(8,128)(2,1)S(1)}, bf16[256,1792]{1,0:T(8,128)(2,1)S(1)}, u32[]{:S(2)}, u32[]{:S(2)}) collective-permute-start(bf16[256,1792]{1,0:T(8,128)(2,1)S(1)} %convolution_convert_fusion), channel_id=1, source_target_pairs={{0,1},{1,0},{2,3},{3,2},{4,5},{5,4},{6,7},{7,6},{8,9},{9,8},{10,11... | collective-permute-start | bytes 2752520 | tf_op jit(solution)/shard_map/ppermute | solution.py:21
  133.5 18.9 %collective-permute-start.30 = (bf16[256,1792]{1,0:T(8,128)(2,1)S(1)}, bf16[256,1792]{1,0:T(8,128)(2,1)S(1)}, u32[]{:S(2)}, u32[]{:S(2)}) collective-permute-start(bf16[256,1792]{1,0:T(8,128)(2,1)S(1)} %convolution_convert_fusion.2), channel_id=1, source_target_pairs={{0,1},{1,0},{2,3},{3,2},{4,5},{5,4},{6,7},{7,6},{8,9},{9,8},{10,11... | collective-permute-start | bytes 2752520 | tf_op jit(solution)/shard_map/ppermute | solution.py:21
  134.1 16.2 %collective-permute-start.38 = (bf16[256,896]{1,0:T(8,128)(2,1)S(1)}, bf16[256,896]{1,0:T(8,128)(2,1)S(1)}, u32[]{:S(2)}, u32[]{:S(2)}) collective-permute-start(bf16[256,896]{1,0:T(8,128)(2,1)S(1)} %fusion.7), channel_id=1, source_target_pairs={{0,2},{1,3},{2,0},{3,1},{4,6},{5,7},{6,4},{7,5},{8,10},{9,11},{10,... | collective-permute-start | bytes 1376264 | tf_op jit(solution)/shard_map/ppermute | solution.py:21
  134.7 13.8 %collective-permute-start.34 = (bf16[256,896]{1,0:T(8,128)(2,1)S(1)}, bf16[256,896]{1,0:T(8,128)(2,1)S(1)}, u32[]{:S(2)}, u32[]{:S(2)}) collective-permute-start(bf16[256,896]{1,0:T(8,128)(2,1)S(1)} %fusion.6), channel_id=1, source_target_pairs={{0,8},{4,12},{8,0},{12,4},{16,24},{20,28},{24,16},{28,20},{1,9},{5... | collective-permute-start | bytes 1376264 | tf_op jit(solution)/shard_map/ppermute | solution.py:21
  137.9 19.4 %collective-permute-start.32 = (bf16[256,896]{1,0:T(8,128)(2,1)S(1)}, bf16[256,896]{1,0:T(8,128)(2,1)S(1)}, u32[]{:S(2)}, u32[]{:S(2)}) collective-permute-start(bf16[256,896]{1,0:T(8,128)(2,1)S(1)} %slice.113), channel_id=1, source_target_pairs={{0,2},{1,3},{2,0},{3,1},{4,6},{5,7},{6,4},{7,5},{8,10},{9,11},{10,... | collective-permute-start | bytes 1376264 | tf_op jit(solution)/shard_map/ppermute | solution.py:21
  140.2 18.1 %collective-permute-start.40 = (bf16[256,896]{1,0:T(8,128)(2,1)S(1)}, bf16[256,896]{1,0:T(8,128)(2,1)S(1)}, u32[]{:S(2)}, u32[]{:S(2)}) collective-permute-start(bf16[256,896]{1,0:T(8,128)(2,1)S(1)} %slice.112), channel_id=1, source_target_pairs={{0,8},{4,12},{8,0},{12,4},{16,24},{20,28},{24,16},{28,20},{1,9},{5... | collective-permute-start | bytes 1376264 | tf_op jit(solution)/shard_map/ppermute | solution.py:21
  148.6 18.1 %collective-permute-start.35 = (bf16[256,896]{1,0:T(8,128)(2,1)S(1)}, bf16[256,896]{1,0:T(8,128)(2,1)S(1)}, u32[]{:S(2)}, u32[]{:S(2)}) collective-permute-start(bf16[256,896]{1,0:T(8,128)(2,1)S(1)} %fusion.9), channel_id=1, source_target_pairs={{0,2},{1,3},{2,0},{3,1},{4,6},{5,7},{6,4},{7,5},{8,10},{9,11},{10,... | collective-permute-start | bytes 1376264 | tf_op jit(solution)/shard_map/ppermute | solution.py:21
  150.3 17.3 %collective-permute-start.39 = (bf16[256,896]{1,0:T(8,128)(2,1)S(1)}, bf16[256,896]{1,0:T(8,128)(2,1)S(1)}, u32[]{:S(2)}, u32[]{:S(2)}) collective-permute-start(bf16[256,896]{1,0:T(8,128)(2,1)S(1)} %fusion.8), channel_id=1, source_target_pairs={{0,8},{4,12},{8,0},{12,4},{16,24},{20,28},{24,16},{28,20},{1,9},{5... | collective-permute-start | bytes 1376264 | tf_op jit(solution)/shard_map/ppermute | solution.py:21

commit v6 on v5

--- a/solution.py
+++ b/solution.py
@@ -267,14 +267,13 @@
     order["grad"] = jnp.concatenate([order["g0"], order["gpair"]], axis=0)
 
     order.after("q0 qother", f"kv{mids[1]}", f"kv{far ^ 1}")
-    order.after(f"kv{mids[1]}", f"kv{near ^ 1}")
     relay("kv", *mids[1:])
     groups_b = spread("b", [[0]])
     send("q", *mids)
     order["kv_even"] = project("kv", even, "a", groups_a)
     order.after("qother", "kv_even")
     send("q", near)
-    order.after("b0 b1", *[f"kv{d ^ 1}" for d in mids[1:]])
+    order.after("b0 b1", *[f"kv{d ^ 1}" for d in mids[1:]], f"kv{near ^ 1}")
     for _ in bits[1:]:
         groups_b = spread("b", groups_b)
     last = ("b", groups_b) if per_f > depth else ("a", groups_a)

time: 169 us -> 168 us (level)
  starting transfers between devices: 50.4 us -> 48.1 us
    ppermute x41, starting transfers between devices: 50.4 us -> 48.1 us  [swap(): return lax.ppermute(array, axis, pairs)]
  transfers between devices with their start and end apart: 41 -> 41, of which waited for: 15 -> 18; matrix products, arithmetic and copies ran while one was open for 8% -> 8% of each run, Pallas kernels for 10% -> 10%
where the time goes in v6:
time: 168 us
  waiting for transfers between devices  82.8 us (49%)
  starting transfers between devices  48.1 us (29%)
  Pallas kernels  20.7 us (12%)
  local copies, waits for them, and re-layouts  6.58 us (4%)
  matrix products  5.91 us (4%)
  other arithmetic  3.07 us (2%)
    ppermute x41, waiting for transfers between devices, swap(): return lax.ppermute(array, axis, pairs)  82.8 us
    ppermute x41, starting transfers between devices, swap(): return lax.ppermute(array, axis, pairs)  48.1 us
    pallas_call x4, Pallas kernels, project(): local_call(functools.partial(project_kernel, groups, len(ds)), out, 1 + l...  7.42 us
    dot_general x10, matrix products, dot_nt(): lax.dot_general(a, b, (((1,), (1,)), ((), ())), preferred_element_type=F32)  5.91 us
  transfers between devices with their start and end apart: 41, of which 18 were waited for; matrix products, arithmetic and copies ran while one was open for 8% of the time, Pallas kernels for 10%

profile of v6, /device:TPU:0, one launch (start us, length us, event | category | flops | bytes accessed | tf_op | source)
XLA Modules:
  0.0 167.7 jit_solution(12354018614767422655)
XLA Ops:
  0.0 1.4 fusion.37
  1.7 4.1 %collective-permute-start.6 = (bf16[896,256]{1,0:T(8,128)(2,1)S(1)}, bf16[896,256]{1,0:T(8,128)(2,1)S(1)}, u32[]{:S(2)}, u32[]{:S(2)}) collective-permute-start(bf16[896,256]{1,0:T(8,128)(2,1)S(1)} %pad_maximum_fusion.3.refs_3_), channel_id=1, source_target_pairs={{0,16},{4,20},{8,24},{12,28},{16,0},{20,4},{24,8},{28,12},{1,17},{... | collective-permute-start | bytes 1376264 | tf_op jit(solution)/shard_map/ppermute | solution.py:21
  5.8 1.5 collective-permute-start.2
  7.9 1.6 collective-permute-start.1
  9.5 2.2 %constant_dynamic-slice_fusion.1 = (bf16[256,896]{1,0:T(8,128)(2,1)}, bf16[256,896]{1,0:T(8,128)(2,1)}) fusion(bf16[256,7168]{1,0:T(8,128)(2,1)} %own_ref.7, s32[]{:T(128)S(6)} %select_n.158, s32[]{:T(128)S(6)} %select_n.157), kind=kLoop, calls=%fused_computation.84 | loop fusion | bytes 1835016 | tf_op jit(solution)/shard_map/dynamic_slice | solution.py:202
  13.0 1.6 collective-permute-start.10
  14.8 2.9 %collective-permute-done.2.refs_3_ = bf16[896,256]{1,0:T(8,128)(2,1)S(1)} collective-permute-done((bf16[896,256]{1,0:T(8,128)(2,1)S(1)}, bf16[896,256]{1,0:T(8,128)(2,1)S(1)}, u32[]{:S(2)}, u32[]{:S(2)}) %collective-permute-start.2) | collective-permute-done | bytes 458784 | tf_op jit(solution)/shard_map/ppermute | solution.py:21
  17.7 1.5 collective-permute-start.3
  19.4 14.6 %collective-permute-done.refs_0_ = bf16[256,896]{1,0:T(8,128)(2,1)S(1)} collective-permute-done((bf16[256,896]{1,0:T(8,128)(2,1)}, bf16[256,896]{1,0:T(8,128)(2,1)S(1)}, u32[]{:S(2)}, u32[]{:S(2)}) %collective-permute-start) | collective-permute-done | bytes 458784 | tf_op jit(solution)/shard_map/ppermute | solution.py:21
  34.0 1.5 collective-permute-start.13
  37.1 1.3 collective-permute-start.7
  38.9 3.6 %collective-permute-done.13.refs_1_ = bf16[256,896]{1,0:T(8,128)(2,1)S(1)} collective-permute-done((bf16[256,896]{1,0:T(8,128)(2,1)S(1)}, bf16[256,896]{1,0:T(8,128)(2,1)S(1)}, u32[]{:S(2)}, u32[]{:S(2)}) %collective-permute-start.13) | collective-permute-done | bytes 458784 | tf_op jit(solution)/shard_map/ppermute | solution.py:21
  42.9 10.8 %collective-permute-done.10.refs_4_ = bf16[896,256]{1,0:T(8,128)(2,1)S(1)} collective-permute-done((bf16[896,256]{1,0:T(8,128)(2,1)}, bf16[896,256]{1,0:T(8,128)(2,1)S(1)}, u32[]{:S(2)}, u32[]{:S(2)}) %collective-permute-start.10) | collective-permute-done | bytes 458784 | tf_op jit(solution)/shard_map/ppermute | solution.py:21
  54.2 1.5 collective-permute-start.9
  55.7 5.8 %collective-permute-done.4.refs_0_ = bf16[256,896]{1,0:T(8,128)(2,1)S(1)} collective-permute-done((bf16[256,896]{1,0:T(8,128)(2,1)}, bf16[256,896]{1,0:T(8,128)(2,1)S(1)}, u32[]{:S(2)}, u32[]{:S(2)}) %collective-permute-start.4) | collective-permute-done | bytes 458784 | tf_op jit(solution)/shard_map/ppermute | solution.py:21
  61.5 1.5 collective-permute-start.5
  63.2 1.4 collective-permute-start.16
  64.5 4.4 %collective-permute-done.9.refs_6_ = bf16[896,256]{1,0:T(8,128)(2,1)S(1)} collective-permute-done((bf16[896,256]{1,0:T(8,128)(2,1)S(1)}, bf16[896,256]{1,0:T(8,128)(2,1)S(1)}, u32[]{:S(2)}, u32[]{:S(2)}) %collective-permute-start.9) | collective-permute-done | bytes 458784 | tf_op jit(solution)/shard_map/ppermute | solution.py:21
  68.9 3.1 %collective-permute-done.5.refs_1_ = bf16[256,896]{1,0:T(8,128)(2,1)S(1)} collective-permute-done((bf16[256,896]{1,0:T(8,128)(2,1)S(1)}, bf16[256,896]{1,0:T(8,128)(2,1)S(1)}, u32[]{:S(2)}, u32[]{:S(2)}) %collective-permute-start.5) | collective-permute-done | bytes 458784 | tf_op jit(solution)/shard_map/ppermute | solution.py:21
  72.0 1.9 %shard_map.46.refs_7_ = f32[512,256]{1,0:T(8,128)S(1)} custom-call(s32[2,4]{1,0:T(2,128)S(1)} %pad_add_fusion.1.place_ref, bf16[256,7168]{1,0:T(8,128)(2,1)S(1)} %copy-done.1, bf16[256,896]{1,0:T(8,128)(2,1)S(1)} %collective-permute-done.refs_0_, bf16[256,896]{1,0:T(8,128)(2,1)S(1)} %collective-permute-done.13.refs_1_, ...), custom_call_target="tpu_custom_call" | custom-call | flops 1 | bytes 1 | tf_op jit(solution)/shard_map/pallas_call | solution.py:228
  74.2 8.5 %collective-permute-done.15.refs_5_ = bf16[896,128]{1,0:T(8,128)(2,1)S(1)} collective-permute-done((bf16[896,128]{1,0:T(8,128)(2,1)S(1)}, bf16[896,128]{1,0:T(8,128)(2,1)S(1)}, u32[]{:S(2)}, u32[]{:S(2)}) %collective-permute-start.15) | collective-permute-done | bytes 229408 | tf_op jit(solution)/shard_map/ppermute | solution.py:21
  85.4 1.9 %shard_map.47.refs_0_.kv_ref = bf16[512,256]{1,0:T(8,128)(2,1)S(1)} custom-call(s32[2,4]{1,0:T(2,128)S(1)} %pad_add_fusion.place_ref, bf16[256,7168]{1,0:T(8,128)(2,1)S(1)} %copy-done.1, bf16[256,896]{1,0:T(8,128)(2,1)S(1)} %collective-permute-done.4.refs_0_, bf16[256,896]{1,0:T(8,128)(2,1)S(1)} %collective-permute-done.5.refs_1_, ...), custom_call_target="tpu_custom_call" | custom-call | flops 1 | bytes 1 | tf_op jit(solution)/shard_map/pallas_call | solution.py:228
  87.3 1.3 collective-permute-start.20
  88.6 1.3 collective-permute-start.19
  90.0 6.4 %collective-permute-start.25 = (bf16[512,256]{1,0:T(8,128)(2,1)S(1)}, bf16[512,256]{1,0:T(8,128)(2,1)S(1)}, u32[]{:S(2)}, u32[]{:S(2)}) collective-permute-start(bf16[512,256]{1,0:T(8,128)(2,1)S(1)} %shard_map.47.refs_0_.kv_ref), channel_id=1, source_target_pairs={{0,20},{4,16},{8,28},{12,24},{1,21},{5,17},{9,29},{13,25},{2,22},{... | collective-permute-start | bytes 786440 | tf_op jit(solution)/shard_map/ppermute | solution.py:21
  96.4 1.3 collective-permute-start.24
  97.7 1.8 %collective-permute-done.19.refs_3_ = bf16[512,128]{1,0:T(8,128)(2,1)S(1)} collective-permute-done((bf16[512,128]{1,0:T(8,128)(2,1)S(1)}, bf16[512,128]{1,0:T(8,128)(2,1)S(1)}, u32[]{:S(2)}, u32[]{:S(2)}) %collective-permute-start.19) | collective-permute-done | bytes 131104 | tf_op jit(solution)/shard_map/ppermute | solution.py:21
  99.5 1.4 collective-permute-done.18
  102.1 1.8 %shard_map.48.refs_7_ = f32[512,128]{1,0:T(8,128)S(1)} custom-call(s32[2,4]{1,0:T(2,128)S(1)} %pad_add_fusion.1.place_ref, bf16[256,7168]{1,0:T(8,128)(2,1)S(1)} %copy-done.1, bf16[256,896]{1,0:T(8,128)(2,1)S(1)} %collective-permute-done.refs_0_, bf16[256,896]{1,0:T(8,128)(2,1)S(1)} %collective-permute-done.13.refs_1_, ...), custom_call_target="tpu_custom_call" | custom-call | flops 1 | bytes 1 | tf_op jit(solution)/shard_map/pallas_call | solution.py:228
  103.9 1.8 %shard_map.49.q_ref.refs_0_ = bf16[512,128]{1,0:T(8,128)(2,1)S(1)} custom-call(s32[2,4]{1,0:T(2,128)S(1)} %pad_add_fusion.place_ref, bf16[256,7168]{1,0:T(8,128)(2,1)S(1)} %copy-done.1, bf16[256,896]{1,0:T(8,128)(2,1)S(1)} %collective-permute-done.4.refs_0_, bf16[256,896]{1,0:T(8,128)(2,1)S(1)} %collective-permute-done.5.refs_1_, ...), custom_call_target="tpu_custom_call" | custom-call | flops 1 | bytes 1 | tf_op jit(solution)/shard_map/pallas_call | solution.py:228
  105.7 1.3 collective-permute-start.22
  108.5 1.3 collective-permute-start.21
  109.8 1.6 collective-permute-done.23.refs_1_
  111.4 2.9 %shard_map.50 = (f32[8,512]{1,0:T(8,128)S(1)}, f32[512,128]{1,0:T(8,128)S(1)}) custom-call(s32[2,8]{1,0:T(2,128)S(1)} %get-tuple-element.100.limit_ref, bf16[512,128]{1,0:T(8,128)(2,1)S(1)} %shard_map.49.q_ref.refs_0_, bf16[512,128]{1,0:T(8,128)(2,1)S(1)} %pad_maximum_fusion.7.grad_ref.refs_2_, bf16[512,256]{1,0:T(8,128)(2,1)S(1)} %shard_map.47.refs_0_.kv_ref, ...), custom_call_target="tpu_custom_call" | custom-call | flops 1 | bytes 1 | tf_op jit(solution)/shard_map/pallas_call | solution.py:323
  114.4 1.3 collective-permute-start.27
  115.7 1.5 collective-permute-start.26
  117.2 3.2 %shard_map.53 = bf16[512,128]{1,0:T(8,128)(2,1)S(1)} custom-call(s32[2,8]{1,0:T(2,128)S(1)} %get-tuple-element.100.limit_ref, bf16[512,128]{1,0:T(8,128)(2,1)S(1)} %shard_map.49.q_ref.refs_0_, bf16[512,128]{1,0:T(8,128)(2,1)S(1)} %pad_maximum_fusion.7.grad_ref.refs_2_, f32[512,128]{1,0:T(8,128)S(1)} %get-tuple-element.76.column_ref, ...), custom_call_target="tpu_custom_call" | custom-call | flops 1 | bytes 1 | tf_op jit(solution)/shard_map/pallas_call | solution.py:336
  120.9 2.9 %shard_map.51.refs_6_ = f32[512,256]{1,0:T(8,128)S(1)} custom-call(s32[2,4]{1,0:T(2,128)S(1)} %get-tuple-element.98.limit_ref, bf16[512,256]{1,0:T(8,128)(2,1)S(1)} %shard_map.47.refs_0_.kv_ref, bf16[512,128]{1,0:T(8,128)(2,1)S(1)} %shard_map.49.q_ref.refs_0_, bf16[512,128]{1,0:T(8,128)(2,1)S(1)} %get-tuple-element.95.refs_1_, ...), custom_call_target="tpu_custom_call" | custom-call | flops 1 | bytes 1 | tf_op jit(solution)/shard_map/pallas_call | solution.py:342
  123.8 3.1 %shard_map.52 = bf16[512,256]{1,0:T(8,128)(2,1)S(1)} custom-call(s32[2,4]{1,0:T(2,128)S(1)} %get-tuple-element.99.limit_ref, bf16[512,256]{1,0:T(8,128)(2,1)S(1)} %shard_map.47.refs_0_.kv_ref, bf16[512,128]{1,0:T(8,128)(2,1)S(1)} %collective-permute-done.21.refs_0_, bf16[512,128]{1,0:T(8,128)(2,1)S(1)} %collective-permute-done.22.refs_1_, ...), custom_call_target="tpu_custom_call" | custom-call | flops 1 | bytes 1 | tf_op jit(solution)/shard_map/pallas_call | solution.py:348
  133.2 2.9 %collective-permute-start.34 = (bf16[256,896]{1,0:T(8,128)(2,1)S(1)}, bf16[256,896]{1,0:T(8,128)(2,1)S(1)}, u32[]{:S(2)}, u32[]{:S(2)}) collective-permute-start(bf16[256,896]{1,0:T(8,128)(2,1)S(1)} %fusion.6), channel_id=1, source_target_pairs={{0,8},{4,12},{8,0},{12,4},{16,24},{20,28},{24,16},{28,20},{1,9},{5... | collective-permute-start | bytes 1376264 | tf_op jit(solution)/shard_map/ppermute | solution.py:21
  136.8 1.6 collective-permute-start.32
  139.2 8.2 %collective-permute-done.34 = bf16[256,896]{1,0:T(8,128)(2,1)S(1)} collective-permute-done((bf16[256,896]{1,0:T(8,128)(2,1)S(1)}, bf16[256,896]{1,0:T(8,128)(2,1)S(1)}, u32[]{:S(2)}, u32[]{:S(2)}) %collective-permute-start.34) | collective-permute-done | bytes 458784 | tf_op jit(solution)/shard_map/ppermute | solution.py:21
  147.4 1.6 collective-permute-start.35
  149.1 2.1 %collective-permute-start.39 = (bf16[256,896]{1,0:T(8,128)(2,1)S(1)}, bf16[256,896]{1,0:T(8,128)(2,1)S(1)}, u32[]{:S(2)}, u32[]{:S(2)}) collective-permute-start(bf16[256,896]{1,0:T(8,128)(2,1)S(1)} %fusion.8), channel_id=1, source_target_pairs={{0,8},{4,12},{8,0},{12,4},{16,24},{20,28},{24,16},{28,20},{1,9},{5... | collective-permute-start | bytes 1376264 | tf_op jit(solution)/shard_map/ppermute | solution.py:21
  151.9 3.1 %collective-permute-done.32.x_a = bf16[256,896]{1,0:T(8,128)(2,1)S(1)} collective-permute-done((bf16[256,896]{1,0:T(8,128)(2,1)S(1)}, bf16[256,896]{1,0:T(8,128)(2,1)S(1)}, u32[]{:S(2)}, u32[]{:S(2)}) %collective-permute-start.32) | collective-permute-done | bytes 458784 | tf_op jit(solution)/shard_map/ppermute | solution.py:21
  155.0 2.1 %collective-permute-done.40.z_b = bf16[256,896]{1,0:T(8,128)(2,1)S(1)} collective-permute-done((bf16[256,896]{1,0:T(8,128)(2,1)S(1)}, bf16[256,896]{1,0:T(8,128)(2,1)S(1)}, u32[]{:S(2)}, u32[]{:S(2)}) %collective-permute-start.40) | collective-permute-done | bytes 458784 | tf_op jit(solution)/shard_map/ppermute | solution.py:21
  157.1 7.2 %collective-permute-done.35.x_b = bf16[256,896]{1,0:T(8,128)(2,1)S(1)} collective-permute-done((bf16[256,896]{1,0:T(8,128)(2,1)S(1)}, bf16[256,896]{1,0:T(8,128)(2,1)S(1)}, u32[]{:S(2)}, u32[]{:S(2)}) %collective-permute-start.35) | collective-permute-done | bytes 458784 | tf_op jit(solution)/shard_map/ppermute | solution.py:21
  164.4 2.1 %collective-permute-done.39.z_a = bf16[256,896]{1,0:T(8,128)(2,1)S(1)} collective-permute-done((bf16[256,896]{1,0:T(8,128)(2,1)S(1)}, bf16[256,896]{1,0:T(8,128)(2,1)S(1)}, u32[]{:S(2)}, u32[]{:S(2)}) %collective-permute-start.39) | collective-permute-done | bytes 458784 | tf_op jit(solution)/shard_map/ppermute | solution.py:21
  (115 shorter events, 21.6 us)
Async XLA Ops:
  0.0 35.7 %copy-start = (s32[4,4]{1,0:T(4,128)S(1)}, s32[4,4]{1,0:T(4,128)}, u32[]{:S(2)}) copy-start(s32[4,4]{1,0:T(4,128)} %param.6) | copy-start | bytes 196
  1.4 5.9 %copy-start.2 = (bf16[256,256]{1,0:T(8,128)(2,1)S(1)}, bf16[256,256]{1,0:T(8,128)(2,1)}, u32[]{:S(2)}) copy-start(bf16[256,256]{1,0:T(8,128)(2,1)} %param.7) | copy-start | bytes 393220
  1.7 35.4 %collective-permute-start.6 = (bf16[896,256]{1,0:T(8,128)(2,1)S(1)}, bf16[896,256]{1,0:T(8,128)(2,1)S(1)}, u32[]{:S(2)}, u32[]{:S(2)}) collective-permute-start(bf16[896,256]{1,0:T(8,128)(2,1)S(1)} %pad_maximum_fusion.3.refs_3_), channel_id=1, source_target_pairs={{0,16},{4,20},{8,24},{12,28},{16,0},{20,4},{24,8},{28,12},{1,17},{... | collective-permute-start | bytes 1376264 | tf_op jit(solution)/shard_map/ppermute | solution.py:21
  5.8 12.0 %collective-permute-start.2 = (bf16[896,256]{1,0:T(8,128)(2,1)S(1)}, bf16[896,256]{1,0:T(8,128)(2,1)S(1)}, u32[]{:S(2)}, u32[]{:S(2)}) collective-permute-start(bf16[896,256]{1,0:T(8,128)(2,1)S(1)} %pad_maximum_fusion.3.refs_3_), channel_id=1, source_target_pairs={{0,4},{4,0},{8,12},{12,8},{16,20},{20,16},{24,28},{28,24},{1,5},{5... | collective-permute-start | bytes 1376264 | tf_op jit(solution)/shard_map/ppermute | solution.py:21
  7.9 11.5 %collective-permute-start.1 = (bf16[256,128]{1,0:T(8,128)(2,1)}, bf16[256,128]{1,0:T(8,128)(2,1)}, u32[]{:S(2)}, u32[]{:S(2)}) collective-permute-start(bf16[256,128]{1,0:T(8,128)(2,1)} %get-tuple-element.97), channel_id=1, source_target_pairs={{0,8},{4,12},{8,0},{12,4},{16,24},{20,28},{24,16},{28,20},{1,9},{5... | collective-permute-start | bytes 196616 | tf_op jit(solution)/shard_map/ppermute | solution.py:21
  11.7 22.3 %collective-permute-start = (bf16[256,896]{1,0:T(8,128)(2,1)}, bf16[256,896]{1,0:T(8,128)(2,1)S(1)}, u32[]{:S(2)}, u32[]{:S(2)}) collective-permute-start(bf16[256,896]{1,0:T(8,128)(2,1)} %get-tuple-element.77), channel_id=1, source_target_pairs={{0,8},{4,12},{8,0},{12,4},{16,24},{20,28},{24,16},{28,20},{1,9},{5... | collective-permute-start | bytes 1376264 | tf_op jit(solution)/shard_map/ppermute | solution.py:21
  13.0 40.7 %collective-permute-start.10 = (bf16[896,256]{1,0:T(8,128)(2,1)}, bf16[896,256]{1,0:T(8,128)(2,1)S(1)}, u32[]{:S(2)}, u32[]{:S(2)}) collective-permute-start(bf16[896,256]{1,0:T(8,128)(2,1)} %pad_maximum_fusion.4), channel_id=1, source_target_pairs={{0,8},{4,12},{8,0},{12,4},{16,24},{20,28},{24,16},{28,20},{1,9},{5... | collective-permute-start | bytes 1376264 | tf_op jit(solution)/shard_map/ppermute | solution.py:21
  17.7 16.3 %collective-permute-start.3 = (bf16[896,128]{1,0:T(8,128)(2,1)S(1)}, bf16[896,128]{1,0:T(8,128)(2,1)S(1)}, u32[]{:S(2)}, u32[]{:S(2)}) collective-permute-start(bf16[896,128]{1,0:T(8,128)(2,1)S(1)} %get-tuple-element.66.refs_3_), channel_id=1, source_target_pairs={{0,4},{4,0},{8,12},{12,8},{16,20},{20,16},{24,28},{28,24},{1,5},{5... | collective-permute-start | bytes 688136 | tf_op jit(solution)/shard_map/ppermute | solution.py:21
  34.0 8.5 %collective-permute-start.13 = (bf16[256,896]{1,0:T(8,128)(2,1)S(1)}, bf16[256,896]{1,0:T(8,128)(2,1)S(1)}, u32[]{:S(2)}, u32[]{:S(2)}) collective-permute-start(bf16[256,896]{1,0:T(8,128)(2,1)S(1)} %collective-permute-done.refs_0_), channel_id=1, source_target_pairs={{0,2},{1,3},{2,0},{3,1},{4,6},{5,7},{6,4},{7,5},{8,10},{9,11},{10,... | collective-permute-start | bytes 1376264 | tf_op jit(solution)/shard_map/ppermute | solution.py:21
  37.1 34.9 %copy-start.1 = (bf16[256,7168]{1,0:T(8,128)(2,1)S(1)}, bf16[256,7168]{1,0:T(8,128)(2,1)}, u32[]{:S(2)}) copy-start(bf16[256,7168]{1,0:T(8,128)(2,1)} %own_ref.7) | copy-start | bytes 11010052
  37.1 17.1 %collective-permute-start.7 = (bf16[896,256]{1,0:T(8,128)(2,1)}, bf16[896,256]{1,0:T(8,128)(2,1)S(1)}, u32[]{:S(2)}, u32[]{:S(2)}) collective-permute-start(bf16[896,256]{1,0:T(8,128)(2,1)} %pad_maximum_fusion.4), channel_id=1, source_target_pairs={{0,24},{4,28},{8,16},{12,20},{16,8},{20,12},{24,0},{28,4},{1,25},{... | collective-permute-start | bytes 1376264 | tf_op jit(solution)/shard_map/ppermute | solution.py:21
  38.4 15.8 %collective-permute-start.8 = (bf16[896,256]{1,0:T(8,128)(2,1)S(1)}, bf16[896,256]{1,0:T(8,128)(2,1)S(1)}, u32[]{:S(2)}, u32[]{:S(2)}) collective-permute-start(bf16[896,256]{1,0:T(8,128)(2,1)S(1)} %collective-permute-done.6.refs_5_), channel_id=1, source_target_pairs={{0,4},{4,0},{8,12},{12,8},{16,20},{20,16},{24,28},{28,24},{1,5},{5... | collective-permute-start | bytes 1376264 | tf_op jit(solution)/shard_map/ppermute | solution.py:21
  38.9 22.6 %collective-permute-start.4 = (bf16[256,896]{1,0:T(8,128)(2,1)}, bf16[256,896]{1,0:T(8,128)(2,1)S(1)}, u32[]{:S(2)}, u32[]{:S(2)}) collective-permute-start(bf16[256,896]{1,0:T(8,128)(2,1)} %get-tuple-element.43), channel_id=1, source_target_pairs={{0,8},{4,12},{8,0},{12,4},{16,24},{20,28},{24,16},{28,20},{1,9},{5... | collective-permute-start | bytes 1376264 | tf_op jit(solution)/shard_map/ppermute | solution.py:21
  42.6 29.4 %collective-permute-start.14 = (bf16[512,896]{1,0:T(8,128)(2,1)S(1)}, bf16[512,896]{1,0:T(8,128)(2,1)S(1)}, u32[]{:S(2)}, u32[]{:S(2)}) collective-permute-start(bf16[512,896]{1,0:T(8,128)(2,1)S(1)} %pad_maximum_fusion.1), channel_id=1, source_target_pairs={{0,1},{1,0},{2,3},{3,2},{4,5},{5,4},{6,7},{7,6},{8,9},{9,8},{10,11... | collective-permute-start | bytes 2752520 | tf_op jit(solution)/shard_map/ppermute | solution.py:21
  53.7 10.8 %collective-permute-start.11 = (bf16[896,256]{1,0:T(8,128)(2,1)S(1)}, bf16[896,256]{1,0:T(8,128)(2,1)S(1)}, u32[]{:S(2)}, u32[]{:S(2)}) collective-permute-start(bf16[896,256]{1,0:T(8,128)(2,1)S(1)} %collective-permute-done.10.refs_4_), channel_id=1, source_target_pairs={{0,4},{4,0},{8,12},{12,8},{16,20},{20,16},{24,28},{28,24},{1,5},{5... | collective-permute-start | bytes 1376264 | tf_op jit(solution)/shard_map/ppermute | solution.py:21
  54.2 14.7 %collective-permute-start.9 = (bf16[896,256]{1,0:T(8,128)(2,1)S(1)}, bf16[896,256]{1,0:T(8,128)(2,1)S(1)}, u32[]{:S(2)}, u32[]{:S(2)}) collective-permute-start(bf16[896,256]{1,0:T(8,128)(2,1)S(1)} %collective-permute-done.7.refs_6_), channel_id=1, source_target_pairs={{0,4},{4,0},{8,12},{12,8},{16,20},{20,16},{24,28},{28,24},{1,5},{5... | collective-permute-start | bytes 1376264 | tf_op jit(solution)/shard_map/ppermute | solution.py:21
  61.5 10.5 %collective-permute-start.5 = (bf16[256,896]{1,0:T(8,128)(2,1)S(1)}, bf16[256,896]{1,0:T(8,128)(2,1)S(1)}, u32[]{:S(2)}, u32[]{:S(2)}) collective-permute-start(bf16[256,896]{1,0:T(8,128)(2,1)S(1)} %collective-permute-done.4.refs_0_), channel_id=1, source_target_pairs={{0,2},{1,3},{2,0},{3,1},{4,6},{5,7},{6,4},{7,5},{8,10},{9,11},{10,... | collective-permute-start | bytes 1376264 | tf_op jit(solution)/shard_map/ppermute | solution.py:21
  63.2 11.0 %collective-permute-start.16 = (bf16[896,128]{1,0:T(8,128)(2,1)S(1)}, bf16[896,128]{1,0:T(8,128)(2,1)S(1)}, u32[]{:S(2)}, u32[]{:S(2)}) collective-permute-start(bf16[896,128]{1,0:T(8,128)(2,1)S(1)} %get-tuple-element.60), channel_id=1, source_target_pairs={{0,24},{4,28},{8,16},{12,20},{16,8},{20,12},{24,0},{28,4},{1,25},{... | collective-permute-start | bytes 688136 | tf_op jit(solution)/shard_map/ppermute | solution.py:21
  64.5 18.2 %collective-permute-start.15 = (bf16[896,128]{1,0:T(8,128)(2,1)S(1)}, bf16[896,128]{1,0:T(8,128)(2,1)S(1)}, u32[]{:S(2)}, u32[]{:S(2)}) collective-permute-start(bf16[896,128]{1,0:T(8,128)(2,1)S(1)} %get-tuple-element.66.refs_3_), channel_id=1, source_target_pairs={{0,16},{4,20},{8,24},{12,28},{16,0},{20,4},{24,8},{28,12},{1,17},{... | collective-permute-start | bytes 688136 | tf_op jit(solution)/shard_map/ppermute | solution.py:21
  73.9 9.9 %collective-permute-start.17 = (bf16[896,128]{1,0:T(8,128)(2,1)S(1)}, bf16[896,128]{1,0:T(8,128)(2,1)S(1)}, u32[]{:S(2)}, u32[]{:S(2)}) collective-permute-start(bf16[896,128]{1,0:T(8,128)(2,1)S(1)} %get-tuple-element.60), channel_id=1, source_target_pairs={{0,8},{4,12},{8,0},{12,4},{16,24},{20,28},{24,16},{28,20},{1,9},{5... | collective-permute-start | bytes 688136 | tf_op jit(solution)/shard_map/ppermute | solution.py:21
  74.0 11.3 %collective-permute-start.12 = (bf16[512,896]{1,0:T(8,128)(2,1)S(1)}, bf16[512,896]{1,0:T(8,128)(2,1)S(1)}, u32[]{:S(2)}, u32[]{:S(2)}) collective-permute-start(bf16[512,896]{1,0:T(8,128)(2,1)S(1)} %pad_maximum_fusion), channel_id=1, source_target_pairs={{0,1},{1,0},{2,3},{3,2},{4,5},{5,4},{6,7},{7,6},{8,9},{9,8},{10,11... | collective-permute-start | bytes 2752520 | tf_op jit(solution)/shard_map/ppermute | solution.py:21
  83.8 17.1 %collective-permute-start.18 = (bf16[2688,128]{1,0:T(8,128)(2,1)S(1)}, bf16[2688,128]{1,0:T(8,128)(2,1)S(1)}, u32[]{:S(2)}, u32[]{:S(2)}) collective-permute-start(bf16[2688,128]{1,0:T(8,128)(2,1)S(1)} %pad_maximum_fusion.2), channel_id=1, source_target_pairs={{0,4},{4,0},{8,12},{12,8},{16,20},{20,16},{24,28},{28,24},{1,5},{5... | collective-permute-start | bytes 2064392 | tf_op jit(solution)/shard_map/ppermute | solution.py:21
  87.3 10.4 %collective-permute-start.20 = (bf16[512,128]{1,0:T(8,128)(2,1)S(1)}, bf16[512,128]{1,0:T(8,128)(2,1)S(1)}, u32[]{:S(2)}, u32[]{:S(2)}) collective-permute-start(bf16[512,128]{1,0:T(8,128)(2,1)S(1)} %pad_maximum_fusion.7.grad_ref.refs_2_), channel_id=1, source_target_pairs={{16,0},{20,4},{24,8},{28,12},{17,1},{21,5},{25,9},{29,13},{18,2},{... | collective-permute-start | bytes 393224 | tf_op jit(solution)/shard_map/ppermute | solution.py:21
  88.6 10.9 %collective-permute-start.19 = (bf16[512,128]{1,0:T(8,128)(2,1)S(1)}, bf16[512,128]{1,0:T(8,128)(2,1)S(1)}, u32[]{:S(2)}, u32[]{:S(2)}) collective-permute-start(bf16[512,128]{1,0:T(8,128)(2,1)S(1)} %pad_maximum_fusion.7.grad_ref.refs_2_), channel_id=1, source_target_pairs={{16,4},{20,0},{24,12},{28,8},{17,5},{21,1},{25,13},{29,9},{18,6},{... | collective-permute-start | bytes 393224 | tf_op jit(solution)/shard_map/ppermute | solution.py:21
  90.0 18.5 %collective-permute-start.25 = (bf16[512,256]{1,0:T(8,128)(2,1)S(1)}, bf16[512,256]{1,0:T(8,128)(2,1)S(1)}, u32[]{:S(2)}, u32[]{:S(2)}) collective-permute-start(bf16[512,256]{1,0:T(8,128)(2,1)S(1)} %shard_map.47.refs_0_.kv_ref), channel_id=1, source_target_pairs={{0,20},{4,16},{8,28},{12,24},{1,21},{5,17},{9,29},{13,25},{2,22},{... | collective-permute-start | bytes 786440 | tf_op jit(solution)/shard_map/ppermute | solution.py:21
  96.4 13.4 %collective-permute-start.24 = (bf16[512,256]{1,0:T(8,128)(2,1)S(1)}, bf16[512,256]{1,0:T(8,128)(2,1)S(1)}, u32[]{:S(2)}, u32[]{:S(2)}) collective-permute-start(bf16[512,256]{1,0:T(8,128)(2,1)S(1)} %shard_map.47.refs_0_.kv_ref), channel_id=1, source_target_pairs={{0,16},{4,20},{8,24},{12,28},{1,17},{5,21},{9,25},{13,29},{2,18},{... | collective-permute-start | bytes 786440 | tf_op jit(solution)/shard_map/ppermute | solution.py:21
  100.9 10.5 %collective-permute-start.23 = (bf16[512,256]{1,0:T(8,128)(2,1)S(1)}, bf16[512,256]{1,0:T(8,128)(2,1)S(1)}, u32[]{:S(2)}, u32[]{:S(2)}) collective-permute-start(bf16[512,256]{1,0:T(8,128)(2,1)S(1)} %shard_map.47.refs_0_.kv_ref), channel_id=1, source_target_pairs={{0,4},{4,0},{8,12},{12,8},{16,20},{20,16},{24,28},{28,24},{1,5},{5... | collective-permute-start | bytes 786440 | tf_op jit(solution)/shard_map/ppermute | solution.py:21
  105.7 18.1 %collective-permute-start.22 = (bf16[512,128]{1,0:T(8,128)(2,1)S(1)}, bf16[512,128]{1,0:T(8,128)(2,1)S(1)}, u32[]{:S(2)}, u32[]{:S(2)}) collective-permute-start(bf16[512,128]{1,0:T(8,128)(2,1)S(1)} %shard_map.49.q_ref.refs_0_), channel_id=1, source_target_pairs={{16,4},{20,0},{24,12},{28,8},{17,5},{21,1},{25,13},{29,9},{18,6},{... | collective-permute-start | bytes 393224 | tf_op jit(solution)/shard_map/ppermute | solution.py:21
  107.0 10.1 %collective-permute-start.28 = (bf16[512,256]{1,0:T(8,128)(2,1)S(1)}, bf16[512,256]{1,0:T(8,128)(2,1)S(1)}, u32[]{:S(2)}, u32[]{:S(2)}) collective-permute-start(bf16[512,256]{1,0:T(8,128)(2,1)S(1)} %pad_maximum_fusion.5), channel_id=1, source_target_pairs={{0,4},{4,0},{8,12},{12,8},{16,20},{20,16},{24,28},{28,24},{1,5},{5... | collective-permute-start | bytes 786440 | tf_op jit(solution)/shard_map/ppermute | solution.py:21
  108.5 15.4 %collective-permute-start.21 = (bf16[512,128]{1,0:T(8,128)(2,1)S(1)}, bf16[512,128]{1,0:T(8,128)(2,1)S(1)}, u32[]{:S(2)}, u32[]{:S(2)}) collective-permute-start(bf16[512,128]{1,0:T(8,128)(2,1)S(1)} %shard_map.49.q_ref.refs_0_), channel_id=1, source_target_pairs={{16,0},{20,4},{24,8},{28,12},{17,1},{21,5},{25,9},{29,13},{18,2},{... | collective-permute-start | bytes 393224 | tf_op jit(solution)/shard_map/ppermute | solution.py:21
  114.4 9.5 %collective-permute-start.27 = (f32[8,512]{1,0:T(8,128)S(1)}, f32[8,512]{1,0:T(8,128)S(1)}, u32[]{:S(2)}, u32[]{:S(2)}) collective-permute-start(f32[8,512]{1,0:T(8,128)S(1)} %get-tuple-element.75.refs_4_), channel_id=1, source_target_pairs={{16,4},{20,0},{24,12},{28,8},{17,5},{21,1},{25,13},{29,9},{18,6},{... | collective-permute-start | bytes 49160 | tf_op jit(solution)/shard_map/ppermute | solution.py:21
  115.7 8.2 %collective-permute-start.26 = (f32[8,512]{1,0:T(8,128)S(1)}, f32[8,512]{1,0:T(8,128)S(1)}, u32[]{:S(2)}, u32[]{:S(2)}) collective-permute-start(f32[8,512]{1,0:T(8,128)S(1)} %get-tuple-element.75.refs_4_), channel_id=1, source_target_pairs={{16,0},{20,4},{24,8},{28,12},{17,1},{21,5},{25,9},{29,13},{18,2},{... | collective-permute-start | bytes 49160 | tf_op jit(solution)/shard_map/ppermute | solution.py:21
  117.1 3.8 %collective-permute-start.29 = (f32[8,512]{1,0:T(8,128)S(1)}, f32[8,512]{1,0:T(8,128)S(1)}, u32[]{:S(2)}, u32[]{:S(2)}) collective-permute-start(f32[8,512]{1,0:T(8,128)S(1)} %get-tuple-element.75.refs_4_), channel_id=1, source_target_pairs={{0,4},{4,0},{8,12},{12,8},{16,20},{20,16},{24,28},{28,24},{1,5},{5... | collective-permute-start | bytes 49160 | tf_op jit(solution)/shard_map/ppermute | solution.py:21
  127.9 3.4 %collective-permute-start.37 = (bf16[256,896]{1,0:T(8,128)(2,1)S(1)}, bf16[256,896]{1,0:T(8,128)(2,1)S(1)}, u32[]{:S(2)}, u32[]{:S(2)}) collective-permute-start(bf16[256,896]{1,0:T(8,128)(2,1)S(1)} %convolution_convert_fusion.3), channel_id=1, source_target_pairs={{0,1},{1,0},{2,3},{3,2},{4,5},{5,4},{6,7},{7,6},{8,9},{9,8},{10,11... | collective-permute-start | bytes 1376264 | tf_op jit(solution)/shard_map/ppermute | solution.py:21
  128.0 4.7 %collective-permute-start.33 = (bf16[256,896]{1,0:T(8,128)(2,1)S(1)}, bf16[256,896]{1,0:T(8,128)(2,1)S(1)}, u32[]{:S(2)}, u32[]{:S(2)}) collective-permute-start(bf16[256,896]{1,0:T(8,128)(2,1)S(1)} %convolution_convert_fusion.4), channel_id=1, source_target_pairs={{0,1},{1,0},{2,3},{3,2},{4,5},{5,4},{6,7},{7,6},{8,9},{9,8},{10,11... | collective-permute-start | bytes 1376264 | tf_op jit(solution)/shard_map/ppermute | solution.py:21
  129.2 6.8 %collective-permute-start.31 = (bf16[256,1792]{1,0:T(8,128)(2,1)S(1)}, bf16[256,1792]{1,0:T(8,128)(2,1)S(1)}, u32[]{:S(2)}, u32[]{:S(2)}) collective-permute-start(bf16[256,1792]{1,0:T(8,128)(2,1)S(1)} %convolution_convert_fusion.1), channel_id=1, source_target_pairs={{0,1},{1,0},{2,3},{3,2},{4,5},{5,4},{6,7},{7,6},{8,9},{9,8},{10,11... | collective-permute-start | bytes 2752520 | tf_op jit(solution)/shard_map/ppermute | solution.py:21
  130.0 8.3 %collective-permute-start.36 = (bf16[256,1792]{1,0:T(8,128)(2,1)S(1)}, bf16[256,1792]{1,0:T(8,128)(2,1)S(1)}, u32[]{:S(2)}, u32[]{:S(2)}) collective-permute-start(bf16[256,1792]{1,0:T(8,128)(2,1)S(1)} %convolution_convert_fusion), channel_id=1, source_target_pairs={{0,1},{1,0},{2,3},{3,2},{4,5},{5,4},{6,7},{7,6},{8,9},{9,8},{10,11... | collective-permute-start | bytes 2752520 | tf_op jit(solution)/shard_map/ppermute | solution.py:21
  131.2 20.0 %collective-permute-start.30 = (bf16[256,1792]{1,0:T(8,128)(2,1)S(1)}, bf16[256,1792]{1,0:T(8,128)(2,1)S(1)}, u32[]{:S(2)}, u32[]{:S(2)}) collective-permute-start(bf16[256,1792]{1,0:T(8,128)(2,1)S(1)} %convolution_convert_fusion.2), channel_id=1, source_target_pairs={{0,1},{1,0},{2,3},{3,2},{4,5},{5,4},{6,7},{7,6},{8,9},{9,8},{10,11... | collective-permute-start | bytes 2752520 | tf_op jit(solution)/shard_map/ppermute | solution.py:21
  131.8 17.2 %collective-permute-start.38 = (bf16[256,896]{1,0:T(8,128)(2,1)S(1)}, bf16[256,896]{1,0:T(8,128)(2,1)S(1)}, u32[]{:S(2)}, u32[]{:S(2)}) collective-permute-start(bf16[256,896]{1,0:T(8,128)(2,1)S(1)} %fusion.7), channel_id=1, source_target_pairs={{0,2},{1,3},{2,0},{3,1},{4,6},{5,7},{6,4},{7,5},{8,10},{9,11},{10,... | collective-permute-start | bytes 1376264 | tf_op jit(solution)/shard_map/ppermute | solution.py:21
  133.2 14.2 %collective-permute-start.34 = (bf16[256,896]{1,0:T(8,128)(2,1)S(1)}, bf16[256,896]{1,0:T(8,128)(2,1)S(1)}, u32[]{:S(2)}, u32[]{:S(2)}) collective-permute-start(bf16[256,896]{1,0:T(8,128)(2,1)S(1)} %fusion.6), channel_id=1, source_target_pairs={{0,8},{4,12},{8,0},{12,4},{16,24},{20,28},{24,16},{28,20},{1,9},{5... | collective-permute-start | bytes 1376264 | tf_op jit(solution)/shard_map/ppermute | solution.py:21
  136.8 18.3 %collective-permute-start.32 = (bf16[256,896]{1,0:T(8,128)(2,1)S(1)}, bf16[256,896]{1,0:T(8,128)(2,1)S(1)}, u32[]{:S(2)}, u32[]{:S(2)}) collective-permute-start(bf16[256,896]{1,0:T(8,128)(2,1)S(1)} %slice.113), channel_id=1, source_target_pairs={{0,2},{1,3},{2,0},{3,1},{4,6},{5,7},{6,4},{7,5},{8,10},{9,11},{10,... | collective-permute-start | bytes 1376264 | tf_op jit(solution)/shard_map/ppermute | solution.py:21
  139.1 18.1 %collective-permute-start.40 = (bf16[256,896]{1,0:T(8,128)(2,1)S(1)}, bf16[256,896]{1,0:T(8,128)(2,1)S(1)}, u32[]{:S(2)}, u32[]{:S(2)}) collective-permute-start(bf16[256,896]{1,0:T(8,128)(2,1)S(1)} %slice.112), channel_id=1, source_target_pairs={{0,8},{4,12},{8,0},{12,4},{16,24},{20,28},{24,16},{28,20},{1,9},{5... | collective-permute-start | bytes 1376264 | tf_op jit(solution)/shard_map/ppermute | solution.py:21
  147.4 17.0 %collective-permute-start.35 = (bf16[256,896]{1,0:T(8,128)(2,1)S(1)}, bf16[256,896]{1,0:T(8,128)(2,1)S(1)}, u32[]{:S(2)}, u32[]{:S(2)}) collective-permute-start(bf16[256,896]{1,0:T(8,128)(2,1)S(1)} %fusion.9), channel_id=1, source_target_pairs={{0,2},{1,3},{2,0},{3,1},{4,6},{5,7},{6,4},{7,5},{8,10},{9,11},{10,... | collective-permute-start | bytes 1376264 | tf_op jit(solution)/shard_map/ppermute | solution.py:21
  149.1 17.4 %collective-permute-start.39 = (bf16[256,896]{1,0:T(8,128)(2,1)S(1)}, bf16[256,896]{1,0:T(8,128)(2,1)S(1)}, u32[]{:S(2)}, u32[]{:S(2)}) collective-permute-start(bf16[256,896]{1,0:T(8,128)(2,1)S(1)} %fusion.8), channel_id=1, source_target_pairs={{0,8},{4,12},{8,0},{12,4},{16,24},{20,28},{24,16},{28,20},{1,9},{5... | collective-permute-start | bytes 1376264 | tf_op jit(solution)/shard_map/ppermute | solution.py:21

commit v7 on v6

--- a/solution.py
+++ b/solution.py
@@ -269,7 +269,7 @@
     order.after("q0 qother", f"kv{mids[1]}", f"kv{far ^ 1}")
     relay("kv", *mids[1:])
     groups_b = spread("b", [[0]])
-    send("q", *mids)
+    send("q", *mids[::-1])
     order["kv_even"] = project("kv", even, "a", groups_a)
     order.after("qother", "kv_even")
     send("q", near)
@@ -293,7 +293,6 @@
     order.after("q0", *[f"grad{d}" for d in others[:-1]])
     order["q_even"] = project("q", even, "a", groups_a)
     order["q"] = project("q", odd, *last, order["q_even"])
-    order.after("q", *[f"grad{d}" for d in others[:-1]])
     for d in others[:-1]:
         start(f"query{d}", order["q"], d, to_earlier)
     start("both", jnp.concatenate([order["q"], order["grad"]], axis=1), others[-1])

time: 168 us -> 168 us (level)
  no operation moved by 1% of the time
where the time goes in v7:
time: 168 us
  waiting for transfers between devices  82.8 us (49%)
  starting transfers between devices  48.1 us (29%)
  Pallas kernels  20.7 us (12%)
  local copies, waits for them, and re-layouts  6.58 us (4%)
  matrix products  5.91 us (4%)
  other arithmetic  3.07 us (2%)
    ppermute x41, waiting for transfers between devices, swap(): return lax.ppermute(array, axis, pairs)  82.8 us
    ppermute x41, starting transfers between devices, swap(): return lax.ppermute(array, axis, pairs)  48.1 us
    pallas_call x4, Pallas kernels, project(): local_call(functools.partial(project_kernel, groups, len(ds)), out, 1 + l...  7.42 us
    dot_general x10, matrix products, dot_nt(): lax.dot_general(a, b, (((1,), (1,)), ((), ())), preferred_element_type=F32)  5.91 us
  transfers between devices with their start and end apart: 41, of which 18 were waited for; matrix products, arithmetic and copies ran while one was open for 8% of the time, Pallas kernels for 10%

profile of v7, /device:TPU:0, one launch (start us, length us, event | category | flops | bytes accessed | tf_op | source)
XLA Modules:
  0.0 167.7 jit_solution(12354018614767422655)
XLA Ops:
  0.0 1.4 fusion.37
  1.7 4.1 %collective-permute-start.6 = (bf16[896,256]{1,0:T(8,128)(2,1)S(1)}, bf16[896,256]{1,0:T(8,128)(2,1)S(1)}, u32[]{:S(2)}, u32[]{:S(2)}) collective-permute-start(bf16[896,256]{1,0:T(8,128)(2,1)S(1)} %pad_maximum_fusion.3.refs_3_), channel_id=1, source_target_pairs={{0,16},{4,20},{8,24},{12,28},{16,0},{20,4},{24,8},{28,12},{1,17},{... | collective-permute-start | bytes 1376264 | tf_op jit(solution)/shard_map/ppermute | solution.py:21
  5.8 1.5 collective-permute-start.2
  7.9 1.6 collective-permute-start.1
  9.5 2.2 %constant_dynamic-slice_fusion.1 = (bf16[256,896]{1,0:T(8,128)(2,1)}, bf16[256,896]{1,0:T(8,128)(2,1)}) fusion(bf16[256,7168]{1,0:T(8,128)(2,1)} %own_ref.7, s32[]{:T(128)S(6)} %select_n.158, s32[]{:T(128)S(6)} %select_n.157), kind=kLoop, calls=%fused_computation.84 | loop fusion | bytes 1835016 | tf_op jit(solution)/shard_map/dynamic_slice | solution.py:202
  13.0 1.6 collective-permute-start.10
  14.8 2.9 %collective-permute-done.2.refs_3_ = bf16[896,256]{1,0:T(8,128)(2,1)S(1)} collective-permute-done((bf16[896,256]{1,0:T(8,128)(2,1)S(1)}, bf16[896,256]{1,0:T(8,128)(2,1)S(1)}, u32[]{:S(2)}, u32[]{:S(2)}) %collective-permute-start.2) | collective-permute-done | bytes 458784 | tf_op jit(solution)/shard_map/ppermute | solution.py:21
  17.7 1.5 collective-permute-start.3
  19.4 14.6 %collective-permute-done.refs_0_ = bf16[256,896]{1,0:T(8,128)(2,1)S(1)} collective-permute-done((bf16[256,896]{1,0:T(8,128)(2,1)}, bf16[256,896]{1,0:T(8,128)(2,1)S(1)}, u32[]{:S(2)}, u32[]{:S(2)}) %collective-permute-start) | collective-permute-done | bytes 458784 | tf_op jit(solution)/shard_map/ppermute | solution.py:21
  34.0 1.5 collective-permute-start.13
  37.1 1.3 collective-permute-start.7
  38.9 3.6 %collective-permute-done.13.refs_1_ = bf16[256,896]{1,0:T(8,128)(2,1)S(1)} collective-permute-done((bf16[256,896]{1,0:T(8,128)(2,1)S(1)}, bf16[256,896]{1,0:T(8,128)(2,1)S(1)}, u32[]{:S(2)}, u32[]{:S(2)}) %collective-permute-start.13) | collective-permute-done | bytes 458784 | tf_op jit(solution)/shard_map/ppermute | solution.py:21
  42.9 10.8 %collective-permute-done.10.refs_4_ = bf16[896,256]{1,0:T(8,128)(2,1)S(1)} collective-permute-done((bf16[896,256]{1,0:T(8,128)(2,1)}, bf16[896,256]{1,0:T(8,128)(2,1)S(1)}, u32[]{:S(2)}, u32[]{:S(2)}) %collective-permute-start.10) | collective-permute-done | bytes 458784 | tf_op jit(solution)/shard_map/ppermute | solution.py:21
  54.2 1.5 collective-permute-start.9
  55.7 5.8 %collective-permute-done.4.refs_0_ = bf16[256,896]{1,0:T(8,128)(2,1)S(1)} collective-permute-done((bf16[256,896]{1,0:T(8,128)(2,1)}, bf16[256,896]{1,0:T(8,128)(2,1)S(1)}, u32[]{:S(2)}, u32[]{:S(2)}) %collective-permute-start.4) | collective-permute-done | bytes 458784 | tf_op jit(solution)/shard_map/ppermute | solution.py:21
  61.5 1.5 collective-permute-start.5
  63.2 1.4 collective-permute-start.16
  64.5 4.4 %collective-permute-done.9.refs_6_ = bf16[896,256]{1,0:T(8,128)(2,1)S(1)} collective-permute-done((bf16[896,256]{1,0:T(8,128)(2,1)S(1)}, bf16[896,256]{1,0:T(8,128)(2,1)S(1)}, u32[]{:S(2)}, u32[]{:S(2)}) %collective-permute-start.9) | collective-permute-done | bytes 458784 | tf_op jit(solution)/shard_map/ppermute | solution.py:21
  68.9 3.1 %collective-permute-done.5.refs_1_ = bf16[256,896]{1,0:T(8,128)(2,1)S(1)} collective-permute-done((bf16[256,896]{1,0:T(8,128)(2,1)S(1)}, bf16[256,896]{1,0:T(8,128)(2,1)S(1)}, u32[]{:S(2)}, u32[]{:S(2)}) %collective-permute-start.5) | collective-permute-done | bytes 458784 | tf_op jit(solution)/shard_map/ppermute | solution.py:21
  72.0 1.9 %shard_map.46.refs_7_ = f32[512,256]{1,0:T(8,128)S(1)} custom-call(s32[2,4]{1,0:T(2,128)S(1)} %pad_add_fusion.1.place_ref, bf16[256,7168]{1,0:T(8,128)(2,1)S(1)} %copy-done.1, bf16[256,896]{1,0:T(8,128)(2,1)S(1)} %collective-permute-done.refs_0_, bf16[256,896]{1,0:T(8,128)(2,1)S(1)} %collective-permute-done.13.refs_1_, ...), custom_call_target="tpu_custom_call" | custom-call | flops 1 | bytes 1 | tf_op jit(solution)/shard_map/pallas_call | solution.py:228
  74.2 8.5 %collective-permute-done.15.refs_5_ = bf16[896,128]{1,0:T(8,128)(2,1)S(1)} collective-permute-done((bf16[896,128]{1,0:T(8,128)(2,1)S(1)}, bf16[896,128]{1,0:T(8,128)(2,1)S(1)}, u32[]{:S(2)}, u32[]{:S(2)}) %collective-permute-start.15) | collective-permute-done | bytes 229408 | tf_op jit(solution)/shard_map/ppermute | solution.py:21
  85.4 1.9 %shard_map.47.refs_0_.kv_ref = bf16[512,256]{1,0:T(8,128)(2,1)S(1)} custom-call(s32[2,4]{1,0:T(2,128)S(1)} %pad_add_fusion.place_ref, bf16[256,7168]{1,0:T(8,128)(2,1)S(1)} %copy-done.1, bf16[256,896]{1,0:T(8,128)(2,1)S(1)} %collective-permute-done.4.refs_0_, bf16[256,896]{1,0:T(8,128)(2,1)S(1)} %collective-permute-done.5.refs_1_, ...), custom_call_target="tpu_custom_call" | custom-call | flops 1 | bytes 1 | tf_op jit(solution)/shard_map/pallas_call | solution.py:228
  87.3 1.3 collective-permute-start.20
  88.6 1.3 collective-permute-start.19
  90.0 6.4 %collective-permute-start.25 = (bf16[512,256]{1,0:T(8,128)(2,1)S(1)}, bf16[512,256]{1,0:T(8,128)(2,1)S(1)}, u32[]{:S(2)}, u32[]{:S(2)}) collective-permute-start(bf16[512,256]{1,0:T(8,128)(2,1)S(1)} %shard_map.47.refs_0_.kv_ref), channel_id=1, source_target_pairs={{0,20},{4,16},{8,28},{12,24},{1,21},{5,17},{9,29},{13,25},{2,22},{... | collective-permute-start | bytes 786440 | tf_op jit(solution)/shard_map/ppermute | solution.py:21
  96.4 1.3 collective-permute-start.24
  97.7 1.8 %collective-permute-done.19.refs_3_ = bf16[512,128]{1,0:T(8,128)(2,1)S(1)} collective-permute-done((bf16[512,128]{1,0:T(8,128)(2,1)S(1)}, bf16[512,128]{1,0:T(8,128)(2,1)S(1)}, u32[]{:S(2)}, u32[]{:S(2)}) %collective-permute-start.19) | collective-permute-done | bytes 131104 | tf_op jit(solution)/shard_map/ppermute | solution.py:21
  99.5 1.4 collective-permute-done.18
  102.1 1.8 %shard_map.48.refs_7_ = f32[512,128]{1,0:T(8,128)S(1)} custom-call(s32[2,4]{1,0:T(2,128)S(1)} %pad_add_fusion.1.place_ref, bf16[256,7168]{1,0:T(8,128)(2,1)S(1)} %copy-done.1, bf16[256,896]{1,0:T(8,128)(2,1)S(1)} %collective-permute-done.refs_0_, bf16[256,896]{1,0:T(8,128)(2,1)S(1)} %collective-permute-done.13.refs_1_, ...), custom_call_target="tpu_custom_call" | custom-call | flops 1 | bytes 1 | tf_op jit(solution)/shard_map/pallas_call | solution.py:228
  103.9 1.8 %shard_map.49.q_ref.refs_0_ = bf16[512,128]{1,0:T(8,128)(2,1)S(1)} custom-call(s32[2,4]{1,0:T(2,128)S(1)} %pad_add_fusion.place_ref, bf16[256,7168]{1,0:T(8,128)(2,1)S(1)} %copy-done.1, bf16[256,896]{1,0:T(8,128)(2,1)S(1)} %collective-permute-done.4.refs_0_, bf16[256,896]{1,0:T(8,128)(2,1)S(1)} %collective-permute-done.5.refs_1_, ...), custom_call_target="tpu_custom_call" | custom-call | flops 1 | bytes 1 | tf_op jit(solution)/shard_map/pallas_call | solution.py:228
  105.7 1.3 collective-permute-start.22
  108.5 1.3 collective-permute-start.21
  109.8 1.6 collective-permute-done.23.refs_1_
  111.4 2.9 %shard_map.50 = (f32[8,512]{1,0:T(8,128)S(1)}, f32[512,128]{1,0:T(8,128)S(1)}) custom-call(s32[2,8]{1,0:T(2,128)S(1)} %get-tuple-element.94.limit_ref, bf16[512,128]{1,0:T(8,128)(2,1)S(1)} %shard_map.49.q_ref.refs_0_, bf16[512,128]{1,0:T(8,128)(2,1)S(1)} %pad_maximum_fusion.7.grad_ref.refs_2_, bf16[512,256]{1,0:T(8,128)(2,1)S(1)} %shard_map.47.refs_0_.kv_ref, ...), custom_call_target="tpu_custom_call" | custom-call | flops 1 | bytes 1 | tf_op jit(solution)/shard_map/pallas_call | solution.py:322
  114.4 1.3 collective-permute-start.27
  115.7 1.5 collective-permute-start.26
  117.2 3.2 %shard_map.53 = bf16[512,128]{1,0:T(8,128)(2,1)S(1)} custom-call(s32[2,8]{1,0:T(2,128)S(1)} %get-tuple-element.94.limit_ref, bf16[512,128]{1,0:T(8,128)(2,1)S(1)} %shard_map.49.q_ref.refs_0_, bf16[512,128]{1,0:T(8,128)(2,1)S(1)} %pad_maximum_fusion.7.grad_ref.refs_2_, f32[512,128]{1,0:T(8,128)S(1)} %get-tuple-element.70.column_ref, ...), custom_call_target="tpu_custom_call" | custom-call | flops 1 | bytes 1 | tf_op jit(solution)/shard_map/pallas_call | solution.py:335
  120.9 2.9 %shard_map.51.refs_6_ = f32[512,256]{1,0:T(8,128)S(1)} custom-call(s32[2,4]{1,0:T(2,128)S(1)} %get-tuple-element.92.limit_ref, bf16[512,256]{1,0:T(8,128)(2,1)S(1)} %shard_map.47.refs_0_.kv_ref, bf16[512,128]{1,0:T(8,128)(2,1)S(1)} %shard_map.49.q_ref.refs_0_, bf16[512,128]{1,0:T(8,128)(2,1)S(1)} %get-tuple-element.89.refs_1_, ...), custom_call_target="tpu_custom_call" | custom-call | flops 1 | bytes 1 | tf_op jit(solution)/shard_map/pallas_call | solution.py:341
  123.8 3.1 %shard_map.52 = bf16[512,256]{1,0:T(8,128)(2,1)S(1)} custom-call(s32[2,4]{1,0:T(2,128)S(1)} %get-tuple-element.93.limit_ref, bf16[512,256]{1,0:T(8,128)(2,1)S(1)} %shard_map.47.refs_0_.kv_ref, bf16[512,128]{1,0:T(8,128)(2,1)S(1)} %collective-permute-done.21.refs_0_, bf16[512,128]{1,0:T(8,128)(2,1)S(1)} %collective-permute-done.22.refs_1_, ...), custom_call_target="tpu_custom_call" | custom-call | flops 1 | bytes 1 | tf_op jit(solution)/shard_map/pallas_call | solution.py:347
  133.2 2.9 %collective-permute-start.34 = (bf16[256,896]{1,0:T(8,128)(2,1)S(1)}, bf16[256,896]{1,0:T(8,128)(2,1)S(1)}, u32[]{:S(2)}, u32[]{:S(2)}) collective-permute-start(bf16[256,896]{1,0:T(8,128)(2,1)S(1)} %fusion.6), channel_id=1, source_target_pairs={{0,8},{4,12},{8,0},{12,4},{16,24},{20,28},{24,16},{28,20},{1,9},{5... | collective-permute-start | bytes 1376264 | tf_op jit(solution)/shard_map/ppermute | solution.py:21
  136.8 1.6 collective-permute-start.32
  139.2 8.2 %collective-permute-done.34 = bf16[256,896]{1,0:T(8,128)(2,1)S(1)} collective-permute-done((bf16[256,896]{1,0:T(8,128)(2,1)S(1)}, bf16[256,896]{1,0:T(8,128)(2,1)S(1)}, u32[]{:S(2)}, u32[]{:S(2)}) %collective-permute-start.34) | collective-permute-done | bytes 458784 | tf_op jit(solution)/shard_map/ppermute | solution.py:21
  147.4 1.6 collective-permute-start.35
  149.1 2.1 %collective-permute-start.39 = (bf16[256,896]{1,0:T(8,128)(2,1)S(1)}, bf16[256,896]{1,0:T(8,128)(2,1)S(1)}, u32[]{:S(2)}, u32[]{:S(2)}) collective-permute-start(bf16[256,896]{1,0:T(8,128)(2,1)S(1)} %fusion.8), channel_id=1, source_target_pairs={{0,8},{4,12},{8,0},{12,4},{16,24},{20,28},{24,16},{28,20},{1,9},{5... | collective-permute-start | bytes 1376264 | tf_op jit(solution)/shard_map/ppermute | solution.py:21
  151.9 3.1 %collective-permute-done.32.x_a = bf16[256,896]{1,0:T(8,128)(2,1)S(1)} collective-permute-done((bf16[256,896]{1,0:T(8,128)(2,1)S(1)}, bf16[256,896]{1,0:T(8,128)(2,1)S(1)}, u32[]{:S(2)}, u32[]{:S(2)}) %collective-permute-start.32) | collective-permute-done | bytes 458784 | tf_op jit(solution)/shard_map/ppermute | solution.py:21
  155.0 2.1 %collective-permute-done.40.z_b = bf16[256,896]{1,0:T(8,128)(2,1)S(1)} collective-permute-done((bf16[256,896]{1,0:T(8,128)(2,1)S(1)}, bf16[256,896]{1,0:T(8,128)(2,1)S(1)}, u32[]{:S(2)}, u32[]{:S(2)}) %collective-permute-start.40) | collective-permute-done | bytes 458784 | tf_op jit(solution)/shard_map/ppermute | solution.py:21
  157.1 7.2 %collective-permute-done.35.x_b = bf16[256,896]{1,0:T(8,128)(2,1)S(1)} collective-permute-done((bf16[256,896]{1,0:T(8,128)(2,1)S(1)}, bf16[256,896]{1,0:T(8,128)(2,1)S(1)}, u32[]{:S(2)}, u32[]{:S(2)}) %collective-permute-start.35) | collective-permute-done | bytes 458784 | tf_op jit(solution)/shard_map/ppermute | solution.py:21
  164.4 2.1 %collective-permute-done.39.z_a = bf16[256,896]{1,0:T(8,128)(2,1)S(1)} collective-permute-done((bf16[256,896]{1,0:T(8,128)(2,1)S(1)}, bf16[256,896]{1,0:T(8,128)(2,1)S(1)}, u32[]{:S(2)}, u32[]{:S(2)}) %collective-permute-start.39) | collective-permute-done | bytes 458784 | tf_op jit(solution)/shard_map/ppermute | solution.py:21
  (115 shorter events, 21.6 us)
Async XLA Ops:
  0.0 35.7 %copy-start = (s32[4,4]{1,0:T(4,128)S(1)}, s32[4,4]{1,0:T(4,128)}, u32[]{:S(2)}) copy-start(s32[4,4]{1,0:T(4,128)} %param.6) | copy-start | bytes 196
  1.4 5.9 %copy-start.2 = (bf16[256,256]{1,0:T(8,128)(2,1)S(1)}, bf16[256,256]{1,0:T(8,128)(2,1)}, u32[]{:S(2)}) copy-start(bf16[256,256]{1,0:T(8,128)(2,1)} %param.7) | copy-start | bytes 393220
  1.7 35.4 %collective-permute-start.6 = (bf16[896,256]{1,0:T(8,128)(2,1)S(1)}, bf16[896,256]{1,0:T(8,128)(2,1)S(1)}, u32[]{:S(2)}, u32[]{:S(2)}) collective-permute-start(bf16[896,256]{1,0:T(8,128)(2,1)S(1)} %pad_maximum_fusion.3.refs_3_), channel_id=1, source_target_pairs={{0,16},{4,20},{8,24},{12,28},{16,0},{20,4},{24,8},{28,12},{1,17},{... | collective-permute-start | bytes 1376264 | tf_op jit(solution)/shard_map/ppermute | solution.py:21
  5.8 12.0 %collective-permute-start.2 = (bf16[896,256]{1,0:T(8,128)(2,1)S(1)}, bf16[896,256]{1,0:T(8,128)(2,1)S(1)}, u32[]{:S(2)}, u32[]{:S(2)}) collective-permute-start(bf16[896,256]{1,0:T(8,128)(2,1)S(1)} %pad_maximum_fusion.3.refs_3_), channel_id=1, source_target_pairs={{0,4},{4,0},{8,12},{12,8},{16,20},{20,16},{24,28},{28,24},{1,5},{5... | collective-permute-start | bytes 1376264 | tf_op jit(solution)/shard_map/ppermute | solution.py:21
  7.9 11.5 %collective-permute-start.1 = (bf16[256,128]{1,0:T(8,128)(2,1)}, bf16[256,128]{1,0:T(8,128)(2,1)}, u32[]{:S(2)}, u32[]{:S(2)}) collective-permute-start(bf16[256,128]{1,0:T(8,128)(2,1)} %get-tuple-element.91), channel_id=1, source_target_pairs={{0,8},{4,12},{8,0},{12,4},{16,24},{20,28},{24,16},{28,20},{1,9},{5... | collective-permute-start | bytes 196616 | tf_op jit(solution)/shard_map/ppermute | solution.py:21
  11.7 22.3 %collective-permute-start = (bf16[256,896]{1,0:T(8,128)(2,1)}, bf16[256,896]{1,0:T(8,128)(2,1)S(1)}, u32[]{:S(2)}, u32[]{:S(2)}) collective-permute-start(bf16[256,896]{1,0:T(8,128)(2,1)} %get-tuple-element.71), channel_id=1, source_target_pairs={{0,8},{4,12},{8,0},{12,4},{16,24},{20,28},{24,16},{28,20},{1,9},{5... | collective-permute-start | bytes 1376264 | tf_op jit(solution)/shard_map/ppermute | solution.py:21
  13.0 40.7 %collective-permute-start.10 = (bf16[896,256]{1,0:T(8,128)(2,1)}, bf16[896,256]{1,0:T(8,128)(2,1)S(1)}, u32[]{:S(2)}, u32[]{:S(2)}) collective-permute-start(bf16[896,256]{1,0:T(8,128)(2,1)} %pad_maximum_fusion.4), channel_id=1, source_target_pairs={{0,8},{4,12},{8,0},{12,4},{16,24},{20,28},{24,16},{28,20},{1,9},{5... | collective-permute-start | bytes 1376264 | tf_op jit(solution)/shard_map/ppermute | solution.py:21
  17.7 16.3 %collective-permute-start.3 = (bf16[896,128]{1,0:T(8,128)(2,1)S(1)}, bf16[896,128]{1,0:T(8,128)(2,1)S(1)}, u32[]{:S(2)}, u32[]{:S(2)}) collective-permute-start(bf16[896,128]{1,0:T(8,128)(2,1)S(1)} %get-tuple-element.63.refs_3_), channel_id=1, source_target_pairs={{0,4},{4,0},{8,12},{12,8},{16,20},{20,16},{24,28},{28,24},{1,5},{5... | collective-permute-start | bytes 688136 | tf_op jit(solution)/shard_map/ppermute | solution.py:21
  34.0 8.5 %collective-permute-start.13 = (bf16[256,896]{1,0:T(8,128)(2,1)S(1)}, bf16[256,896]{1,0:T(8,128)(2,1)S(1)}, u32[]{:S(2)}, u32[]{:S(2)}) collective-permute-start(bf16[256,896]{1,0:T(8,128)(2,1)S(1)} %collective-permute-done.refs_0_), channel_id=1, source_target_pairs={{0,2},{1,3},{2,0},{3,1},{4,6},{5,7},{6,4},{7,5},{8,10},{9,11},{10,... | collective-permute-start | bytes 1376264 | tf_op jit(solution)/shard_map/ppermute | solution.py:21
  37.1 34.9 %copy-start.1 = (bf16[256,7168]{1,0:T(8,128)(2,1)S(1)}, bf16[256,7168]{1,0:T(8,128)(2,1)}, u32[]{:S(2)}) copy-start(bf16[256,7168]{1,0:T(8,128)(2,1)} %own_ref.7) | copy-start | bytes 11010052
  37.1 17.1 %collective-permute-start.7 = (bf16[896,256]{1,0:T(8,128)(2,1)}, bf16[896,256]{1,0:T(8,128)(2,1)S(1)}, u32[]{:S(2)}, u32[]{:S(2)}) collective-permute-start(bf16[896,256]{1,0:T(8,128)(2,1)} %pad_maximum_fusion.4), channel_id=1, source_target_pairs={{0,24},{4,28},{8,16},{12,20},{16,8},{20,12},{24,0},{28,4},{1,25},{... | collective-permute-start | bytes 1376264 | tf_op jit(solution)/shard_map/ppermute | solution.py:21
  38.4 15.8 %collective-permute-start.8 = (bf16[896,256]{1,0:T(8,128)(2,1)S(1)}, bf16[896,256]{1,0:T(8,128)(2,1)S(1)}, u32[]{:S(2)}, u32[]{:S(2)}) collective-permute-start(bf16[896,256]{1,0:T(8,128)(2,1)S(1)} %collective-permute-done.6.refs_5_), channel_id=1, source_target_pairs={{0,4},{4,0},{8,12},{12,8},{16,20},{20,16},{24,28},{28,24},{1,5},{5... | collective-permute-start | bytes 1376264 | tf_op jit(solution)/shard_map/ppermute | solution.py:21
  38.9 22.6 %collective-permute-start.4 = (bf16[256,896]{1,0:T(8,128)(2,1)}, bf16[256,896]{1,0:T(8,128)(2,1)S(1)}, u32[]{:S(2)}, u32[]{:S(2)}) collective-permute-start(bf16[256,896]{1,0:T(8,128)(2,1)} %get-tuple-element.40), channel_id=1, source_target_pairs={{0,8},{4,12},{8,0},{12,4},{16,24},{20,28},{24,16},{28,20},{1,9},{5... | collective-permute-start | bytes 1376264 | tf_op jit(solution)/shard_map/ppermute | solution.py:21
  42.6 29.4 %collective-permute-start.14 = (bf16[512,896]{1,0:T(8,128)(2,1)S(1)}, bf16[512,896]{1,0:T(8,128)(2,1)S(1)}, u32[]{:S(2)}, u32[]{:S(2)}) collective-permute-start(bf16[512,896]{1,0:T(8,128)(2,1)S(1)} %pad_maximum_fusion.1), channel_id=1, source_target_pairs={{0,1},{1,0},{2,3},{3,2},{4,5},{5,4},{6,7},{7,6},{8,9},{9,8},{10,11... | collective-permute-start | bytes 2752520 | tf_op jit(solution)/shard_map/ppermute | solution.py:21
  53.7 10.8 %collective-permute-start.11 = (bf16[896,256]{1,0:T(8,128)(2,1)S(1)}, bf16[896,256]{1,0:T(8,128)(2,1)S(1)}, u32[]{:S(2)}, u32[]{:S(2)}) collective-permute-start(bf16[896,256]{1,0:T(8,128)(2,1)S(1)} %collective-permute-done.10.refs_4_), channel_id=1, source_target_pairs={{0,4},{4,0},{8,12},{12,8},{16,20},{20,16},{24,28},{28,24},{1,5},{5... | collective-permute-start | bytes 1376264 | tf_op jit(solution)/shard_map/ppermute | solution.py:21
  54.2 14.7 %collective-permute-start.9 = (bf16[896,256]{1,0:T(8,128)(2,1)S(1)}, bf16[896,256]{1,0:T(8,128)(2,1)S(1)}, u32[]{:S(2)}, u32[]{:S(2)}) collective-permute-start(bf16[896,256]{1,0:T(8,128)(2,1)S(1)} %collective-permute-done.7.refs_6_), channel_id=1, source_target_pairs={{0,4},{4,0},{8,12},{12,8},{16,20},{20,16},{24,28},{28,24},{1,5},{5... | collective-permute-start | bytes 1376264 | tf_op jit(solution)/shard_map/ppermute | solution.py:21
  61.5 10.5 %collective-permute-start.5 = (bf16[256,896]{1,0:T(8,128)(2,1)S(1)}, bf16[256,896]{1,0:T(8,128)(2,1)S(1)}, u32[]{:S(2)}, u32[]{:S(2)}) collective-permute-start(bf16[256,896]{1,0:T(8,128)(2,1)S(1)} %collective-permute-done.4.refs_0_), channel_id=1, source_target_pairs={{0,2},{1,3},{2,0},{3,1},{4,6},{5,7},{6,4},{7,5},{8,10},{9,11},{10,... | collective-permute-start | bytes 1376264 | tf_op jit(solution)/shard_map/ppermute | solution.py:21
  63.2 11.0 %collective-permute-start.16 = (bf16[896,128]{1,0:T(8,128)(2,1)S(1)}, bf16[896,128]{1,0:T(8,128)(2,1)S(1)}, u32[]{:S(2)}, u32[]{:S(2)}) collective-permute-start(bf16[896,128]{1,0:T(8,128)(2,1)S(1)} %get-tuple-element.57), channel_id=1, source_target_pairs={{0,24},{4,28},{8,16},{12,20},{16,8},{20,12},{24,0},{28,4},{1,25},{... | collective-permute-start | bytes 688136 | tf_op jit(solution)/shard_map/ppermute | solution.py:21
  64.5 18.2 %collective-permute-start.15 = (bf16[896,128]{1,0:T(8,128)(2,1)S(1)}, bf16[896,128]{1,0:T(8,128)(2,1)S(1)}, u32[]{:S(2)}, u32[]{:S(2)}) collective-permute-start(bf16[896,128]{1,0:T(8,128)(2,1)S(1)} %get-tuple-element.63.refs_3_), channel_id=1, source_target_pairs={{0,16},{4,20},{8,24},{12,28},{16,0},{20,4},{24,8},{28,12},{1,17},{... | collective-permute-start | bytes 688136 | tf_op jit(solution)/shard_map/ppermute | solution.py:21
  73.9 9.9 %collective-permute-start.17 = (bf16[896,128]{1,0:T(8,128)(2,1)S(1)}, bf16[896,128]{1,0:T(8,128)(2,1)S(1)}, u32[]{:S(2)}, u32[]{:S(2)}) collective-permute-start(bf16[896,128]{1,0:T(8,128)(2,1)S(1)} %get-tuple-element.57), channel_id=1, source_target_pairs={{0,8},{4,12},{8,0},{12,4},{16,24},{20,28},{24,16},{28,20},{1,9},{5... | collective-permute-start | bytes 688136 | tf_op jit(solution)/shard_map/ppermute | solution.py:21
  74.0 11.3 %collective-permute-start.12 = (bf16[512,896]{1,0:T(8,128)(2,1)S(1)}, bf16[512,896]{1,0:T(8,128)(2,1)S(1)}, u32[]{:S(2)}, u32[]{:S(2)}) collective-permute-start(bf16[512,896]{1,0:T(8,128)(2,1)S(1)} %pad_maximum_fusion), channel_id=1, source_target_pairs={{0,1},{1,0},{2,3},{3,2},{4,5},{5,4},{6,7},{7,6},{8,9},{9,8},{10,11... | collective-permute-start | bytes 2752520 | tf_op jit(solution)/shard_map/ppermute | solution.py:21
  83.8 17.1 %collective-permute-start.18 = (bf16[2688,128]{1,0:T(8,128)(2,1)S(1)}, bf16[2688,128]{1,0:T(8,128)(2,1)S(1)}, u32[]{:S(2)}, u32[]{:S(2)}) collective-permute-start(bf16[2688,128]{1,0:T(8,128)(2,1)S(1)} %pad_maximum_fusion.2), channel_id=1, source_target_pairs={{0,4},{4,0},{8,12},{12,8},{16,20},{20,16},{24,28},{28,24},{1,5},{5... | collective-permute-start | bytes 2064392 | tf_op jit(solution)/shard_map/ppermute | solution.py:21
  87.3 10.4 %collective-permute-start.20 = (bf16[512,128]{1,0:T(8,128)(2,1)S(1)}, bf16[512,128]{1,0:T(8,128)(2,1)S(1)}, u32[]{:S(2)}, u32[]{:S(2)}) collective-permute-start(bf16[512,128]{1,0:T(8,128)(2,1)S(1)} %pad_maximum_fusion.7.grad_ref.refs_2_), channel_id=1, source_target_pairs={{16,0},{20,4},{24,8},{28,12},{17,1},{21,5},{25,9},{29,13},{18,2},{... | collective-permute-start | bytes 393224 | tf_op jit(solution)/shard_map/ppermute | solution.py:21
  88.6 10.9 %collective-permute-start.19 = (bf16[512,128]{1,0:T(8,128)(2,1)S(1)}, bf16[512,128]{1,0:T(8,128)(2,1)S(1)}, u32[]{:S(2)}, u32[]{:S(2)}) collective-permute-start(bf16[512,128]{1,0:T(8,128)(2,1)S(1)} %pad_maximum_fusion.7.grad_ref.refs_2_), channel_id=1, source_target_pairs={{16,4},{20,0},{24,12},{28,8},{17,5},{21,1},{25,13},{29,9},{18,6},{... | collective-permute-start | bytes 393224 | tf_op jit(solution)/shard_map/ppermute | solution.py:21
  90.0 18.5 %collective-permute-start.25 = (bf16[512,256]{1,0:T(8,128)(2,1)S(1)}, bf16[512,256]{1,0:T(8,128)(2,1)S(1)}, u32[]{:S(2)}, u32[]{:S(2)}) collective-permute-start(bf16[512,256]{1,0:T(8,128)(2,1)S(1)} %shard_map.47.refs_0_.kv_ref), channel_id=1, source_target_pairs={{0,20},{4,16},{8,28},{12,24},{1,21},{5,17},{9,29},{13,25},{2,22},{... | collective-permute-start | bytes 786440 | tf_op jit(solution)/shard_map/ppermute | solution.py:21
  96.4 13.4 %collective-permute-start.24 = (bf16[512,256]{1,0:T(8,128)(2,1)S(1)}, bf16[512,256]{1,0:T(8,128)(2,1)S(1)}, u32[]{:S(2)}, u32[]{:S(2)}) collective-permute-start(bf16[512,256]{1,0:T(8,128)(2,1)S(1)} %shard_map.47.refs_0_.kv_ref), channel_id=1, source_target_pairs={{0,16},{4,20},{8,24},{12,28},{1,17},{5,21},{9,25},{13,29},{2,18},{... | collective-permute-start | bytes 786440 | tf_op jit(solution)/shard_map/ppermute | solution.py:21
  100.9 10.5 %collective-permute-start.23 = (bf16[512,256]{1,0:T(8,128)(2,1)S(1)}, bf16[512,256]{1,0:T(8,128)(2,1)S(1)}, u32[]{:S(2)}, u32[]{:S(2)}) collective-permute-start(bf16[512,256]{1,0:T(8,128)(2,1)S(1)} %shard_map.47.refs_0_.kv_ref), channel_id=1, source_target_pairs={{0,4},{4,0},{8,12},{12,8},{16,20},{20,16},{24,28},{28,24},{1,5},{5... | collective-permute-start | bytes 786440 | tf_op jit(solution)/shard_map/ppermute | solution.py:21
  105.7 18.1 %collective-permute-start.22 = (bf16[512,128]{1,0:T(8,128)(2,1)S(1)}, bf16[512,128]{1,0:T(8,128)(2,1)S(1)}, u32[]{:S(2)}, u32[]{:S(2)}) collective-permute-start(bf16[512,128]{1,0:T(8,128)(2,1)S(1)} %shard_map.49.q_ref.refs_0_), channel_id=1, source_target_pairs={{16,4},{20,0},{24,12},{28,8},{17,5},{21,1},{25,13},{29,9},{18,6},{... | collective-permute-start | bytes 393224 | tf_op jit(solution)/shard_map/ppermute | solution.py:21
  107.0 10.1 %collective-permute-start.28 = (bf16[512,256]{1,0:T(8,128)(2,1)S(1)}, bf16[512,256]{1,0:T(8,128)(2,1)S(1)}, u32[]{:S(2)}, u32[]{:S(2)}) collective-permute-start(bf16[512,256]{1,0:T(8,128)(2,1)S(1)} %pad_maximum_fusion.5), channel_id=1, source_target_pairs={{0,4},{4,0},{8,12},{12,8},{16,20},{20,16},{24,28},{28,24},{1,5},{5... | collective-permute-start | bytes 786440 | tf_op jit(solution)/shard_map/ppermute | solution.py:21
  108.5 15.4 %collective-permute-start.21 = (bf16[512,128]{1,0:T(8,128)(2,1)S(1)}, bf16[512,128]{1,0:T(8,128)(2,1)S(1)}, u32[]{:S(2)}, u32[]{:S(2)}) collective-permute-start(bf16[512,128]{1,0:T(8,128)(2,1)S(1)} %shard_map.49.q_ref.refs_0_), channel_id=1, source_target_pairs={{16,0},{20,4},{24,8},{28,12},{17,1},{21,5},{25,9},{29,13},{18,2},{... | collective-permute-start | bytes 393224 | tf_op jit(solution)/shard_map/ppermute | solution.py:21
  114.4 9.5 %collective-permute-start.27 = (f32[8,512]{1,0:T(8,128)S(1)}, f32[8,512]{1,0:T(8,128)S(1)}, u32[]{:S(2)}, u32[]{:S(2)}) collective-permute-start(f32[8,512]{1,0:T(8,128)S(1)} %get-tuple-element.69.refs_4_), channel_id=1, source_target_pairs={{16,4},{20,0},{24,12},{28,8},{17,5},{21,1},{25,13},{29,9},{18,6},{... | collective-permute-start | bytes 49160 | tf_op jit(solution)/shard_map/ppermute | solution.py:21
  115.7 8.2 %collective-permute-start.26 = (f32[8,512]{1,0:T(8,128)S(1)}, f32[8,512]{1,0:T(8,128)S(1)}, u32[]{:S(2)}, u32[]{:S(2)}) collective-permute-start(f32[8,512]{1,0:T(8,128)S(1)} %get-tuple-element.69.refs_4_), channel_id=1, source_target_pairs={{16,0},{20,4},{24,8},{28,12},{17,1},{21,5},{25,9},{29,13},{18,2},{... | collective-permute-start | bytes 49160 | tf_op jit(solution)/shard_map/ppermute | solution.py:21
  117.1 3.8 %collective-permute-start.29 = (f32[8,512]{1,0:T(8,128)S(1)}, f32[8,512]{1,0:T(8,128)S(1)}, u32[]{:S(2)}, u32[]{:S(2)}) collective-permute-start(f32[8,512]{1,0:T(8,128)S(1)} %get-tuple-element.69.refs_4_), channel_id=1, source_target_pairs={{0,4},{4,0},{8,12},{12,8},{16,20},{20,16},{24,28},{28,24},{1,5},{5... | collective-permute-start | bytes 49160 | tf_op jit(solution)/shard_map/ppermute | solution.py:21
  127.9 3.4 %collective-permute-start.37 = (bf16[256,896]{1,0:T(8,128)(2,1)S(1)}, bf16[256,896]{1,0:T(8,128)(2,1)S(1)}, u32[]{:S(2)}, u32[]{:S(2)}) collective-permute-start(bf16[256,896]{1,0:T(8,128)(2,1)S(1)} %convolution_convert_fusion.3), channel_id=1, source_target_pairs={{0,1},{1,0},{2,3},{3,2},{4,5},{5,4},{6,7},{7,6},{8,9},{9,8},{10,11... | collective-permute-start | bytes 1376264 | tf_op jit(solution)/shard_map/ppermute | solution.py:21
  128.0 4.7 %collective-permute-start.33 = (bf16[256,896]{1,0:T(8,128)(2,1)S(1)}, bf16[256,896]{1,0:T(8,128)(2,1)S(1)}, u32[]{:S(2)}, u32[]{:S(2)}) collective-permute-start(bf16[256,896]{1,0:T(8,128)(2,1)S(1)} %convolution_convert_fusion.4), channel_id=1, source_target_pairs={{0,1},{1,0},{2,3},{3,2},{4,5},{5,4},{6,7},{7,6},{8,9},{9,8},{10,11... | collective-permute-start | bytes 1376264 | tf_op jit(solution)/shard_map/ppermute | solution.py:21
  129.2 6.8 %collective-permute-start.31 = (bf16[256,1792]{1,0:T(8,128)(2,1)S(1)}, bf16[256,1792]{1,0:T(8,128)(2,1)S(1)}, u32[]{:S(2)}, u32[]{:S(2)}) collective-permute-start(bf16[256,1792]{1,0:T(8,128)(2,1)S(1)} %convolution_convert_fusion.1), channel_id=1, source_target_pairs={{0,1},{1,0},{2,3},{3,2},{4,5},{5,4},{6,7},{7,6},{8,9},{9,8},{10,11... | collective-permute-start | bytes 2752520 | tf_op jit(solution)/shard_map/ppermute | solution.py:21
  130.0 8.3 %collective-permute-start.36 = (bf16[256,1792]{1,0:T(8,128)(2,1)S(1)}, bf16[256,1792]{1,0:T(8,128)(2,1)S(1)}, u32[]{:S(2)}, u32[]{:S(2)}) collective-permute-start(bf16[256,1792]{1,0:T(8,128)(2,1)S(1)} %convolution_convert_fusion), channel_id=1, source_target_pairs={{0,1},{1,0},{2,3},{3,2},{4,5},{5,4},{6,7},{7,6},{8,9},{9,8},{10,11... | collective-permute-start | bytes 2752520 | tf_op jit(solution)/shard_map/ppermute | solution.py:21
  131.2 20.0 %collective-permute-start.30 = (bf16[256,1792]{1,0:T(8,128)(2,1)S(1)}, bf16[256,1792]{1,0:T(8,128)(2,1)S(1)}, u32[]{:S(2)}, u32[]{:S(2)}) collective-permute-start(bf16[256,1792]{1,0:T(8,128)(2,1)S(1)} %convolution_convert_fusion.2), channel_id=1, source_target_pairs={{0,1},{1,0},{2,3},{3,2},{4,5},{5,4},{6,7},{7,6},{8,9},{9,8},{10,11... | collective-permute-start | bytes 2752520 | tf_op jit(solution)/shard_map/ppermute | solution.py:21
  131.8 17.2 %collective-permute-start.38 = (bf16[256,896]{1,0:T(8,128)(2,1)S(1)}, bf16[256,896]{1,0:T(8,128)(2,1)S(1)}, u32[]{:S(2)}, u32[]{:S(2)}) collective-permute-start(bf16[256,896]{1,0:T(8,128)(2,1)S(1)} %fusion.7), channel_id=1, source_target_pairs={{0,2},{1,3},{2,0},{3,1},{4,6},{5,7},{6,4},{7,5},{8,10},{9,11},{10,... | collective-permute-start | bytes 1376264 | tf_op jit(solution)/shard_map/ppermute | solution.py:21
  133.2 14.2 %collective-permute-start.34 = (bf16[256,896]{1,0:T(8,128)(2,1)S(1)}, bf16[256,896]{1,0:T(8,128)(2,1)S(1)}, u32[]{:S(2)}, u32[]{:S(2)}) collective-permute-start(bf16[256,896]{1,0:T(8,128)(2,1)S(1)} %fusion.6), channel_id=1, source_target_pairs={{0,8},{4,12},{8,0},{12,4},{16,24},{20,28},{24,16},{28,20},{1,9},{5... | collective-permute-start | bytes 1376264 | tf_op jit(solution)/shard_map/ppermute | solution.py:21
  136.8 18.3 %collective-permute-start.32 = (bf16[256,896]{1,0:T(8,128)(2,1)S(1)}, bf16[256,896]{1,0:T(8,128)(2,1)S(1)}, u32[]{:S(2)}, u32[]{:S(2)}) collective-permute-start(bf16[256,896]{1,0:T(8,128)(2,1)S(1)} %slice.113), channel_id=1, source_target_pairs={{0,2},{1,3},{2,0},{3,1},{4,6},{5,7},{6,4},{7,5},{8,10},{9,11},{10,... | collective-permute-start | bytes 1376264 | tf_op jit(solution)/shard_map/ppermute | solution.py:21
  139.1 18.1 %collective-permute-start.40 = (bf16[256,896]{1,0:T(8,128)(2,1)S(1)}, bf16[256,896]{1,0:T(8,128)(2,1)S(1)}, u32[]{:S(2)}, u32[]{:S(2)}) collective-permute-start(bf16[256,896]{1,0:T(8,128)(2,1)S(1)} %slice.112), channel_id=1, source_target_pairs={{0,8},{4,12},{8,0},{12,4},{16,24},{20,28},{24,16},{28,20},{1,9},{5... | collective-permute-start | bytes 1376264 | tf_op jit(solution)/shard_map/ppermute | solution.py:21
  147.4 17.0 %collective-permute-start.35 = (bf16[256,896]{1,0:T(8,128)(2,1)S(1)}, bf16[256,896]{1,0:T(8,128)(2,1)S(1)}, u32[]{:S(2)}, u32[]{:S(2)}) collective-permute-start(bf16[256,896]{1,0:T(8,128)(2,1)S(1)} %fusion.9), channel_id=1, source_target_pairs={{0,2},{1,3},{2,0},{3,1},{4,6},{5,7},{6,4},{7,5},{8,10},{9,11},{10,... | collective-permute-start | bytes 1376264 | tf_op jit(solution)/shard_map/ppermute | solution.py:21
  149.1 17.4 %collective-permute-start.39 = (bf16[256,896]{1,0:T(8,128)(2,1)S(1)}, bf16[256,896]{1,0:T(8,128)(2,1)S(1)}, u32[]{:S(2)}, u32[]{:S(2)}) collective-permute-start(bf16[256,896]{1,0:T(8,128)(2,1)S(1)} %fusion.8), channel_id=1, source_target_pairs={{0,8},{4,12},{8,0},{12,4},{16,24},{20,28},{24,16},{28,20},{1,9},{5... | collective-permute-start | bytes 1376264 | tf_op jit(solution)/shard_map/ppermute | solution.py:21
